TPU v7x, 32 devices: a whole 2x2x4 slice. The times are simulated.
32 devices in a mesh: scene: 16 (over z, y, core), frame: 2 (over x).
Axes of the slice: x: 2, y: 2, z: 4, core: 2. Of those that a mesh axis runs over, the one named last changes fastest.
Arguments:
- tokens: bfloat16 [4096, 1024], P(('scene', 'frame')), may hold values from -6 to 6
- cotangent: bfloat16 [4096, 1024], P(('scene', 'frame')), may hold values from -6 to 6
- scene_ids: int32 [4096], P(('scene', 'frame')), may hold values from 0 to 63, as said below
- frame_index: int32 [4096], P(('scene', 'frame')), may hold values from 0 to 3, as said below
- qkv_weight: bfloat16 [2, 1024, 3072], P(None, ('scene', 'frame')), may hold values from -0.1875 to 0.1875
- qkv_bias: bfloat16 [2, 3072], P(None, ('scene', 'frame')), may hold values from -1.796875 to 1.796875
- proj_weight: bfloat16 [2, 1024, 1024], P(None, ('scene', 'frame')), may hold values from -2 to 2
- fc1_weight: bfloat16 [2, 1024, 4096], P(None, ('scene', 'frame')), may hold values from -0.1875 to 0.1875
- fc1_bias: bfloat16 [2, 4096], P(None, ('scene', 'frame')), may hold values from -1.796875 to 1.796875
- fc2_weight: bfloat16 [2, 4096, 1024], P(None, ('scene', 'frame')), may hold values from -0.09375 to 0.09375
- out_bias: bfloat16 [2, 2, 1024], P(None, None, ('scene', 'frame')), may hold values from -1.796875 to 1.796875
- norm_gain: bfloat16 [2, 2, 1024], P(None, None, ('scene', 'frame')), may hold values from 0.5 to 1.5
- norm_bias: bfloat16 [2, 2, 1024], P(None, None, ('scene', 'frame')), may hold values from -1.796875 to 1.796875
- layer_scale: bfloat16 [2, 2, 1024], P(None, None, ('scene', 'frame')), may hold values from 0.29882812 to 1
- qk_gain: bfloat16 [2, 2, 64], replicated, may hold values from 0.5 to 1.5
- qk_bias: bfloat16 [2, 2, 64], replicated, may hold values from -1.796875 to 1.796875
Outputs:
- activations: bfloat16 [4096, 1024], P(('scene', 'frame'))
- input_grad: bfloat16 [4096, 1024], P(('scene', 'frame'))
- qkv_weight_grad: float32 [2, 1024, 3072], P(None, ('scene', 'frame'))
- qkv_bias_grad: float32 [2, 3072], P(None, ('scene', 'frame'))
- proj_weight_grad: float32 [2, 1024, 1024], P(None, ('scene', 'frame'))
- fc1_weight_grad: float32 [2, 1024, 4096], P(None, ('scene', 'frame'))
- fc1_bias_grad: float32 [2, 4096], P(None, ('scene', 'frame'))
- fc2_weight_grad: float32 [2, 4096, 1024], P(None, ('scene', 'frame'))
- out_bias_grad: float32 [2, 2, 1024], P(None, None, ('scene', 'frame'))
- norm_gain_grad: float32 [2, 2, 1024], P(None, None, ('scene', 'frame'))
- norm_bias_grad: float32 [2, 2, 1024], P(None, None, ('scene', 'frame'))
- layer_scale_grad: float32 [2, 2, 1024], P(None, None, ('scene', 'frame'))
- qk_gain_grad: float32 [2, 2, 64], replicated
- qk_bias_grad: float32 [2, 2, 64], replicated
Inputs may be any that keep to these rules, and one draw needn't show every extreme that they name: `scene_ids`: tokens of one scene are whole consecutive frames of 64 tokens within the tokens of one index of scene; a scene's id is the number of its first frame among all frames; index 0 of scene holds a single scene; the last frame of the last index of scene is a scene of its own. `frame_index`: the frame's position within its scene, counted from 0, equal for the 64 tokens of one frame.
All inputs are finite; a program needn't handle non-finite values.
Results may differ from a plain program's by a relative error of at most 0.014.
Values may be sent and summed in bfloat16 or wider, within the bound.
No kernel may reach another device: no remote copies, remote signals or barrier semaphores. Data moves between devices by JAX's collectives and lax.ppermute only.
A program may use at most 320 MiB of HBM per device.

v0:
```python
import math

import jax
import jax.numpy as jnp
from jax import lax
from jax.sharding import PartitionSpec as P

EPSILON = 1e-06
FLOOR = -1e30


def layer_norm(values_in, gain_vec, shift_vec):
    center = values_in - jnp.mean(values_in, axis=-1, keepdims=True)
    spread = jnp.mean(center * center, axis=-1, keepdims=True)
    return center * lax.rsqrt(spread + EPSILON) * gain_vec + shift_vec


def exact_gelu(values_in):
    return jax.nn.gelu(values_in, approximate=False)


def slice_keys(arrays, number, block_rows):
    return tuple(
        (lax.dynamic_slice_in_dim(member, number * block_rows, block_rows, 0) for member in arrays)
    )


def scores_of(queries, key_block, scene_rows, scene_cols, frame_rows, frame_cols, use_frame):
    score_scale = queries.shape[-1] ** (-0.5)
    scores = (
        jnp.einsum("qhd,khd->hqk", queries, key_block, preferred_element_type=jnp.float32)
        * score_scale
    )
    allowed = scene_rows[:, None] == scene_cols[None, :]
    if use_frame:
        allowed = allowed & (frame_rows[:, None] == frame_cols[None, :])
    return jnp.where(allowed[None], scores, -jnp.inf)


def attend_forward(queries, far_rows, scene_rows, frame_rows, frame_cols, use_frame):
    key_all, value_all, scene_cols = far_rows
    block_rows = math.gcd(key_all.shape[0], 512)
    block_count = key_all.shape[0] // block_rows
    stat_shape = (queries.shape[1], queries.shape[0])

    def scores_at(number):
        key_block, value_block, scene_block, frame_block = slice_keys(
            (key_all, value_all, scene_cols, frame_cols), number, block_rows
        )
        return (
            scores_of(
                queries, key_block, scene_rows, scene_block, frame_rows, frame_block, use_frame
            ),
            value_block,
        )

    def output_from(scores, value_block, log_sum):
        probs = jnp.exp(scores - log_sum[..., None]).astype(jnp.bfloat16)
        return jnp.einsum("hqk,khd->qhd", probs, value_block, preferred_element_type=jnp.float32)

    if block_count == 1:
        scores, value_block = scores_at(0)
        top_now = jnp.max(scores, axis=-1)
        log_sum = top_now + jnp.log(jnp.sum(jnp.exp(scores - top_now[..., None]), axis=-1))
        return (output_from(scores, value_block, log_sum), log_sum)

    def advance_stats(state_pair, number):
        top_now, running_sum = state_pair
        scores, value_block = scores_at(number)
        top_new = jnp.maximum(top_now, jnp.max(scores, axis=-1))
        running_sum = running_sum * jnp.exp(top_now - top_new) + jnp.sum(
            jnp.exp(scores - top_new[..., None]), axis=-1
        )
        return ((top_new, running_sum), None)

    start_pair = (jnp.full(stat_shape, FLOOR, jnp.float32), jnp.zeros(stat_shape, jnp.float32))
    (top_now, running_sum), _ = lax.scan(advance_stats, start_pair, jnp.arange(block_count))
    log_sum = top_now + jnp.log(running_sum)

    def advance_output(accumulated, number):
        scores, value_block = scores_at(number)
        return (accumulated + output_from(scores, value_block, log_sum), None)

    start_out = jnp.zeros((queries.shape[0], queries.shape[1], value_all.shape[-1]), jnp.float32)
    attended, _ = lax.scan(advance_output, start_out, jnp.arange(block_count))
    return (attended, log_sum)


def attend_backward(
    queries, far_rows, scene_rows, frame_rows, frame_cols, use_frame, log_sum, grad_out
):
    key_all, value_all, scene_cols = far_rows
    block_rows = math.gcd(key_all.shape[0], 512)
    block_count = key_all.shape[0] // block_rows
    score_scale = queries.shape[-1] ** (-0.5)

    def probs_at(number):
        key_block, value_block, scene_block, frame_block = slice_keys(
            (key_all, value_all, scene_cols, frame_cols), number, block_rows
        )
        scores = scores_of(
            queries, key_block, scene_rows, scene_block, frame_rows, frame_block, use_frame
        )
        probs = jnp.exp(scores - log_sum[..., None])
        grad_probs = jnp.einsum(
            "qhd,khd->hqk", grad_out, value_block, preferred_element_type=jnp.float32
        )
        return (probs, grad_probs, key_block)

    def grads_from(probs, grad_probs, delta, key_block):
        grad_scores = (probs * (grad_probs - delta[..., None])).astype(jnp.bfloat16)
        query_part = jnp.einsum(
            "hqk,khd->qhd", grad_scores, key_block, preferred_element_type=jnp.float32
        )
        key_part = (
            jnp.einsum("hqk,qhd->khd", grad_scores, queries, preferred_element_type=jnp.float32)
            * score_scale
        )
        value_part = jnp.einsum(
            "hqk,qhd->khd", probs.astype(jnp.bfloat16), grad_out, preferred_element_type=jnp.float32
        )
        return (query_part, key_part, value_part)

    if block_count == 1:
        probs, grad_probs, key_block = probs_at(0)
        delta = jnp.sum(probs * grad_probs, axis=-1)
        query_part, key_grad, value_grad = grads_from(probs, grad_probs, delta, key_block)
        return (query_part * score_scale, key_grad, value_grad)

    def advance_delta(delta, number):
        probs, grad_probs, key_block = probs_at(number)
        return (delta + jnp.sum(probs * grad_probs, axis=-1), None)

    delta, _ = lax.scan(
        advance_delta, jnp.zeros(log_sum.shape, jnp.float32), jnp.arange(block_count)
    )

    def advance_grads(query_grad, number):
        probs, grad_probs, key_block = probs_at(number)
        query_part, key_part, value_part = grads_from(probs, grad_probs, delta, key_block)
        return (query_grad + query_part, (key_part, value_part))

    start_grad = jnp.zeros(queries.shape, jnp.float32)
    query_grad, (key_grad, value_grad) = lax.scan(
        advance_grads, start_grad, jnp.arange(block_count)
    )
    key_grad = key_grad.reshape(key_all.shape)
    value_grad = value_grad.reshape(value_all.shape)
    return (query_grad * score_scale, key_grad, value_grad)


def block_forward(stream, gathered, head_gain, head_shift, scene_ids, frame_index, use_frame):
    (
        weight_qkv,
        bias_qkv,
        weight_proj,
        weight_up,
        bias_up,
        weight_down,
        out_shift,
        gains,
        shifts,
        scales,
    ) = gathered
    row_count, model_width = stream.shape
    head_size = head_gain.shape[-1]
    head_count = model_width // head_size
    gains = gains.astype(jnp.float32)
    shifts = shifts.astype(jnp.float32)
    scales = scales.astype(jnp.float32)
    out_shift = out_shift.astype(jnp.float32)
    first_normed = layer_norm(stream, gains[0], shifts[0]).astype(jnp.bfloat16)
    mixed = jnp.dot(first_normed, weight_qkv, preferred_element_type=jnp.float32) + bias_qkv.astype(
        jnp.float32
    )
    mixed = mixed.reshape(row_count, 3, head_count, head_size)
    queries = layer_norm(mixed[:, 0], head_gain[0], head_shift[0]).astype(jnp.bfloat16)
    keys_own = layer_norm(mixed[:, 1], head_gain[1], head_shift[1]).astype(jnp.bfloat16)
    values_own = mixed[:, 2].astype(jnp.bfloat16)
    if use_frame:
        far_rows = (keys_own, values_own, scene_ids)
        frame_cols = frame_index
    else:
        far_rows = (
            lax.all_gather(keys_own, "frame", axis=0, tiled=True),
            lax.all_gather(values_own, "frame", axis=0, tiled=True),
            lax.all_gather(scene_ids, "frame", axis=0, tiled=True),
        )
        frame_cols = far_rows[2]
    attended, log_sum = attend_forward(
        queries, far_rows, scene_ids, frame_index, frame_cols, use_frame
    )
    flat_out = attended.astype(jnp.bfloat16).reshape(row_count, model_width)
    branch_one = jnp.dot(flat_out, weight_proj, preferred_element_type=jnp.float32) + out_shift[0]
    middle = stream + scales[0] * branch_one
    second_normed = layer_norm(middle, gains[1], shifts[1]).astype(jnp.bfloat16)
    pre_act = jnp.dot(
        second_normed, weight_up, preferred_element_type=jnp.float32
    ) + bias_up.astype(jnp.float32)
    hidden = exact_gelu(pre_act).astype(jnp.bfloat16)
    branch_two = jnp.dot(hidden, weight_down, preferred_element_type=jnp.float32) + out_shift[1]
    output = middle + scales[1] * branch_two
    saved_state = (
        stream,
        first_normed,
        mixed,
        queries,
        keys_own,
        values_own,
        far_rows,
        log_sum,
        flat_out,
        branch_one,
        middle,
        second_normed,
        pre_act,
        hidden,
        branch_two,
    )
    return (output, saved_state)


def block_backward(
    grad_stream, saved_state, gathered, head_gain, head_shift, scene_ids, frame_index, use_frame
):
    (
        stream,
        first_normed,
        mixed,
        queries,
        keys_own,
        values_own,
        far_saved,
        log_sum,
        flat_out,
        branch_one,
        middle,
        second_normed,
        pre_act,
        hidden,
        branch_two,
    ) = saved_state
    (
        weight_qkv,
        bias_qkv,
        weight_proj,
        weight_up,
        bias_up,
        weight_down,
        out_shift,
        gains,
        shifts,
        scales,
    ) = gathered
    row_count, model_width = stream.shape
    head_size = head_gain.shape[-1]
    head_count = model_width // head_size
    gains = gains.astype(jnp.float32)
    shifts = shifts.astype(jnp.float32)
    scales = scales.astype(jnp.float32)
    scale_two = jnp.sum(grad_stream * branch_two, axis=0)
    grad_branch = grad_stream * scales[1]
    shift_two = jnp.sum(grad_branch, axis=0)
    branch_low = grad_branch.astype(jnp.bfloat16)
    grad_down = jnp.einsum("tf,td->fd", hidden, branch_low, preferred_element_type=jnp.float32)
    grad_hidden = jnp.einsum(
        "td,fd->tf", branch_low, weight_down, preferred_element_type=jnp.float32
    )
    _, gelu_back = jax.vjp(exact_gelu, pre_act)
    grad_pre = gelu_back(grad_hidden)[0]
    grad_bias_up = jnp.sum(grad_pre, axis=0)
    pre_low = grad_pre.astype(jnp.bfloat16)
    grad_up = jnp.einsum("tc,tf->cf", second_normed, pre_low, preferred_element_type=jnp.float32)
    grad_second = jnp.einsum("tf,cf->tc", pre_low, weight_up, preferred_element_type=jnp.float32)
    _, norm_two_back = jax.vjp(layer_norm, middle, gains[1], shifts[1])
    middle_part, gain_two, shift_norm_two = norm_two_back(grad_second)
    grad_middle = grad_stream + middle_part
    scale_one = jnp.sum(grad_middle * branch_one, axis=0)
    grad_att = grad_middle * scales[0]
    shift_one = jnp.sum(grad_att, axis=0)
    att_low = grad_att.astype(jnp.bfloat16)
    grad_proj = jnp.einsum("tc,td->cd", flat_out, att_low, preferred_element_type=jnp.float32)
    grad_flat = jnp.einsum("td,cd->tc", att_low, weight_proj, preferred_element_type=jnp.float32)
    grad_flat = grad_flat.astype(jnp.bfloat16).reshape(row_count, head_count, head_size)
    if use_frame:
        far_rows = far_saved
        frame_cols = frame_index
    else:
        far_rows = (
            lax.all_gather(keys_own, "frame", axis=0, tiled=True),
            lax.all_gather(values_own, "frame", axis=0, tiled=True),
            lax.all_gather(scene_ids, "frame", axis=0, tiled=True),
        )
        frame_cols = far_rows[2]
    grad_query, grad_keys, grad_values = attend_backward(
        queries, far_rows, scene_ids, frame_index, frame_cols, use_frame, log_sum, grad_flat
    )
    if not use_frame:
        grad_keys, grad_values = (
            lax.psum_scatter(
                grad_keys.astype(jnp.bfloat16), "frame", scatter_dimension=0, tiled=True
            ).astype(jnp.float32),
            lax.psum_scatter(
                grad_values.astype(jnp.bfloat16), "frame", scatter_dimension=0, tiled=True
            ).astype(jnp.float32),
        )
    _, query_norm_back = jax.vjp(layer_norm, mixed[:, 0], head_gain[0], head_shift[0])
    mixed_query, query_gain, query_shift = query_norm_back(grad_query)
    _, key_norm_back = jax.vjp(layer_norm, mixed[:, 1], head_gain[1], head_shift[1])
    mixed_key, key_gain, key_shift = key_norm_back(grad_keys)
    grad_mixed = jnp.stack([mixed_query, mixed_key, grad_values], axis=1).reshape(
        row_count, 3 * model_width
    )
    grad_bias_qkv = jnp.sum(grad_mixed, axis=0)
    mixed_low = grad_mixed.astype(jnp.bfloat16)
    grad_qkv = jnp.einsum("tc,te->ce", first_normed, mixed_low, preferred_element_type=jnp.float32)
    grad_first = jnp.einsum("te,ce->tc", mixed_low, weight_qkv, preferred_element_type=jnp.float32)
    _, norm_one_back = jax.vjp(layer_norm, stream, gains[0], shifts[0])
    stream_part, gain_one, shift_norm_one = norm_one_back(grad_first)
    grad_input = grad_middle + stream_part
    vector_grads = jnp.stack(
        [
            jnp.stack([shift_one, shift_two]),
            jnp.stack([gain_one, gain_two]),
            jnp.stack([shift_norm_one, shift_norm_two]),
            jnp.stack([scale_one, scale_two]),
        ]
    )
    local_grads = (
        grad_qkv,
        grad_bias_qkv,
        grad_proj,
        grad_up,
        grad_bias_up,
        grad_down,
        vector_grads,
    )
    head_grads = (jnp.stack([query_gain, key_gain]), jnp.stack([query_shift, key_shift]))
    return (grad_input, local_grads, head_grads)


def on_device(
    tokens,
    cotangent,
    scene_ids,
    frame_index,
    qkv_weight,
    qkv_bias,
    proj_weight,
    fc1_weight,
    fc1_bias,
    fc2_weight,
    out_bias,
    norm_gain,
    norm_bias,
    layer_scale,
    qk_gain,
    qk_bias,
):
    stream = tokens.astype(jnp.float32)
    gathered_all = []
    saved_all = []
    for depth in range(2):
        gathered = (
            lax.all_gather(qkv_weight[depth], ("scene", "frame"), axis=0, tiled=True),
            lax.all_gather(qkv_bias[depth], ("scene", "frame"), axis=0, tiled=True),
            lax.all_gather(proj_weight[depth], ("scene", "frame"), axis=0, tiled=True),
            lax.all_gather(fc1_weight[depth], ("scene", "frame"), axis=0, tiled=True),
            lax.all_gather(fc1_bias[depth], ("scene", "frame"), axis=0, tiled=True),
            lax.all_gather(fc2_weight[depth], ("scene", "frame"), axis=0, tiled=True),
            lax.all_gather(out_bias[depth], ("scene", "frame"), axis=1, tiled=True),
            lax.all_gather(norm_gain[depth], ("scene", "frame"), axis=1, tiled=True),
            lax.all_gather(norm_bias[depth], ("scene", "frame"), axis=1, tiled=True),
            lax.all_gather(layer_scale[depth], ("scene", "frame"), axis=1, tiled=True),
        )
        stream, saved_state = block_forward(
            stream,
            gathered,
            qk_gain[depth].astype(jnp.float32),
            qk_bias[depth].astype(jnp.float32),
            scene_ids,
            frame_index,
            depth == 0,
        )
        gathered_all.append(gathered)
        saved_all.append(saved_state)
    grad_stream = cotangent.astype(jnp.float32)
    shares = [None, None]
    head_terms = [None, None]
    for depth in (1, 0):
        gathered = (
            lax.all_gather(qkv_weight[depth], ("scene", "frame"), axis=0, tiled=True),
            lax.all_gather(qkv_bias[depth], ("scene", "frame"), axis=0, tiled=True),
            lax.all_gather(proj_weight[depth], ("scene", "frame"), axis=0, tiled=True),
            lax.all_gather(fc1_weight[depth], ("scene", "frame"), axis=0, tiled=True),
            lax.all_gather(fc1_bias[depth], ("scene", "frame"), axis=0, tiled=True),
            lax.all_gather(fc2_weight[depth], ("scene", "frame"), axis=0, tiled=True),
            lax.all_gather(out_bias[depth], ("scene", "frame"), axis=1, tiled=True),
            lax.all_gather(norm_gain[depth], ("scene", "frame"), axis=1, tiled=True),
            lax.all_gather(norm_bias[depth], ("scene", "frame"), axis=1, tiled=True),
            lax.all_gather(layer_scale[depth], ("scene", "frame"), axis=1, tiled=True),
        )
        grad_stream, local_grads, head_grads = block_backward(
            grad_stream,
            saved_all[depth],
            gathered,
            qk_gain[depth].astype(jnp.float32),
            qk_bias[depth].astype(jnp.float32),
            scene_ids,
            frame_index,
            depth == 0,
        )
        width = local_grads[6].shape[-1]
        vector_rows = local_grads[6].reshape(8, width).T
        summed = (
            lax.psum_scatter(local_grads[0], ("scene", "frame"), scatter_dimension=0, tiled=True),
            lax.psum_scatter(local_grads[1], ("scene", "frame"), scatter_dimension=0, tiled=True),
            lax.psum_scatter(local_grads[2], ("scene", "frame"), scatter_dimension=0, tiled=True),
            lax.psum_scatter(local_grads[3], ("scene", "frame"), scatter_dimension=0, tiled=True),
            lax.psum_scatter(local_grads[4], ("scene", "frame"), scatter_dimension=0, tiled=True),
            lax.psum_scatter(local_grads[5], ("scene", "frame"), scatter_dimension=0, tiled=True),
            lax.psum_scatter(vector_rows, ("scene", "frame"), scatter_dimension=0, tiled=True),
        )
        vector_share = summed[6].T.reshape(4, 2, summed[6].shape[0])
        shares[depth] = (
            summed[0],
            summed[1],
            summed[2],
            summed[3],
            summed[4],
            summed[5],
            vector_share[0],
            vector_share[1],
            vector_share[2],
            vector_share[3],
        )
        head_terms[depth] = head_grads
    head_sums = lax.psum(
        (
            jnp.stack([head_terms[0][0], head_terms[1][0]]),
            jnp.stack([head_terms[0][1], head_terms[1][1]]),
        ),
        ("scene", "frame"),
    )
    stacked = [jnp.stack([shares[0][member], shares[1][member]]) for member in range(10)]
    return (
        stream.astype(jnp.bfloat16),
        grad_stream.astype(jnp.bfloat16),
        stacked[0],
        stacked[1],
        stacked[2],
        stacked[3],
        stacked[4],
        stacked[5],
        stacked[6],
        stacked[7],
        stacked[8],
        stacked[9],
        head_sums[0],
        head_sums[1],
    )


def solution(mesh):
    return jax.shard_map(
        on_device,
        mesh=mesh,
        in_specs=(
            P(("scene", "frame"), None),
            P(("scene", "frame"), None),
            P(("scene", "frame")),
            P(("scene", "frame")),
            P(None, ("scene", "frame"), None),
            P(None, ("scene", "frame")),
            P(None, ("scene", "frame"), None),
            P(None, ("scene", "frame"), None),
            P(None, ("scene", "frame")),
            P(None, ("scene", "frame"), None),
            P(None, None, ("scene", "frame")),
            P(None, None, ("scene", "frame")),
            P(None, None, ("scene", "frame")),
            P(None, None, ("scene", "frame")),
            P(),
            P(),
        ),
        out_specs=(
            P(("scene", "frame"), None),
            P(("scene", "frame"), None),
            P(None, ("scene", "frame"), None),
            P(None, ("scene", "frame")),
            P(None, ("scene", "frame"), None),
            P(None, ("scene", "frame"), None),
            P(None, ("scene", "frame")),
            P(None, ("scene", "frame"), None),
            P(None, None, ("scene", "frame")),
            P(None, None, ("scene", "frame")),
            P(None, None, ("scene", "frame")),
            P(None, None, ("scene", "frame")),
            P(),
            P(),
        ),
        check_vma=False,
    )
```

profile of v0, /device:TPU:7, one launch (start us, length us, event | category | flops | bytes accessed | tf_op | source)
XLA Modules:
  0.0 3289.0 jit_solution(11617729317311721626)
XLA Ops:
  16.4 59.2 %all-gather.1 = bf16[1,2,1024]{1,0,2:T(2,128)(2,1)S(1)} all-gather(bf16[1,2,32]{1,0,2:T(2,128)(2,1)S(1)} %copy.101), channel_id=3, replica_groups=mesh['scene'=16,'frame'=2] {'scene','frame'}, dimensions={2}, use_global_device_ids=true | all-gather | bytes 4224 | tf_op jit(solution)/shard_map/all_gather | solution.py:372
  76.6 49.8 %all-reduce.7 = (bf16[3072]{0:T(1024)(128)(2,1)S(1)}, bf16[3072]{0:T(1024)(128)(2,1)S(1)}) all-reduce(bf16[3072]{0:T(1024)(128)(2,1)S(1)} %dynamic-update-slice, bf16[3072]{0:T(1024)(128)(2,1)S(1)} %dynamic-update-slice.1), channel_id=6, replica_groups=mesh['scene'=16,'frame'=2] {'scene','frame'}, use_global_device_ids=true, to_apply=%add | all-reduce | flops 6144 | bytes 24576
  126.6 60.2 %all-gather.2 = bf16[1,2,1024]{1,0,2:T(2,128)(2,1)S(1)} all-gather(bf16[1,2,32]{1,0,2:T(2,128)(2,1)S(1)} %copy.102), channel_id=4, replica_groups=mesh['scene'=16,'frame'=2] {'scene','frame'}, dimensions={2}, use_global_device_ids=true | all-gather | bytes 4224 | tf_op jit(solution)/shard_map/all_gather | solution.py:373
  187.4 68.8 %all-gather = bf16[1,2,1024]{1,0,2:T(2,128)(2,1)S(1)} all-gather(bf16[1,2,32]{1,0,2:T(2,128)(2,1)S(1)} %copy.100), channel_id=2, replica_groups=mesh['scene'=16,'frame'=2] {'scene','frame'}, dimensions={2}, use_global_device_ids=true | all-gather | bytes 4224 | tf_op jit(solution)/shard_map/all_gather | solution.py:374
  256.9 68.8 %all-gather.6 = bf16[1,2,1024]{1,0,2:T(2,128)(2,1)S(1)} all-gather(bf16[1,2,32]{1,0,2:T(2,128)(2,1)S(1)} %copy.103), channel_id=8, replica_groups=mesh['scene'=16,'frame'=2] {'scene','frame'}, dimensions={2}, use_global_device_ids=true | all-gather | bytes 4224 | tf_op jit(solution)/shard_map/all_gather | solution.py:371
  326.2 65.7 %all-gather.8 = bf16[1,4096]{1,0:T(2,128)(2,1)S(1)} all-gather(bf16[1,128]{1,0:T(2,128)(2,1)S(1)} %get-tuple-element.137), channel_id=10, replica_groups=mesh['scene'=16,'frame'=2] {'scene','frame'}, dimensions={1}, use_global_device_ids=true | all-gather | bytes 8448 | tf_op jit(solution)/shard_map/all_gather | solution.py:369
  392.1 67.9 %all-gather.11 = bf16[1,2,1024]{1,0,2:T(2,128)(2,1)S(1)} all-gather(bf16[1,2,32]{1,0,2:T(2,128)(2,1)S(1)} %copy.105), channel_id=13, replica_groups=mesh['scene'=16,'frame'=2] {'scene','frame'}, dimensions={2}, use_global_device_ids=true | all-gather | bytes 4224 | tf_op jit(solution)/shard_map/all_gather | solution.py:372
  461.2 70.0 %all-gather.12 = bf16[1,2,1024]{1,0,2:T(2,128)(2,1)S(1)} all-gather(bf16[1,2,32]{1,0,2:T(2,128)(2,1)S(1)} %copy.106), channel_id=14, replica_groups=mesh['scene'=16,'frame'=2] {'scene','frame'}, dimensions={2}, use_global_device_ids=true | all-gather | bytes 4224 | tf_op jit(solution)/shard_map/all_gather | solution.py:373
  531.9 71.0 %all-gather.10 = bf16[1,2,1024]{1,0,2:T(2,128)(2,1)S(1)} all-gather(bf16[1,2,32]{1,0,2:T(2,128)(2,1)S(1)} %copy.104), channel_id=12, replica_groups=mesh['scene'=16,'frame'=2] {'scene','frame'}, dimensions={2}, use_global_device_ids=true | all-gather | bytes 4224 | tf_op jit(solution)/shard_map/all_gather | solution.py:374
  604.4 66.2 %all-gather.17 = bf16[1,2,1024]{1,0,2:T(2,128)(2,1)S(1)} all-gather(bf16[1,2,32]{1,0,2:T(2,128)(2,1)S(1)} %copy.107), channel_id=19, replica_groups=mesh['scene'=16,'frame'=2] {'scene','frame'}, dimensions={2}, use_global_device_ids=true | all-gather | bytes 4224 | tf_op jit(solution)/shard_map/all_gather | solution.py:371
  671.1 63.0 %all-gather.19 = bf16[1,4096]{1,0:T(2,128)(2,1)S(1)} all-gather(bf16[1,128]{1,0:T(2,128)(2,1)S(1)} %get-tuple-element.136), channel_id=21, replica_groups=mesh['scene'=16,'frame'=2] {'scene','frame'}, dimensions={1}, use_global_device_ids=true | all-gather | bytes 8448 | tf_op jit(solution)/shard_map/all_gather | solution.py:369
  741.4 6.2 slice_reduce_fusion.10
  747.6 6.2 slice_reduce_fusion.9
  753.8 6.3 slice_reduce_fusion.11
  760.1 6.7 slice_reduce_fusion.8
  766.8 6.6 slice_reduce_fusion.2
  773.4 6.2 slice_reduce_fusion.1
  779.6 6.2 slice_reduce_fusion.3
  785.8 6.9 slice_reduce_fusion
  792.7 5.0 fusion.30
  805.1 6.1 fusion.24
  811.2 10.6 fusion.156
  830.4 6.0 all_gather.101
  836.4 7.5 all-gather.15
  852.4 6.2 fusion.27
  858.6 10.7 fusion.169
  873.1 7.0 fusion.90
  902.4 14.6 reduce-scatter.37.cloned.1.call-done
  924.4 9.3 reduce-scatter.39.cloned.1.call-done
  936.5 5.4 multiply_reduce_fusion.4
  943.6 10.7 fusion.170
  981.6 6.4 fusion.145
  989.1 6.4 fusion.149
  997.1 9.7 fusion.122
  1008.6 9.7 fusion.131
  1019.7 8.2 fusion.116
  1029.2 8.2 fusion.113
  1042.6 40.6 %all-reduce.6 = (f32[3072]{0:T(1024)S(1)}, f32[3072]{0:T(1024)S(1)}, f32[4096]{0:T(1024)S(1)}, f32[4096]{0:T(1024)S(1)}, f32[2,2,64]{2,1,0:T(2,128)}, /*index=5*/f32[2,2,64]{2,1,0:T(2,128)}) all-reduce(f32[3072]{0:T(1024)S(1)} %reduce_sum.636, ...), channel_id=28, replica_groups=mesh['scene'=16,'frame'=2] {'scene','frame'}, use_global_device_ids=true, to_apply=%region_45.46.clone | all-reduce | flops 14848 | bytes 118784
  1085.6 8.1 reduce-scatter.41.cloned.1.call-done
  1094.5 131.4 %reduce-scatter.43.cloned.1.call-done = f32[32,8]{1,0:T(8,128)} async-done(((f32[1024,8]{1,0:T(8,128)}), f32[32,8]{1,0:T(8,128)}) %reduce-scatter.43.cloned.1.call-update) | async-done | bytes 1040
  1229.0 139.2 %reduce-scatter.27.cloned.1.call-done = f32[32,1024]{1,0:T(8,128)} async-done(((f32[1024,1024]{1,0:T(8,128)}), f32[32,1024]{1,0:T(8,128)}) %reduce-scatter.27.cloned.1.call-update) | async-done | bytes 131088 | tf_op jit(solution)/shard_map/reduce_scatter | solution.py:418
  1368.2 141.1 %reduce-scatter.25.cloned.1.call-done = f32[32,1024]{1,0:T(8,128)} async-done(((f32[1024,1024]{1,0:T(8,128)}), f32[32,1024]{1,0:T(8,128)}) %reduce-scatter.25.cloned.1.call-update) | async-done | bytes 131088 | tf_op jit(solution)/shard_map/reduce_scatter | solution.py:418
  1511.0 166.9 %reduce-scatter.21.cloned.1.call-done = f32[32,3072]{1,0:T(8,128)} async-done(((f32[1024,3072]{1,0:T(8,128)}), f32[32,3072]{1,0:T(8,128)}) %reduce-scatter.21.cloned.1.call-update) | async-done | bytes 393232 | tf_op jit(solution)/shard_map/reduce_scatter | solution.py:416
  1677.9 161.4 %reduce-scatter.23.cloned.1.call-done = f32[32,3072]{1,0:T(8,128)} async-done(((f32[1024,3072]{1,0:T(8,128)}), f32[32,3072]{1,0:T(8,128)}) %reduce-scatter.23.cloned.1.call-update) | async-done | bytes 393232 | tf_op jit(solution)/shard_map/reduce_scatter | solution.py:416
  1841.3 355.9 %reduce-scatter.35.cloned.1.call-done = f32[128,1024]{1,0:T(8,128)} async-done(((f32[4096,1024]{1,0:T(8,128)}), f32[128,1024]{1,0:T(8,128)}) %reduce-scatter.35.cloned.1.call-update) | async-done | bytes 524304 | tf_op jit(solution)/shard_map/reduce_scatter | solution.py:421
  2197.3 360.7 %reduce-scatter.33.cloned.1.call-done = f32[128,1024]{1,0:T(8,128)} async-done(((f32[4096,1024]{1,0:T(8,128)}), f32[128,1024]{1,0:T(8,128)}) %reduce-scatter.33.cloned.1.call-update) | async-done | bytes 524304 | tf_op jit(solution)/shard_map/reduce_scatter | solution.py:421
  2560.3 358.7 %reduce-scatter.31.cloned.1.call-done = f32[32,4096]{1,0:T(8,128)} async-done(((f32[1024,4096]{1,0:T(8,128)}), f32[32,4096]{1,0:T(8,128)}) %reduce-scatter.31.cloned.1.call-update) | async-done | bytes 524304 | tf_op jit(solution)/shard_map/reduce_scatter | solution.py:419
  2918.9 360.8 %reduce-scatter.29.cloned.1.call-done = f32[32,4096]{1,0:T(8,128)} async-done(((f32[1024,4096]{1,0:T(8,128)}), f32[32,4096]{1,0:T(8,128)}) %reduce-scatter.29.cloned.1.call-update) | async-done | bytes 524304 | tf_op jit(solution)/shard_map/reduce_scatter | solution.py:419
  (561 shorter events, 137.9 us)
Async XLA Ops:
  7.2 785.5 %all-gather.31.cloned.1.call-start = ((), (), s32[]{:S(2)}) async-start(), calls=%async_computation.20 | async-start | bytes 6488064 | tf_op jit(solution)/shard_map/all_gather | solution.py:365
  9.1 792.3 %all-gather.33.cloned.1.call-start = ((), (), s32[]{:S(2)}) async-start(), calls=%async_computation.21 | async-start | bytes 2162688 | tf_op jit(solution)/shard_map/all_gather | solution.py:367
  10.7 793.9 %all-gather.35.cloned.1.call-start = ((), (), s32[]{:S(2)}) async-start(), calls=%async_computation.22 | async-start | bytes 8650752 | tf_op jit(solution)/shard_map/all_gather | solution.py:368
  12.6 63.5 %copy-start.134 = (bf16[2,96]{1,0:T(2,128)(2,1)S(1)}, bf16[2,96]{1,0:T(2,128)(2,1)}, u32[]{:S(2)}) copy-start(bf16[2,96]{1,0:T(2,128)(2,1)} %param.21) | copy-start | bytes 1156
  12.6 113.9 %copy-start.140 = (bf16[2,2,32]{2,1,0:T(2,128)(2,1)S(1)}, bf16[2,2,32]{2,1,0:T(2,128)(2,1)}, u32[]{:S(2)}) copy-start(bf16[2,2,32]{2,1,0:T(2,128)(2,1)} %param.28) | copy-start | bytes 772
  12.6 798.5 %all-gather.37.cloned.1.call-start = ((), (), s32[]{:S(2)}) async-start(), calls=%async_computation.23 | async-start | bytes 8650752 | tf_op jit(solution)/shard_map/all_gather | solution.py:370
  13.5 173.8 %copy-start.141 = (bf16[2,2,32]{2,1,0:T(2,128)(2,1)S(1)}, bf16[2,2,32]{2,1,0:T(2,128)(2,1)}, u32[]{:S(2)}) copy-start(bf16[2,2,32]{2,1,0:T(2,128)(2,1)} %param.29) | copy-start | bytes 772
  13.5 808.5 %all-gather.39.cloned.1.call-start = ((), (), s32[]{:S(2)}) async-start(), calls=%async_computation.24 | async-start | bytes 6488064 | tf_op jit(solution)/shard_map/all_gather | solution.py:365
  14.1 833.7 %all-gather.41.cloned.1.call-start = ((), (), s32[]{:S(2)}) async-start(), calls=%async_computation.25 | async-start | bytes 2162688 | tf_op jit(solution)/shard_map/all_gather | solution.py:367
  14.7 837.2 %all-gather.43.cloned.1.call-start = ((), (), s32[]{:S(2)}) async-start(), calls=%async_computation.26 | async-start | bytes 8650752 | tf_op jit(solution)/shard_map/all_gather | solution.py:368
  15.5 843.1 %all-gather.45.cloned.1.call-start = ((), (), s32[]{:S(2)}) async-start(), calls=%async_computation.27 | async-start | bytes 8650752 | tf_op jit(solution)/shard_map/all_gather | solution.py:370
  16.2 900.8 %reduce-scatter.37.cloned.1.call-start = ((), (), s32[]{:S(2)}) async-start(), calls=%async_computation.28 | async-start | bytes 786432
  75.6 181.2 %copy-start.142 = (bf16[2,2,32]{2,1,0:T(2,128)(2,1)S(1)}, bf16[2,2,32]{2,1,0:T(2,128)(2,1)}, u32[]{:S(2)}) copy-start(bf16[2,2,32]{2,1,0:T(2,128)(2,1)} %param.26) | copy-start | bytes 772
  186.8 139.4 %copy-start.135 = (bf16[2,128]{1,0:T(2,128)(2,1)S(1)}, bf16[2,128]{1,0:T(2,128)(2,1)}, u32[]{:S(2)}) copy-start(bf16[2,128]{1,0:T(2,128)(2,1)} %param.24) | copy-start | bytes 1540
  531.2 203.5 %copy-start.117 = (s32[128]{0:T(128)S(1)}, s32[128]{0:T(128)}, u32[]{:S(2)}) copy-start(s32[128]{0:T(128)} %param.18) | copy-start | bytes 1540
  531.2 207.8 %copy-start.10 = (bf16[128,1024]{1,0:T(8,128)(2,1)S(1)}, bf16[128,1024]{1,0:T(8,128)(2,1)}, u32[]{:S(2)}) copy-start(bf16[128,1024]{1,0:T(8,128)(2,1)} %param.16) | copy-start | bytes 786436
  531.8 207.7 %copy-start.137 = (bf16[2,2,64]{2,1,0:T(2,128)(2,1)S(1)}, bf16[2,2,64]{2,1,0:T(2,128)(2,1)}, u32[]{:S(2)}) copy-start(bf16[2,2,64]{2,1,0:T(2,128)(2,1)} %param.30) | copy-start | bytes 1540
  531.8 207.7 %copy-start.138 = (bf16[2,2,64]{2,1,0:T(2,128)(2,1)S(1)}, bf16[2,2,64]{2,1,0:T(2,128)(2,1)}, u32[]{:S(2)}) copy-start(bf16[2,2,64]{2,1,0:T(2,128)(2,1)} %param.31) | copy-start | bytes 1540
  531.8 208.8 %copy-start.133 = (s32[128]{0:T(128)S(1)}, s32[128]{0:T(128)}, u32[]{:S(2)}) copy-start(s32[128]{0:T(128)} %param.19) | copy-start | bytes 1540
  739.2 53.5 %copy-start.81 = (f32[128]{0:T(128)}, f32[128]{0:T(128)S(1)}, u32[]{:S(2)}) copy-start(f32[128]{0:T(128)S(1)} %broadcast_multiply_fusion.10) | copy-start | bytes 1540
  739.5 53.3 %copy-start.87 = (f32[128]{0:T(128)}, f32[128]{0:T(128)S(1)}, u32[]{:S(2)}) copy-start(f32[128]{0:T(128)S(1)} %fusion.138) | copy-start | bytes 1540
  753.7 39.0 %copy-start.65 = (f32[1024]{0:T(1024)}, f32[1024]{0:T(1024)S(1)}, u32[]{:S(2)}) copy-start(f32[1024]{0:T(1024)S(1)} %get-tuple-element.63) | copy-start | bytes 12292
  753.8 51.3 %copy-start.61 = (f32[1024]{0:T(1024)}, f32[1024]{0:T(1024)S(1)}, u32[]{:S(2)}) copy-start(f32[1024]{0:T(1024)S(1)} %get-tuple-element.62) | copy-start | bytes 12292
  753.8 25.9 copy-start.35
  779.6 72.7 %copy-start.63 = (f32[1024]{0:T(1024)}, f32[1024]{0:T(1024)S(1)}, u32[]{:S(2)}) copy-start(f32[1024]{0:T(1024)S(1)} %get-tuple-element.54) | copy-start | bytes 12292
  829.6 14.3 copy-start.118
  829.9 15.9 copy-start.73
  850.9 22.1 copy-start.93
  851.9 21.1 copy-start.109
  858.6 14.4 copy-start.160
  892.5 41.3 %reduce-scatter.39.cloned.1.call-start = ((), (), s32[]{:S(2)}) async-start(), calls=%async_computation.29 | async-start | bytes 786432
  897.5 21.3 copy-start.2
  897.5 21.3 copy-start.112
  899.6 23.8 copy-start.17
  899.7 21.2 copy-start.72
  899.7 194.0 %reduce-scatter.41.cloned.1.call-start = ((), (), s32[]{:S(2)}) async-start(), calls=%async_computation.30 | async-start | bytes 540672
  936.5 17.7 slice-start
  943.1 15.1 copy-start.53
  973.0 252.9 %reduce-scatter.43.cloned.1.call-start = ((), (), s32[]{:S(2)}) async-start(), calls=%async_computation.31 | async-start | bytes 540672
  974.2 394.0 %reduce-scatter.27.cloned.1.call-start = ((), (), s32[]{:S(2)}) async-start(), calls=%async_computation.15 | async-start | bytes 4325376 | tf_op jit(solution)/shard_map/reduce_scatter | solution.py:418
  977.1 532.2 %reduce-scatter.25.cloned.1.call-start = ((), (), s32[]{:S(2)}) async-start(), calls=%async_computation.14 | async-start | bytes 4325376 | tf_op jit(solution)/shard_map/reduce_scatter | solution.py:418
  980.9 697.0 %reduce-scatter.21.cloned.1.call-start = ((), (), s32[]{:S(2)}) async-start(), calls=%async_computation.12 | async-start | bytes 12976128 | tf_op jit(solution)/shard_map/reduce_scatter | solution.py:416
  988.0 851.3 %reduce-scatter.23.cloned.1.call-start = ((), (), s32[]{:S(2)}) async-start(), calls=%async_computation.13 | async-start | bytes 12976128 | tf_op jit(solution)/shard_map/reduce_scatter | solution.py:416
  995.6 1201.7 %reduce-scatter.35.cloned.1.call-start = ((), (), s32[]{:S(2)}) async-start(), calls=%async_computation.19 | async-start | bytes 17301504 | tf_op jit(solution)/shard_map/reduce_scatter | solution.py:421
  1006.9 1551.1 %reduce-scatter.33.cloned.1.call-start = ((), (), s32[]{:S(2)}) async-start(), calls=%async_computation.18 | async-start | bytes 17301504 | tf_op jit(solution)/shard_map/reduce_scatter | solution.py:421
  1018.3 1900.6 %reduce-scatter.31.cloned.1.call-start = ((), (), s32[]{:S(2)}) async-start(), calls=%async_computation.17 | async-start | bytes 17301504 | tf_op jit(solution)/shard_map/reduce_scatter | solution.py:419
  1027.9 2251.9 %reduce-scatter.29.cloned.1.call-start = ((), (), s32[]{:S(2)}) async-start(), calls=%async_computation.16 | async-start | bytes 17301504 | tf_op jit(solution)/shard_map/reduce_scatter | solution.py:419
  1038.7 46.0 %copy-start.40 = (f32[128,1024]{1,0:T(8,128)S(1)}, f32[128,1024]{1,0:T(8,128)}, u32[]{:S(2)}) copy-start(f32[128,1024]{1,0:T(8,128)} %copy-done.39) | copy-start | bytes 1572868
  (137 other events, 497.5 us)
Sparse Core Ops, SparseCore 0:
  10.9 73.1 all-gather.30
  87.1 56.2 all-gather.32
  147.0 81.7 all-gather.34
  232.2 81.0 all-gather.36
  316.6 67.7 all-gather.38
  387.3 56.1 all-gather.40
  447.1 80.6 all-gather.42
  531.3 79.9 all-gather.44
  892.6 24.3 reduce-scatter.36
  919.2 14.5 reduce-scatter.38
  973.1 120.4 reduce-scatter.40
  1095.9 129.9 reduce-scatter.42
  1228.1 140.0 reduce-scatter.26
  1370.3 138.9 reduce-scatter.24
  1515.2 162.6 reduce-scatter.20
  1684.8 154.4 reduce-scatter.22
  1841.4 355.7 reduce-scatter.34
  2199.4 358.5 reduce-scatter.32
  2560.3 358.6 reduce-scatter.30
  2921.1 358.6 reduce-scatter.28
where the time goes:
time: 3300 us; the launch traced here: 3290 us
  waiting for transfers between devices  2210 us (67%)
  blocking collectives  769 us (23%)
  matrix products  155 us (5%)
  local copies, waits for them, and re-layouts  94.9 us (3%)
  other arithmetic  41.1 us (1%)
    reduce_scatter x2, waiting for transfers between devices, on_device(): lax.psum_scatter(local_grads[3], ('scene', 'frame'), scatter_dimension=0,...  719 us
    reduce_scatter x2, waiting for transfers between devices, on_device(): lax.psum_scatter(local_grads[5], ('scene', 'frame'), scatter_dimension=0,...  717 us
    reduce_scatter x2, waiting for transfers between devices, on_device(): lax.psum_scatter(local_grads[0], ('scene', 'frame'), scatter_dimension=0,...  328 us
    reduce_scatter x2, waiting for transfers between devices, on_device(): lax.psum_scatter(local_grads[2], ('scene', 'frame'), scatter_dimension=0,...  280 us
    unnamed x24, waiting for transfers between devices  166 us
    all_gather x2, blocking collectives, on_device(): lax.all_gather(layer_scale[depth], ('scene', 'frame'), axis=1, tiled=True)  140 us
    all_gather x2, blocking collectives, on_device(): lax.all_gather(out_bias[depth], ('scene', 'frame'), axis=1, tiled=True)  135 us
    all_gather x2, blocking collectives, on_device(): lax.all_gather(norm_bias[depth], ('scene', 'frame'), axis=1, tiled=True)  130 us
  transfers between devices with their start and end apart: 20, of which 12 were waited for; matrix products, arithmetic and copies ran while one was open for 6% of the time, Pallas kernels for 0%

commit v1 on v0

v1 whole, which is shorter than its diff:
```python
import jax
import jax.numpy as jnp
import numpy as np
from jax import lax
from jax.sharding import Mesh
from jax.sharding import PartitionSpec as P

EPSILON = 1e-06
FRAME_TOK = 64
LOW = jnp.bfloat16
WIDE = jnp.float32
EVERY = ("outer", "inner", "core", "frame")
REST = ("outer", "inner")
TEAM = ("core", "frame")


def dot(left, right):
    return jnp.dot(left, right, preferred_element_type=WIDE)


def dot_tn(left, right):
    return lax.dot_general(left, right, (((0,), (0,)), ((), ())), preferred_element_type=WIDE)


def dot_nt(left, right):
    return lax.dot_general(left, right, (((1,), (1,)), ((), ())), preferred_element_type=WIDE)


def normed(values):
    center = values - jnp.mean(values, axis=-1, keepdims=True)
    rate = lax.rsqrt(jnp.mean(center * center, axis=-1, keepdims=True) + EPSILON)
    return center * rate, rate


def normed_back(grad, unit, rate, gain):
    inner = grad * gain
    mean_one = jnp.mean(inner, axis=-1, keepdims=True)
    mean_two = jnp.mean(inner * unit, axis=-1, keepdims=True)
    return rate * (inner - mean_one - unit * mean_two)


def swap(values, axis):
    return lax.ppermute(values, axis, [(0, 1), (1, 0)])


def team_gather(values):
    if lax.axis_size("frame") == 2:
        pair = jnp.concatenate([values, swap(values, "frame")], axis=0)
    else:
        pair = lax.all_gather(values, "frame", axis=0, tiled=True)
    return jnp.concatenate([pair, swap(pair, "core")], axis=0)


def team_sum(parts):
    half = parts.shape[0] // 2
    pair = parts[:half] + swap(parts[half:].astype(LOW), "core").astype(WIDE)
    if lax.axis_size("frame") == 2:
        rows = half // 2
        return pair[:rows] + swap(pair[rows:].astype(LOW), "frame").astype(WIDE)
    return lax.psum_scatter(pair.astype(LOW), "frame", scatter_dimension=0, tiled=True).astype(WIDE)


def head_split(flat, heads):
    return flat.reshape(flat.shape[0], heads, flat.shape[1] // heads)


def attend_scores(queries, keys, ids, use_frame):
    scale = queries.shape[-1] ** (-0.5)
    scores = jnp.einsum("gqhd,gkhd->ghqk", queries, keys, preferred_element_type=WIDE) * scale
    if use_frame:
        return scores
    allowed = ids[:, :, None] == ids[:, None, :]
    return jnp.where(allowed[:, None], scores, -jnp.inf)


def in_groups(flat, group):
    return flat.reshape((flat.shape[0] // group, group) + flat.shape[1:])


def attend(queries, keys, values, ids, use_frame, group):
    queries, keys, values, ids = (in_groups(m, group) for m in (queries, keys, values, ids))
    scores = attend_scores(queries, keys, ids, use_frame)
    top = jnp.max(scores, axis=-1, keepdims=True)
    log_sum = top + jnp.log(jnp.sum(jnp.exp(scores - top), axis=-1, keepdims=True))
    probs = jnp.exp(scores - log_sum).astype(LOW)
    out = jnp.einsum("ghqk,gkhd->gqhd", probs, values, preferred_element_type=WIDE)
    return out.reshape(-1, out.shape[2] * out.shape[3]), log_sum


def attend_back(queries, keys, values, ids, use_frame, group, log_sum, grad_out):
    queries, keys, values, ids, grad_out = (
        in_groups(m, group) for m in (queries, keys, values, ids, grad_out)
    )
    scale = queries.shape[-1] ** (-0.5)
    scores = attend_scores(queries, keys, ids, use_frame)
    probs = jnp.exp(scores - log_sum)
    grad_probs = jnp.einsum("gqhd,gkhd->ghqk", grad_out, values, preferred_element_type=WIDE)
    delta = jnp.sum(probs * grad_probs, axis=-1, keepdims=True)
    grad_scores = (probs * (grad_probs - delta)).astype(LOW)
    grad_q = jnp.einsum("ghqk,gkhd->gqhd", grad_scores, keys, preferred_element_type=WIDE) * scale
    grad_k = jnp.einsum("ghqk,gqhd->gkhd", grad_scores, queries, preferred_element_type=WIDE) * scale
    grad_v = jnp.einsum(
        "ghqk,gqhd->gkhd", probs.astype(LOW), grad_out, preferred_element_type=WIDE
    )
    return tuple(m.reshape((-1,) + m.shape[2:]) for m in (grad_q, grad_k, grad_v))


def exact_gelu(values):
    return jax.nn.gelu(values, approximate=False)


def exchange_columns(values, count):
    rows, team, width = values.shape
    cores = 2
    frames = team // cores
    parts = values.reshape(rows, cores, frames, width).transpose(1, 2, 0, 3)
    here_x = lax.axis_index("frame")
    here_c = lax.axis_index("core")
    if frames == 2:
        keep = lax.dynamic_index_in_dim(parts, here_x, 1, keepdims=False)
        send = lax.dynamic_index_in_dim(parts, 1 - here_x, 1, keepdims=False)
        came = swap(send, "frame")
        both = jnp.stack([jnp.where(here_x == 0, keep, came), jnp.where(here_x == 0, came, keep)], axis=1)
    else:
        both = lax.all_to_all(parts, "frame", 1, 1, tiled=True)
    keep = lax.dynamic_index_in_dim(both, here_c, 0, keepdims=False)
    send = lax.dynamic_index_in_dim(both, 1 - here_c, 0, keepdims=False)
    came = swap(send, "core")
    out = jnp.stack([jnp.where(here_c == 0, keep, came), jnp.where(here_c == 0, came, keep)], axis=0)
    return out.reshape(team, rows, width)


def spread(count, team):
    rest = count // team
    return [(i, (i % rest) * team + i // rest) for i in range(count)]


def widen(rows, width):
    height, columns = rows.shape
    parts = columns // width
    if parts == 1:
        return rows
    return rows.reshape(height, parts, width).transpose(1, 0, 2).reshape(parts * height, width)


def narrow(stacked, height):
    lead = stacked.shape[:-2]
    parts = stacked.shape[-2] // height
    if parts == 1:
        return stacked
    width = stacked.shape[-1]
    shaped = stacked.reshape(lead + (parts, height, width))
    return jnp.moveaxis(shaped, -3, -2).reshape(lead + (height, parts * width))


def rest_gather(values):
    return lax.all_gather(values, REST, axis=0, tiled=False)


def rest_sum(values):
    return lax.psum_scatter(values, REST, scatter_dimension=0, tiled=False)


def on_device(
    tokens,
    cotangent,
    scene_ids,
    frame_index,
    qkv_weight,
    qkv_bias,
    proj_weight,
    fc1_weight,
    fc1_bias,
    fc2_weight,
    out_bias,
    norm_gain,
    norm_bias,
    layer_scale,
    qk_gain,
    qk_bias,
):
    frames = lax.axis_size("frame")
    team = 2 * frames
    rest = lax.axis_size("outer") * lax.axis_size("inner")
    count = team * rest
    rows, width = tokens.shape
    head_size = qk_gain.shape[-1]
    heads = width // head_size // team
    part = heads * head_size
    hidden_all = fc1_weight.shape[-1]
    hidden = hidden_all // team
    mine = lax.axis_index("core") * frames + lax.axis_index("frame")
    shard_rows = qkv_weight.shape[1]
    fc2_rows = fc2_weight.shape[1]

    small = jnp.concatenate(
        [m.reshape(-1) for m in (qkv_bias, fc1_bias, out_bias, norm_gain, norm_bias, layer_scale)]
    )
    small = lax.all_gather(small, EVERY, axis=0, tiled=False)
    sizes = [m.size for m in (qkv_bias, fc1_bias, out_bias, norm_gain, norm_bias, layer_scale)]
    cuts = np.cumsum([0] + sizes)
    small = [small[:, cuts[i] : cuts[i + 1]].astype(WIDE) for i in range(6)]
    bias_qkv = small[0].reshape(count, 2, -1).transpose(1, 0, 2).reshape(2, 3, team, part)
    bias_qkv = lax.dynamic_index_in_dim(bias_qkv, mine, 2, keepdims=False).reshape(2, 3 * part)
    bias_up = small[1].reshape(rest, team, 2, -1)
    bias_up = lax.dynamic_index_in_dim(bias_up, mine, 1, keepdims=False)
    bias_up = bias_up.transpose(1, 0, 2).reshape(2, hidden)
    out_shift, gains, shifts, scales = (
        m.reshape(count, 2, 2, -1).transpose(1, 2, 0, 3).reshape(2, 2, width) for m in small[2:]
    )

    proj_here = lax.ppermute(proj_weight, EVERY, spread(count, team))
    packs = []
    for depth in range(2):
        qkv_part = exchange_columns(
            qkv_weight[depth].reshape(shard_rows, 3, team, part).transpose(0, 2, 1, 3).reshape(shard_rows, team, 3 * part),
            count,
        ).reshape(team * shard_rows, 3 * part)
        up_part = exchange_columns(
            fc1_weight[depth]
            .reshape(shard_rows, rest, team, hidden // rest)
            .transpose(0, 2, 1, 3)
            .reshape(shard_rows, team, hidden),
            count,
        ).reshape(team * shard_rows, hidden)
        attn_part = jnp.concatenate([qkv_part, widen(proj_here[depth], part)], axis=1)
        down_part = widen(fc2_weight[depth], hidden)
        packs.append(jnp.concatenate([attn_part, up_part, down_part], axis=0))

    unit = team * shard_rows

    def unpack(pack):
        attn, up, down = pack[:, :unit], pack[:, unit : 2 * unit], pack[:, 2 * unit :]
        weight_qkv = attn[..., : 3 * part].reshape(width, 3 * part)
        weight_proj = narrow(attn[..., 3 * part :], shard_rows).reshape(part, width)
        return (
            weight_qkv,
            weight_proj,
            up.reshape(width, hidden),
            narrow(down, fc2_rows).reshape(hidden, width),
        )

    weights = [unpack(rest_gather(packs[depth])) for depth in range(2)]

    ids = scene_ids.reshape(1, rows)
    if frames == 2:
        ids = jnp.concatenate([ids, swap(ids, "frame")], axis=0)
    else:
        ids = lax.all_gather(ids, "frame", axis=0, tiled=True)
    ids = jnp.concatenate([ids, swap(ids, "core")], axis=0).reshape(team * rows)

    stream = tokens.astype(WIDE)
    saved = []
    for depth in range(2):
        weight_qkv, weight_proj, weight_up, weight_down = weights[depth]
        use_frame = depth == 0
        group = FRAME_TOK if use_frame else frames * rows
        unit_one, rate_one = normed(stream)
        first = (unit_one * gains[depth, 0] + shifts[depth, 0]).astype(LOW)
        first = team_gather(first)
        mixed = dot(first, weight_qkv) + bias_qkv[depth]
        gain_head, shift_head = qk_gain[depth].astype(WIDE), qk_bias[depth].astype(WIDE)
        unit_q, rate_q = normed(head_split(mixed[:, :part], heads))
        unit_k, rate_k = normed(head_split(mixed[:, part : 2 * part], heads))
        queries = (unit_q * gain_head[0] + shift_head[0]).astype(LOW)
        keys = (unit_k * gain_head[1] + shift_head[1]).astype(LOW)
        values = head_split(mixed[:, 2 * part :], heads).astype(LOW)
        attended, log_sum = attend(queries, keys, values, ids, use_frame, group)
        attended = attended.astype(LOW)
        branch_one = team_sum(dot(attended, weight_proj)) + out_shift[depth, 0]
        middle = stream + scales[depth, 0] * branch_one
        unit_two, rate_two = normed(middle)
        second = team_gather((unit_two * gains[depth, 1] + shifts[depth, 1]).astype(LOW))
        pre_act = dot(second, weight_up) + bias_up[depth]
        act = exact_gelu(pre_act).astype(LOW)
        branch_two = team_sum(dot(act, weight_down)) + out_shift[depth, 1]
        stream = middle + scales[depth, 1] * branch_two
        saved.append(
            (
                unit_one, rate_one, first, unit_q, rate_q, unit_k, rate_k, queries, keys, values,
                log_sum, attended, branch_one, unit_two, rate_two, second, pre_act, act, branch_two,
            )
        )

    grad = cotangent.astype(WIDE)
    sums = [None, None]
    pieces = [None, None]
    head_sums = [None, None]
    for depth in (1, 0):
        weight_qkv, weight_proj, weight_up, weight_down = weights[depth]
        use_frame = depth == 0
        group = FRAME_TOK if use_frame else frames * rows
        (
            unit_one, rate_one, first, unit_q, rate_q, unit_k, rate_k, queries, keys, values,
            log_sum, attended, branch_one, unit_two, rate_two, second, pre_act, act, branch_two,
        ) = saved[depth]
        scale_two = jnp.sum(grad * branch_two, axis=0)
        grad_branch = grad * scales[depth, 1]
        shift_two = jnp.sum(grad_branch, axis=0)
        branch_low = team_gather(grad_branch.astype(LOW))
        grad_down = dot_tn(act, branch_low).astype(LOW)
        grad_act = dot_nt(branch_low, weight_down)
        _, gelu_back = jax.vjp(exact_gelu, pre_act)
        grad_pre = gelu_back(grad_act)[0]
        sum_up = jnp.sum(grad_pre, axis=0)
        pre_low = grad_pre.astype(LOW)
        grad_up = dot_tn(second, pre_low).astype(LOW)
        grad_second = team_sum(dot_nt(pre_low, weight_up))
        gain_two = jnp.sum(grad_second * unit_two, axis=0)
        norm_shift_two = jnp.sum(grad_second, axis=0)
        grad_middle = grad + normed_back(grad_second, unit_two, rate_two, gains[depth, 1])
        scale_one = jnp.sum(grad_middle * branch_one, axis=0)
        grad_att = grad_middle * scales[depth, 0]
        shift_one = jnp.sum(grad_att, axis=0)
        att_low = team_gather(grad_att.astype(LOW))
        grad_proj = dot_tn(attended, att_low).astype(LOW)
        grad_flat = dot_nt(att_low, weight_proj).astype(LOW)
        grad_q, grad_k, grad_v = attend_back(
            queries, keys, values, ids, use_frame, group, log_sum, head_split(grad_flat, heads)
        )
        gain_head = qk_gain[depth].astype(WIDE)
        head_gain = jnp.stack(
            [jnp.sum(grad_q * unit_q, axis=(0, 1)), jnp.sum(grad_k * unit_k, axis=(0, 1))]
        )
        head_shift = jnp.stack([jnp.sum(grad_q, axis=(0, 1)), jnp.sum(grad_k, axis=(0, 1))])
        mixed_q = normed_back(grad_q, unit_q, rate_q, gain_head[0])
        mixed_k = normed_back(grad_k, unit_k, rate_k, gain_head[1])
        grad_mixed = jnp.concatenate(
            [m.reshape(team * rows, part) for m in (mixed_q, mixed_k, grad_v)], axis=1
        )
        sum_qkv = jnp.sum(grad_mixed, axis=0)
        mixed_low = grad_mixed.astype(LOW)
        grad_qkv = dot_tn(first, mixed_low).astype(LOW)
        grad_first = team_sum(dot_nt(mixed_low, weight_qkv))
        gain_one = jnp.sum(grad_first * unit_one, axis=0)
        norm_shift_one = jnp.sum(grad_first, axis=0)
        grad = grad_middle + normed_back(grad_first, unit_one, rate_one, gains[depth, 0])

        proj_wide = grad_proj.reshape(rest, shard_rows, team, part).transpose(0, 2, 1, 3)
        attn_pack = jnp.concatenate(
            [grad_qkv.reshape(rest, unit, 3 * part), proj_wide.reshape(rest, unit, part)], axis=2
        )
        down_wide = grad_down.reshape(rest, fc2_rows, width // hidden, hidden).transpose(0, 2, 1, 3)
        pack = jnp.concatenate(
            [attn_pack, grad_up.reshape(rest, unit, hidden), down_wide.reshape(rest, -1, hidden)], axis=1
        )
        pack = rest_sum(pack)
        attn, up, down = pack[:unit], pack[unit : 2 * unit], pack[2 * unit :]
        proj_mine = narrow(attn[:, 3 * part :], shard_rows)
        down_mine = narrow(down, fc2_rows)
        qkv_mine = exchange_columns(
            attn[:, : 3 * part].reshape(team, shard_rows, 3 * part).transpose(1, 0, 2), count
        )
        qkv_mine = (
            qkv_mine.reshape(team, shard_rows, 3, part).transpose(1, 2, 0, 3).reshape(shard_rows, -1)
        )
        up_mine = exchange_columns(up.reshape(team, shard_rows, hidden).transpose(1, 0, 2), count)
        up_mine = (
            up_mine.reshape(team, shard_rows, rest, hidden // rest)
            .transpose(1, 2, 0, 3)
            .reshape(shard_rows, -1)
        )
        pieces[depth] = (qkv_mine, proj_mine, up_mine, down_mine)
        full_qkv = jnp.zeros((3, team, part), WIDE)
        full_qkv = lax.dynamic_update_slice(full_qkv, sum_qkv.reshape(3, 1, part), (0, mine, 0))
        full_up = jnp.zeros((rest, team, hidden // rest), WIDE)
        full_up = lax.dynamic_update_slice(full_up, sum_up.reshape(rest, 1, hidden // rest), (0, mine, 0))
        vectors = jnp.stack(
            [shift_one, shift_two, gain_one, gain_two, norm_shift_one, norm_shift_two, scale_one, scale_two]
        )
        sums[depth] = jnp.concatenate(
            [
                full_qkv.reshape(count, -1),
                full_up.reshape(count, -1),
                vectors.reshape(8, count, -1).transpose(1, 0, 2).reshape(count, -1),
            ],
            axis=1,
        )
        head_sums[depth] = jnp.stack([head_gain, head_shift])

    summed = lax.psum_scatter(jnp.concatenate(sums, axis=1), EVERY, scatter_dimension=0, tiled=False)
    summed = summed.reshape(2, -1)
    n_qkv, n_up = qkv_bias.shape[1], fc1_bias.shape[1]
    grad_bias_qkv = summed[:, :n_qkv]
    grad_bias_up = summed[:, n_qkv : n_qkv + n_up]
    vectors = summed[:, n_qkv + n_up :].reshape(2, 4, 2, -1)
    head_all = lax.psum(jnp.stack(head_sums), EVERY)
    proj_grad = lax.ppermute(
        jnp.stack([pieces[0][1], pieces[1][1]]), EVERY, [(b, a) for a, b in spread(count, team)]
    )

    def both(member):
        return jnp.stack([pieces[0][member], pieces[1][member]]).astype(WIDE)

    return (
        stream.astype(LOW),
        grad.astype(LOW),
        both(0),
        grad_bias_qkv,
        proj_grad.astype(WIDE),
        both(2),
        grad_bias_up,
        both(3),
        vectors[:, 0],
        vectors[:, 1],
        vectors[:, 2],
        vectors[:, 3],
        head_all[:, 0],
        head_all[:, 1],
    )


def solution(mesh):
    scenes, frames = mesh.shape["scene"], mesh.shape["frame"]
    rest = scenes // 2
    outer = 4 if rest % 4 == 0 else rest
    grid = Mesh(mesh.devices.reshape(outer, rest // outer, 2, frames), EVERY)
    by_rows = P(EVERY, None)
    second = P(None, EVERY)
    second_rows = P(None, EVERY, None)
    last = P(None, None, EVERY)
    return jax.shard_map(
        on_device,
        mesh=grid,
        in_specs=(
            by_rows, by_rows, P(EVERY), P(EVERY), second_rows, second, second_rows, second_rows,
            second, second_rows, last, last, last, last, P(), P(),
        ),
        out_specs=(
            by_rows, by_rows, second_rows, second, second_rows, second_rows, second, second_rows,
            last, last, last, last, P(), P(),
        ),
        check_vma=False,
    )
```

time: 3300 us -> 865 us (0.26)
  waiting for transfers between devices: 2210 us -> 450 us
  blocking collectives: 769 us -> 84.1 us
  matrix products: 155 us -> 78.5 us
  starting transfers between devices: 1.2 us -> 59.3 us
    reduce_scatter x8 -> x2, waiting for transfers between devices: 2040 us -> 228 us  [rest_sum(): return lax.psum_scatter(values, REST, scatter_dimension=0, tiled=False)]
    all_gather x13 -> x0, blocking collectives: 679 us -> none  [the longest x2 140 us: on_device(): lax.all_gather(layer_scale[depth], ('scene', 'frame'), axis=1, tiled=True)]
    unnamed x24 -> x6, waiting for transfers between devices: 166 us -> 53.5 us
    ppermute x0 -> x52, waiting for transfers between devices: none -> 109 us  [the longest x50 106 us: swap(): return lax.ppermute(values, axis, [(0, 1), (1, 0)])]
    dot_general x36, matrix products: 155 us -> 78.5 us  [the longest x8 25 us: dot_tn(): lax.dot_general(left, right, (((0,), (0,)), ((), ())), preferred_element_...]
    all_gather x8 -> x2, waiting for transfers between devices: 0.09 us -> 59.3 us  [rest_gather(): return lax.all_gather(values, REST, axis=0, tiled=False)]
    ppermute x0 -> x52, starting transfers between devices: none -> 58.8 us  [the longest x50 47.7 us: swap(): return lax.ppermute(values, axis, [(0, 1), (1, 0)])]
    unnamed x2 -> x1, blocking collectives: 90.4 us -> 44.4 us
  transfers between devices with their start and end apart: 20 -> 57, of which waited for: 12 -> 33; matrix products, arithmetic and copies ran while one was open for 6% -> 15% of each run, Pallas kernels for 0% -> 0%
where the time goes in v1:
time: 865 us; the launch traced here: 859 us
  waiting for transfers between devices  450 us (52%)
  local copies, waits for them, and re-layouts  119 us (14%)
  blocking collectives  84.1 us (10%)
  matrix products  78.5 us (9%)
  starting transfers between devices  59.3 us (7%)
  other arithmetic  50 us (6%)
  between operations  17.7 us (2%)
    reduce_scatter x2, waiting for transfers between devices, rest_sum(): return lax.psum_scatter(values, REST, scatter_dimension=0, tiled=False)  228 us
    ppermute x50, waiting for transfers between devices, swap(): return lax.ppermute(values, axis, [(0, 1), (1, 0)])  106 us
    all_gather x2, waiting for transfers between devices, rest_gather(): return lax.all_gather(values, REST, axis=0, tiled=False)  59.3 us
    unnamed x6, waiting for transfers between devices  53.5 us
    ppermute x50, starting transfers between devices, swap(): return lax.ppermute(values, axis, [(0, 1), (1, 0)])  47.7 us
    unnamed x1, blocking collectives  44.4 us
    psum x1, blocking collectives, on_device(): head_all = lax.psum(jnp.stack(head_sums), EVERY)  39.7 us
    dot_general x8, matrix products, dot_tn(): lax.dot_general(left, right, (((0,), (0,)), ((), ())), preferred_element_...  25 us
  transfers between devices with their start and end apart: 57, of which 33 were waited for; matrix products, arithmetic and copies ran while one was open for 15% of the time, Pallas kernels for 0%

profile of v1, /device:TPU:7, one launch (start us, length us, event | category | flops | bytes accessed | tf_op | source)
XLA Modules:
  0.0 858.6 jit_solution(1720039734660104169)
XLA Ops:
  10.9 6.3 collective-permute-start.4
  18.0 2.9 collective-permute-done.4
  23.0 44.4 %all-reduce = bf16[30720]{0:T(1024)(128)(2,1)S(1)} all-reduce(bf16[30720]{0:T(1024)(128)(2,1)S(1)} %dynamic-update-slice), channel_id=2, replica_groups=mesh['outer'=4,'inner'=2,'core'=2,'frame'=2] {'outer','inner','core','fr..., use_global_device_ids=true, to_apply=%add | all-reduce | flops 30720 | bytes 122880
  78.5 4.5 collective-permute-start.16
  86.7 37.8 %all-gather.6.cloned.1.call-done = bf16[3072,1024]{1,0:T(8,128)(2,1)} async-done(((bf16[384,1024]{1,0:T(8,128)(2,1)}), bf16[3072,1024]{1,0:T(8,128)(2,1)}) %all-gather.6.cloned.1.call-update) | async-done | bytes 6291472 | tf_op jit(solution)/shard_map/all_gather | solution.py:157
  136.2 3.0 fusion.173
  151.0 6.8 collective-permute-done.8
  160.2 6.7 collective-permute-done.9
  168.5 3.2 fusion.160
  171.8 8.5 multiply_convert_fusion.2
  184.4 7.5 collective-permute-done.12
  194.0 5.6 collective-permute-done.19
  203.0 21.6 %all-gather.8.cloned.1.call-done = bf16[3072,1024]{1,0:T(8,128)(2,1)} async-done(((bf16[384,1024]{1,0:T(8,128)(2,1)}), bf16[3072,1024]{1,0:T(8,128)(2,1)}) %all-gather.8.cloned.1.call-update) | async-done | bytes 6291472 | tf_op jit(solution)/shard_map/all_gather | solution.py:157
  249.8 7.2 collective-permute-done.22
  259.4 5.0 collective-permute-done.23
  264.4 3.9 collective-permute-start.24
  272.9 5.7 multiply_convert_fusion.1
  286.1 6.0 collective-permute-done.30
  292.9 4.8 collective-permute-done.26
  300.7 6.6 collective-permute-done.31
  322.4 2.5 convolution_convert_fusion.10
  336.8 2.8 reshape.846
  352.2 3.3 subtract_multiply_fusion.3
  359.2 7.5 collective-permute-done.34
  368.4 6.6 collective-permute-done.35
  378.5 2.5 fusion.175
  385.1 7.2 collective-permute-done.38
  394.6 6.3 collective-permute-done.39
  409.7 4.3 convolution_convert_fusion.1
  422.0 2.4 multiply_reduce_fusion.1
  424.4 2.6 multiply_reduce_fusion.2
  430.2 2.6 reshape.781
  440.7 3.6 subtract_multiply_fusion.1
  446.6 2.6 convolution_convert_fusion
  449.8 2.4 convolution_convert_fusion.6
  456.4 3.8 convolution_convert_fusion.4
  469.5 5.8 pad_maximum_fusion.1
  476.3 4.2 convolution_convert_fusion.3
  480.6 2.6 convolution_convert_fusion.2
  487.0 2.7 convolution_convert_fusion.5
  489.9 3.3 pad_maximum_fusion
  494.0 39.7 %psum.7 = f32[2,2,2,64]{3,2,1,0:T(2,128)S(1)} all-reduce(f32[2,2,2,64]{3,2,1,0:T(2,128)S(1)} %pad_maximum_fusion.51), channel_id=1, replica_groups=mesh['outer'=4,'inner'=2,'core'=2,'frame'=2] {'outer','inner','core','fr..., use_global_device_ids=true, to_apply=%region_69.70 | all-reduce | flops 512 | bytes 4096 | tf_op jit(solution)/shard_map/psum | solution.py:387
  536.2 53.5 %all-reduce.4.cloned.1.call-done = f32[32,960]{1,0:T(8,128)} async-done(((f32[32,960]{1,0:T(8,128)}), f32[32,960]{1,0:T(8,128)}) %all-reduce.4.cloned.1.call-update) | async-done | bytes 122896
  592.5 118.5 %reduce-scatter.5.cloned.1.call-done = bf16[1,384,1024]{2,1,0:T(8,128)(2,1)} async-done(((bf16[8,384,1024]{2,1,0:T(8,128)(2,1)}), bf16[1,384,1024]{2,1,0:T(8,128)(2,1)}) %reduce-scatter.5.cloned.1.call-update) | async-done | bytes 786448 | tf_op jit(solution)/shard_map/reduce_scatter | solution.py:161
  715.8 3.2 collective-permute-start.46
  721.9 109.6 %reduce-scatter.3.cloned.1.call-done = bf16[1,384,1024]{2,1,0:T(8,128)(2,1)} async-done(((bf16[8,384,1024]{2,1,0:T(8,128)(2,1)}), bf16[1,384,1024]{2,1,0:T(8,128)(2,1)}) %reduce-scatter.3.cloned.1.call-update) | async-done | bytes 786448 | tf_op jit(solution)/shard_map/reduce_scatter | solution.py:161
  833.2 4.8 collective-permute-start.47
  840.4 5.4 collective-permute-done.43
  (900 shorter events, 226.8 us)
Async XLA Ops:
  7.2 117.3 %all-gather.6.cloned.1.call-start = ((), (), s32[]{:S(2)}) async-start(), calls=%async_computation.4 | async-start | bytes 7077888 | tf_op jit(solution)/shard_map/all_gather | solution.py:157
  8.9 8.4 collective-permute-start.2
  9.6 7.8 collective-permute-start.5
  10.9 10.0 %collective-permute-start.4 = (bf16[2,32,1024]{2,1,0:T(8,128)(2,1)S(1)}, bf16[2,32,1024]{2,1,0:T(8,128)(2,1)S(1)}, u32[]{:S(2)}, u32[]{:S(2)}) collective-permute-start(bf16[2,32,1024]{2,1,0:T(8,128)(2,1)S(1)} %copy-done.179), channel_id=1, source_target_pairs={{0,0},{1,4},{2,8},{3,12},{4,16},{5,20},{6,24},{7,28},{8,1},{9,5},{... | collective-permute-start | bytes 393224 | tf_op jit(solution)/shard_map/ppermute | solution.py:212
  17.3 3.6 collective-permute-start.3
  17.5 3.6 collective-permute-start.6
  22.2 202.4 %all-gather.8.cloned.1.call-start = ((), (), s32[]{:S(2)}) async-start(), calls=%async_computation.5 | async-start | bytes 7077888 | tf_op jit(solution)/shard_map/all_gather | solution.py:157
  70.5 13.9 %collective-permute-start = (bf16[128,1024]{1,0:T(8,128)(2,1)S(1)}, bf16[128,1024]{1,0:T(8,128)(2,1)S(1)}, u32[]{:S(2)}, u32[]{:S(2)}) collective-permute-start(bf16[128,1024]{1,0:T(8,128)(2,1)S(1)} %fusion.33), channel_id=1, source_target_pairs={{0,1},{1,0},{2,3},{3,2},{4,5},{5,4},{6,7},{7,6},{8,9},{9,8},{10,11... | collective-permute-start | bytes 786440 | tf_op jit(solution)/shard_map/ppermute | solution.py:43
  72.5 5.9 collective-permute-start.15
  73.0 9.9 %collective-permute-start.17 = (bf16[2,32,1024]{2,1,0:T(8,128)(2,1)S(1)}, bf16[2,32,1024]{2,1,0:T(8,128)(2,1)S(1)}, u32[]{:S(2)}, u32[]{:S(2)}) collective-permute-start(bf16[2,32,1024]{2,1,0:T(8,128)(2,1)S(1)} %dynamic-slice_bitcast_fusion.2), channel_id=1, source_target_pairs={{0,1},{1,0},{2,3},{3,2},{4,5},{5,4},{6,7},{7,6},{8,9},{9,8},{10,11... | collective-permute-start | bytes 393224 | tf_op jit(solution)/shard_map/ppermute | solution.py:43
  78.5 5.9 collective-permute-start.16
  84.5 41.5 %collective-permute-start.1 = (bf16[256,1024]{1,0:T(8,128)(2,1)S(1)}, bf16[256,1024]{1,0:T(8,128)(2,1)S(1)}, u32[]{:S(2)}, u32[]{:S(2)}) collective-permute-start(bf16[256,1024]{1,0:T(8,128)(2,1)S(1)} %pad_maximum_fusion.14), channel_id=1, source_target_pairs={{0,2},{2,0},{1,3},{3,1},{4,6},{6,4},{5,7},{7,5},{8,10},{10,8},{9,1... | collective-permute-start | bytes 1572872 | tf_op jit(solution)/shard_map/ppermute | solution.py:43
  86.4 503.3 %all-reduce.4.cloned.1.call-start = ((), (), s32[]{:S(2)}) async-start(), calls=%async_computation.6 | async-start | bytes 262144
  143.9 3.6 collective-permute-start.7
  149.7 8.1 collective-permute-start.8
  159.6 7.2 collective-permute-start.9
  166.9 4.9 collective-permute-start.10
  183.9 7.9 collective-permute-start.12
  192.5 8.9 %collective-permute-start.13 = (bf16[128,1024]{1,0:T(8,128)(2,1)S(1)}, bf16[128,1024]{1,0:T(8,128)(2,1)S(1)}, u32[]{:S(2)}, u32[]{:S(2)}) collective-permute-start(bf16[128,1024]{1,0:T(8,128)(2,1)S(1)} %add_convert_fusion.6), channel_id=1, source_target_pairs={{0,1},{1,0},{2,3},{3,2},{4,5},{5,4},{6,7},{7,6},{8,9},{9,8},{10,11... | collective-permute-start | bytes 786440 | tf_op jit(solution)/shard_map/ppermute | solution.py:43
  193.0 6.7 collective-permute-start.19
  201.4 27.5 %collective-permute-start.14 = (bf16[256,1024]{1,0:T(8,128)(2,1)S(1)}, bf16[256,1024]{1,0:T(8,128)(2,1)}, u32[]{:S(2)}, u32[]{:S(2)}) collective-permute-start(bf16[256,1024]{1,0:T(8,128)(2,1)S(1)} %pad_maximum_fusion.16), channel_id=1, source_target_pairs={{0,2},{2,0},{1,3},{3,1},{4,6},{6,4},{5,7},{7,5},{8,10},{10,8},{9,1... | collective-permute-start | bytes 1572872 | tf_op jit(solution)/shard_map/ppermute | solution.py:43
  246.5 2.8 collective-permute-start.21
  249.5 7.6 collective-permute-start.22
  257.7 6.7 collective-permute-start.23
  258.1 11.9 %collective-permute-start.27 = (bf16[128,1024]{1,0:T(8,128)(2,1)S(1)}, bf16[128,1024]{1,0:T(8,128)(2,1)S(1)}, u32[]{:S(2)}, u32[]{:S(2)}) collective-permute-start(bf16[128,1024]{1,0:T(8,128)(2,1)S(1)} %fusion.31), channel_id=1, source_target_pairs={{0,1},{1,0},{2,3},{3,2},{4,5},{5,4},{6,7},{7,6},{8,9},{9,8},{10,11... | collective-permute-start | bytes 786440 | tf_op jit(solution)/shard_map/ppermute | solution.py:43
  264.4 8.4 collective-permute-start.24
  270.0 8.6 collective-permute-start.28
  284.2 7.8 collective-permute-start.30
  285.7 11.9 %collective-permute-start.26 = (bf16[128,1024]{1,0:T(8,128)(2,1)S(1)}, bf16[128,1024]{1,0:T(8,128)(2,1)S(1)}, u32[]{:S(2)}, u32[]{:S(2)}) collective-permute-start(bf16[128,1024]{1,0:T(8,128)(2,1)S(1)} %slice.747), channel_id=1, source_target_pairs={{0,1},{1,0},{2,3},{3,2},{4,5},{5,4},{6,7},{7,6},{8,9},{9,8},{10,11... | collective-permute-start | bytes 786440 | tf_op jit(solution)/shard_map/ppermute | solution.py:43
  300.4 6.9 collective-permute-start.31
  308.2 14.2 %collective-permute-start.32 = (bf16[256,1024]{1,0:T(8,128)(2,1)}, bf16[256,1024]{1,0:T(8,128)(2,1)}, u32[]{:S(2)}, u32[]{:S(2)}) collective-permute-start(bf16[256,1024]{1,0:T(8,128)(2,1)} %pad_maximum_fusion.19), channel_id=1, source_target_pairs={{0,2},{2,0},{1,3},{3,1},{4,6},{6,4},{5,7},{7,5},{8,10},{10,8},{9,1... | collective-permute-start | bytes 1572872 | tf_op jit(solution)/shard_map/ppermute | solution.py:43
  358.9 7.8 collective-permute-start.34
  368.1 6.9 collective-permute-start.35
  375.0 3.5 collective-permute-start.36
  384.7 7.6 collective-permute-start.38
  394.3 6.7 collective-permute-start.39
  401.8 12.2 %collective-permute-start.40 = (bf16[256,1024]{1,0:T(8,128)(2,1)}, bf16[256,1024]{1,0:T(8,128)(2,1)}, u32[]{:S(2)}, u32[]{:S(2)}) collective-permute-start(bf16[256,1024]{1,0:T(8,128)(2,1)} %pad_maximum_fusion.21), channel_id=1, source_target_pairs={{0,2},{2,0},{1,3},{3,1},{4,6},{6,4},{5,7},{7,5},{8,10},{10,8},{9,1... | collective-permute-start | bytes 1572872 | tf_op jit(solution)/shard_map/ppermute | solution.py:43
  446.5 5.8 collective-permute-start.41
  454.3 12.6 %collective-permute-start.42 = (bf16[128,1024]{1,0:T(8,128)(2,1)}, bf16[128,1024]{1,0:T(8,128)(2,1)}, u32[]{:S(2)}, u32[]{:S(2)}) collective-permute-start(bf16[128,1024]{1,0:T(8,128)(2,1)} %slice.743), channel_id=1, source_target_pairs={{0,1},{1,0},{2,3},{3,2},{4,5},{5,4},{6,7},{7,6},{8,9},{9,8},{10,11... | collective-permute-start | bytes 786440 | tf_op jit(solution)/shard_map/ppermute | solution.py:43
  469.5 241.5 %reduce-scatter.5.cloned.1.call-start = ((), (), s32[]{:S(2)}) async-start(), calls=%async_computation.3 | async-start | bytes 7077888 | tf_op jit(solution)/shard_map/reduce_scatter | solution.py:161
  475.3 356.2 %reduce-scatter.3.cloned.1.call-start = ((), (), s32[]{:S(2)}) async-start(), calls=%async_computation.2 | async-start | bytes 7077888 | tf_op jit(solution)/shard_map/reduce_scatter | solution.py:161
  712.2 3.5 collective-permute-start.45
  712.5 6.5 collective-permute-start.50
  715.8 4.6 collective-permute-start.46
  832.8 15.1 %collective-permute-start.48 = (bf16[2,32,1024]{2,1,0:T(8,128)(2,1)S(1)}, bf16[2,32,1024]{2,1,0:T(8,128)(2,1)S(1)}, u32[]{:S(2)}, u32[]{:S(2)}) collective-permute-start(bf16[2,32,1024]{2,1,0:T(8,128)(2,1)S(1)} %dynamic-slice_bitcast_fusion.1), channel_id=1, source_target_pairs={{0,1},{1,0},{2,3},{3,2},{4,5},{5,4},{6,7},{7,6},{8,9},{9,8},{10,11... | collective-permute-start | bytes 393224 | tf_op jit(solution)/shard_map/ppermute | solution.py:43
  833.2 14.8 %collective-permute-start.47 = (bf16[2,32,1024]{2,1,0:T(8,128)(2,1)S(1)}, bf16[2,32,1024]{2,1,0:T(8,128)(2,1)S(1)}, u32[]{:S(2)}, u32[]{:S(2)}) collective-permute-start(bf16[2,32,1024]{2,1,0:T(8,128)(2,1)S(1)} %pad_maximum_fusion.50), channel_id=1, source_target_pairs={{0,0},{4,1},{8,2},{12,3},{16,4},{20,5},{24,6},{28,7},{1,8},{5,9},{... | collective-permute-start | bytes 393224 | tf_op jit(solution)/shard_map/ppermute | solution.py:388
  838.1 7.7 collective-permute-start.43
  845.8 3.0 collective-permute-start.44
  (204 other events, 1596.7 us)
Sparse Core Ops, SparseCore 0:
  22.3 102.1 all-gather.5
  127.3 97.2 all-gather.7
  469.6 120.0 all-reduce.3
  593.1 117.8 reduce-scatter.4
  714.4 117.1 reduce-scatter.2

commit v2 on v1

v2 whole, which is shorter than its diff:
```python
import jax
import jax.numpy as jnp
import numpy as np
from jax import lax
from jax.experimental import pallas as pl
from jax.experimental.pallas import tpu as pltpu
from jax.sharding import Mesh
from jax.sharding import PartitionSpec as P

EPSILON = 1e-06
FRAME_TOK = 64
LOW = jnp.bfloat16
WIDE = jnp.float32
EVERY = ("outer", "inner", "core", "frame")
REST = ("outer", "inner")
TEAM = ("core", "frame")
HIGHEST = lax.Precision.HIGHEST
ROOT_HALF = 0.7071067811865476
ROOT_TWO_PI = 0.3989422804014327
VMEM_LIMIT = 56 * 1024 * 1024
OUT, GAIN, SHIFT, SCALE = 0, 4, 8, 12


def dot(left, right):
    return jnp.dot(left, right, preferred_element_type=WIDE)


def dot_tn(left, right):
    return lax.dot_general(left, right, (((0,), (0,)), ((), ())), preferred_element_type=WIDE)


def dot_nt(left, right):
    return lax.dot_general(left, right, (((1,), (1,)), ((), ())), preferred_element_type=WIDE)


def normed(values):
    center = values - jnp.mean(values, axis=-1, keepdims=True)
    rate = lax.rsqrt(jnp.mean(center * center, axis=-1, keepdims=True) + EPSILON)
    return center * rate, rate


def normed_back(grad, unit, rate, gain):
    inner = grad * gain
    mean_one = jnp.mean(inner, axis=-1, keepdims=True)
    mean_two = jnp.mean(inner * unit, axis=-1, keepdims=True)
    return rate * (inner - mean_one - unit * mean_two)


def shape_of(shape, dtype):
    return jax.ShapeDtypeStruct(shape, dtype)


def call(kernel, outs, args, name, flops=0, scratch=(), specs=None, scalars=0):
    vmem = pl.BlockSpec(memory_space=pltpu.VMEM)
    smem = pl.BlockSpec(memory_space=pltpu.SMEM)
    specs = specs or {}
    in_specs = [smem if i < scalars else specs.get(i, vmem) for i in range(len(args))]
    bytes_all = sum(m.size * m.dtype.itemsize for m in args)
    bytes_all += sum(int(np.prod(s.shape)) * s.dtype.itemsize for s in outs)
    return pl.pallas_call(
        kernel,
        out_shape=list(outs),
        in_specs=in_specs,
        out_specs=[vmem] * len(outs),
        scratch_shapes=list(scratch),
        compiler_params=pltpu.CompilerParams(vmem_limit_bytes=VMEM_LIMIT),
        cost_estimate=pl.CostEstimate(flops=flops, bytes_accessed=bytes_all, transcendentals=0),
        name=name,
    )(*args)


def swap(values, axis):
    return lax.ppermute(values, axis, [(0, 1), (1, 0)])


def cross(values):
    return lax.ppermute(values, TEAM, [(0, 3), (1, 2), (2, 1), (3, 0)])


def team_gather(values):
    if lax.axis_size("frame") == 2:
        far = swap(values, "frame")
        near = swap(values, "core")
        return [values, far, near, swap(far, "core")]
    both = lax.all_gather(values, "frame", axis=0, tiled=True)
    return [both, swap(both, "core")]


def team_sum(own, peer):
    if lax.axis_size("frame") == 2:
        far = own[1] + swap(peer[1], "core").astype(WIDE)
        came = swap(far.astype(LOW), "frame")
        return [own[0], swap(peer[0], "core"), came]
    total = own[0] + swap(peer[0], "core").astype(WIDE)
    return [lax.psum_scatter(total.astype(LOW), "frame", scatter_dimension=0, tiled=True).astype(WIDE)]


def exchange_columns(values):
    parts = values.transpose(1, 0, 2)
    frames = lax.axis_size("frame")
    parts = parts.reshape((2, frames) + parts.shape[1:])
    both = lax.all_to_all(parts, "frame", 1, 1, tiled=True)
    here = lax.axis_index("core")
    keep = lax.dynamic_index_in_dim(both, here, 0, keepdims=False)
    came = swap(lax.dynamic_index_in_dim(both, 1 - here, 0, keepdims=False), "core")
    out = jnp.stack([jnp.where(here == 0, keep, came), jnp.where(here == 0, came, keep)], axis=0)
    return out.reshape((2 * frames,) + out.shape[2:])


def split_weights(qkv, up, part, rest, me):
    rows = qkv.shape[0]
    width, hidden_all = qkv.shape[1] // 3, up.shape[1]
    lanes = hidden_all // 4 // rest

    def kernel(me_ref, qkv_ref, up_ref, *outs):
        for away, out in enumerate(outs):
            member = jnp.bitwise_xor(me_ref[0], away)
            for s in range(3):
                start = pl.multiple_of(s * width + member * part, 128)
                out[:, s * part : (s + 1) * part] = qkv_ref[:, pl.ds(start, part)]
            for f in range(rest):
                start = pl.multiple_of((f * 4 + member) * lanes, 128)
                at = 3 * part + f * lanes
                out[:, at : at + lanes] = up_ref[:, pl.ds(start, lanes)]

    out = shape_of((rows, 3 * part + hidden_all // 4), qkv.dtype)
    return call(kernel, [out] * 4, [me, qkv, up], "split_weights", scalars=1)


def pack_weights(pieces, proj, part, me):
    rows = proj.shape[0]
    hidden = pieces[0].shape[1] - 3 * part

    def kernel(me_ref, p0, p1, p2, p3, proj_ref, attn, up):
        for away, ref in enumerate((p0, p1, p2, p3)):
            member = jnp.bitwise_xor(me_ref[0], away)
            start = pl.multiple_of(member * rows, rows)
            attn[pl.ds(start, rows), : 3 * part] = ref[:, : 3 * part]
            up[pl.ds(start, rows), :] = ref[:, 3 * part :]
        for j in range(4):
            attn[j * rows : (j + 1) * rows, 3 * part :] = proj_ref[:, j * part : (j + 1) * part]

    outs = [shape_of((4 * rows, 4 * part), LOW), shape_of((4 * rows, hidden), LOW)]
    return call(kernel, outs, [me, *pieces, proj], "pack_weights", scalars=1)


def spread(count, team):
    rest = count // team
    return [(i, (i % rest) * team + i // rest) for i in range(count)]


def widen(rows, width):
    height, columns = rows.shape
    parts = columns // width
    if parts == 1:
        return rows
    return rows.reshape(height, parts, width).transpose(1, 0, 2).reshape(parts * height, width)


def narrow(stacked, height):
    lead = stacked.shape[:-2]
    parts = stacked.shape[-2] // height
    if parts == 1:
        return stacked
    width = stacked.shape[-1]
    shaped = stacked.reshape(lead + (parts, height, width))
    return jnp.moveaxis(shaped, -3, -2).reshape(lead + (height, parts * width))


def ring_order(outer, inner):
    order = []
    for a in range(outer):
        row = range(1, inner) if a % 2 == 0 else range(inner - 1, 0, -1)
        order += [a * inner + b for b in row]
    return order + [a * inner for a in range(outer - 1, -1, -1)]


def ring_table():
    outer, inner = lax.axis_size("outer"), lax.axis_size("inner")
    order = ring_order(outer, inner)
    rest = outer * inner
    place = {team: i for i, team in enumerate(order)}
    table = np.array(
        [
            [[order[(place[f] + sign * k) % rest] for k in range(rest)] for sign in (-1, 1)]
            for f in range(rest)
        ],
        np.int32,
    )
    here = lax.axis_index("outer") * inner + lax.axis_index("inner")
    return lax.dynamic_index_in_dim(jnp.asarray(table), here, 0, keepdims=False)


def ring_shift(values, sign):
    order = ring_order(lax.axis_size("outer"), lax.axis_size("inner"))
    rest = len(order)
    return lax.ppermute(values, REST, [(order[i], order[(i + sign) % rest]) for i in range(rest)])


def ring_step(low_half, high_half):
    low_half, high_half = ring_shift(low_half, 1), ring_shift(high_half, -1)
    return lax.optimization_barrier((low_half, high_half))


def ring_gather(low_half, high_half, table, joined):
    rest = table.shape[1]
    rows, columns = low_half.shape
    back, ahead = [low_half], [high_half]
    for _ in range(rest - 1):
        low_half, high_half = ring_step(low_half, high_half)
        back.append(low_half)
        ahead.append(high_half)

    def kernel(table_ref, *refs):
        outs = refs[2 * rest :]
        for k in range(rest):
            if joined:
                outs[0][table_ref[0, k], :rows, :] = refs[k][...]
                outs[0][table_ref[1, k], rows:, :] = refs[rest + k][...]
            else:
                outs[0][table_ref[0, k], :, :] = refs[k][...]
                outs[1][table_ref[1, k], :, :] = refs[rest + k][...]

    if joined:
        outs = [shape_of((rest, 2 * rows, columns), LOW)]
    else:
        outs = [shape_of((rest, rows, columns), LOW)] * 2
    return call(kernel, outs, [table, *back, *ahead], "assemble", scalars=1)


def ring_sum(low_parts, high_parts, table, joined):
    rest = table.shape[1]
    _, rows, columns = low_parts.shape
    rows = rows // 2 if joined else rows

    def step(k, came):
        last = k == rest
        dtype = WIDE if last else LOW

        def kernel(table_ref, *refs):
            ins, outs = refs[: len(refs) - 2], refs[len(refs) - 2 :]
            for i in range(2):
                value = ins[i][0]
                if came:
                    value = (value.astype(WIDE) + ins[2 + i][...].astype(WIDE)).astype(dtype)
                outs[i][...] = value

        whole = pl.BlockSpec((rows, columns), lambda i, t: (0, 0))
        grid_spec = pltpu.PrefetchScalarGridSpec(
            num_scalar_prefetch=1,
            grid=(1,),
            in_specs=[
                pl.BlockSpec((1, rows, columns), lambda i, t: (t[0, k % rest], 0, 0)),
                pl.BlockSpec(
                    (1, rows, columns), lambda i, t: (t[1, k % rest], 1 if joined else 0, 0)
                ),
            ]
            + [whole] * len(came),
            out_specs=[whole, whole],
        )
        return pl.pallas_call(
            kernel,
            grid_spec=grid_spec,
            out_shape=[shape_of((rows, columns), dtype)] * 2,
            cost_estimate=pl.CostEstimate(
                flops=0, bytes_accessed=12 * rows * columns, transcendentals=0
            ),
            name="ring_add",
        )(table, low_parts, high_parts, *came)

    came = step(1, [])
    for k in range(2, rest + 1):
        came = step(k, ring_step(*came))
    return came


def small_gather(values):
    out = values[None]
    for axis in ("frame", "core", "inner", "outer"):
        size, here, step = lax.axis_size(axis), lax.axis_index(axis), 1
        while step < size:
            came = lax.ppermute(out, axis, [(i, i ^ step) for i in range(size)])
            first = (here & step) == 0
            out = jnp.concatenate([jnp.where(first, out, came), jnp.where(first, came, out)], axis=0)
            step *= 2
    return out


def small_sum(split, common):
    for axis in ("outer", "inner"):
        size, here = lax.axis_size(axis), lax.axis_index(axis)
        step = size // 2
        while step >= 1:
            half = split.shape[1] // 2
            bit = (here // step) % 2
            keep = lax.dynamic_slice_in_dim(split, bit * half, half, 1)
            send = lax.dynamic_slice_in_dim(split, (1 - bit) * half, half, 1)
            pairs = [(i, i ^ step) for i in range(size)]
            packed = jnp.concatenate([send.reshape(-1), common.reshape(-1)])
            came = lax.ppermute(packed, axis, pairs)
            split = keep + came[: keep.size].reshape(keep.shape)
            common = common + came[keep.size :].reshape(common.shape)
            step //= 2
    return split, common


def head_means(part, head_size):
    row = lax.broadcasted_iota(jnp.int32, (part, part), 0) // head_size
    column = lax.broadcasted_iota(jnp.int32, (part, part), 1) // head_size
    return jnp.where(row == column, 1.0 / head_size, 0.0).astype(WIDE)


def head_mean(values, matrix):
    return jnp.dot(values, matrix, precision=HIGHEST, preferred_element_type=WIDE)


def head_normed(values, matrix):
    center = values - head_mean(values, matrix)
    rate = lax.rsqrt(head_mean(center * center, matrix) + EPSILON)
    return center * rate, rate


def join(refs, out_ref):
    start = 0
    for ref in refs:
        out_ref[start : start + ref.shape[0], :] = ref[...]
        start += ref.shape[0]


def spans(refs):
    start = 0
    for ref in refs:
        yield start, start + ref.shape[0], ref
        start += ref.shape[0]


def flat_rows(ref, first, height, columns):
    block = ref[:, first : first + height, columns]
    return block.reshape(block.shape[0] * height, block.shape[2])


def tiles_of(total, group, block):
    for base in range(0, total, group):
        for start in range(base, base + group, block):
            yield start, base


def allowed_of(ids_col, ids_row, start, base, block, group, use_frame):
    if use_frame:
        row = lax.broadcasted_iota(jnp.int32, (block, group), 0) // FRAME_TOK
        column = lax.broadcasted_iota(jnp.int32, (block, group), 1) // FRAME_TOK
        return row == column
    return ids_col[start : start + block, :] == ids_row[:, base : base + group]


def plan(frames, rows, use_frame):
    group = 2 * FRAME_TOK if use_frame else frames * rows
    return group, min(group, 256)


def part_shapes(pieces, width):
    half = len(pieces) // 2
    return [shape_of((m.shape[0], width), WIDE if i < half else LOW) for i, m in enumerate(pieces)]


def attn_forward(pieces, weights, bias, head_gain, head_shift, ids, head_size, frames, use_frame):
    attn, proj, height, wide = weights
    rest, unit, _ = attn.shape
    width, part = rest * unit, head_gain.shape[-1]
    total = sum(m.shape[0] for m in pieces)
    count = len(pieces)
    group, block = plan(frames, total // (2 * frames), use_frame)
    lanes = min(128, part)
    per = lanes // head_size
    scale = head_size ** (-0.5)

    def kernel(*refs):
        piece_refs = refs[:count]
        wq, wp, bias_ref, gain_ref, shift_ref, ids_col, ids_row = refs[count : count + 7]
        first, raw, qkv, lse, flat = refs[count + 7 : count + 12]
        outs = refs[count + 12 :]
        join(piece_refs, first)
        matrix = head_means(part, head_size)
        mixed = dot(first[...], flat_rows(wq, 0, unit, slice(0, 3 * part))) + bias_ref[...]
        raw[...] = mixed[:, : 2 * part]
        for i in range(2):
            unit_i, _ = head_normed(mixed[:, i * part : (i + 1) * part], matrix)
            value = unit_i * gain_ref[i : i + 1, :] + shift_ref[i : i + 1, :]
            qkv[:, i * part : (i + 1) * part] = value.astype(LOW)
        qkv[:, 2 * part :] = mixed[:, 2 * part :].astype(LOW)
        place = lax.broadcasted_iota(jnp.int32, (1, lanes), 1) // head_size
        for start, base in tiles_of(total, group, block):
            allowed = allowed_of(ids_col, ids_row, start, base, block, group, use_frame)
            stats = []
            for lane in range(0, part, lanes):
                query = qkv[start : start + block, lane : lane + lanes] * jnp.asarray(scale, LOW)
                key = qkv[base : base + group, part + lane : part + lane + lanes]
                value = qkv[base : base + group, 2 * part + lane : 2 * part + lane + lanes]
                out = jnp.zeros((block, lanes), WIDE)
                for h in range(per):
                    mask = place == h
                    scores = dot_nt(jnp.where(mask, query, jnp.zeros_like(query)), key)
                    scores = jnp.where(allowed, scores, -jnp.inf)
                    top = jnp.max(scores, axis=-1, keepdims=True)
                    weight = jnp.exp(scores - top)
                    norm = jnp.sum(weight, axis=-1, keepdims=True)
                    stats.append(top + jnp.log(norm))
                    probs = (weight * (1.0 / norm)).astype(LOW)
                    out = jnp.where(mask, dot(probs, value), out)
                flat[start : start + block, lane : lane + lanes] = out.astype(LOW)
            lse[start : start + block, :] = jnp.concatenate(stats, axis=1)
        for a in range(0, width, wide):
            b = a + wide
            chunk = flat_rows(wp, a // wide * height, height, slice(wp.shape[2] - wide, wp.shape[2]))
            for start, stop, ref in spans(outs):
                ref[:, a:b] = dot(flat[start:stop, :], chunk).astype(ref.dtype)

    outs = [
        shape_of((total, width), LOW),
        shape_of((total, 2 * part), WIDE),
        shape_of((total, 3 * part), LOW),
        shape_of((total, part // head_size), WIDE),
        shape_of((total, part), LOW),
    ] + part_shapes(pieces, width)
    args = list(pieces) + [attn, proj, bias, head_gain, head_shift, ids.reshape(-1, 1), ids.reshape(1, -1)]
    flops = 2 * total * (width * 4 * part + group * 2 * part)
    res = call(kernel, outs, args, "attn_forward", flops)
    return res[:5], res[5 : 5 + count // 2], res[5 + count // 2 :]


def attn_backward(pieces, weights, head_gain, kept, ids, head_size, frames, use_frame):
    _, raw, qkv, lse, _ = kept
    attn, proj, height, wide = weights
    rest, unit, _ = attn.shape
    width, part = rest * unit, head_gain.shape[-1]
    total = sum(m.shape[0] for m in pieces)
    count = len(pieces)
    group, block = plan(frames, total // (2 * frames), use_frame)
    lanes = min(128, part)
    per = lanes // head_size
    scale = head_size ** (-0.5)

    def kernel(*refs):
        piece_refs = refs[:count]
        wq, wp, gain_ref, raw_ref, qkv_ref, lse_ref, ids_col, ids_row = refs[count : count + 8]
        joined, low_mixed, sums, head_sums = refs[count + 8 : count + 12]
        outs = refs[count + 12 : count + 12 + count]
        grad_out, grad_three = refs[count + 12 + count :]
        join(piece_refs, joined)
        grad_flat = jnp.zeros((total, part), WIDE)
        for a in range(0, width, wide):
            b = a + wide
            chunk = flat_rows(wp, a // wide * height, height, slice(wp.shape[2] - wide, wp.shape[2]))
            grad_flat += dot_nt(joined[:, a:b], chunk)
        grad_out[...] = grad_flat.astype(LOW)
        place = lax.broadcasted_iota(jnp.int32, (1, lanes), 1) // head_size
        for start, base in tiles_of(total, group, block):
            allowed = allowed_of(ids_col, ids_row, start, base, block, group, use_frame)
            stats = lse_ref[start : start + block, :]
            for lane in range(0, part, lanes):
                query = qkv_ref[start : start + block, lane : lane + lanes] * jnp.asarray(scale, LOW)
                key = qkv_ref[base : base + group, part + lane : part + lane + lanes]
                value = qkv_ref[base : base + group, 2 * part + lane : 2 * part + lane + lanes]
                grad_here = grad_out[start : start + block, lane : lane + lanes]
                grad_q = jnp.zeros((block, lanes), WIDE)
                grad_k = jnp.zeros((group, lanes), WIDE)
                grad_v = jnp.zeros((group, lanes), WIDE)
                for h in range(per):
                    mask = place == h
                    head = lane // head_size + h
                    scores = dot_nt(jnp.where(mask, query, jnp.zeros_like(query)), key)
                    probs = jnp.exp(jnp.where(allowed, scores - stats[:, head : head + 1], -jnp.inf))
                    grad_p = dot_nt(jnp.where(mask, grad_here, jnp.zeros_like(grad_here)), value)
                    delta = jnp.sum(probs * grad_p, axis=-1, keepdims=True)
                    grad_s = (probs * (grad_p - delta)).astype(LOW)
                    grad_q = jnp.where(mask, dot(grad_s, key), grad_q)
                    grad_k = jnp.where(mask, dot_tn(grad_s, query), grad_k)
                    grad_v = jnp.where(mask, dot_tn(probs.astype(LOW), grad_here), grad_v)
                grad_three[start : start + block, lane : lane + lanes] = grad_q * scale
                for at, grad in ((part, grad_k), (2 * part, grad_v)):
                    spot = (slice(base, base + group), slice(at + lane, at + lane + lanes))
                    if start == base:
                        grad_three[spot] = grad
                    else:
                        grad_three[spot] = grad_three[spot] + grad
        matrix = head_means(part, head_size)
        for i in range(2):
            here = slice(i * part, (i + 1) * part)
            grad = grad_three[:, here]
            unit_i, rate = head_normed(raw_ref[:, here], matrix)
            head_sums[i : i + 1, :] = jnp.sum(grad * unit_i, axis=0, keepdims=True)
            head_sums[2 + i : 3 + i, :] = jnp.sum(grad, axis=0, keepdims=True)
            inner = grad * gain_ref[i : i + 1, :]
            mean_one = head_mean(inner, matrix)
            mean_two = head_mean(inner * unit_i, matrix)
            result = rate * (inner - mean_one - unit_i * mean_two)
            sums[:, here] = jnp.sum(result, axis=0, keepdims=True)
            low_mixed[:, here] = result.astype(LOW)
        result = grad_three[:, 2 * part :]
        sums[:, 2 * part :] = jnp.sum(result, axis=0, keepdims=True)
        low_mixed[:, 2 * part :] = result.astype(LOW)
        weight = flat_rows(wq, 0, unit, slice(0, 3 * part))
        for start, stop, ref in spans(outs):
            ref[...] = dot_nt(low_mixed[start:stop, :], weight).astype(ref.dtype)

    outs = [
        shape_of((total, width), LOW),
        shape_of((total, 3 * part), LOW),
        shape_of((1, 3 * part), WIDE),
        shape_of((4, part), WIDE),
    ] + part_shapes(pieces, width)
    scratch = [pltpu.VMEM((total, part), LOW), pltpu.VMEM((total, 3 * part), WIDE)]
    args = list(pieces) + [attn, proj, head_gain, raw, qkv, lse, ids.reshape(-1, 1), ids.reshape(1, -1)]
    flops = 2 * total * (width * 4 * part + group * 5 * part)
    res = call(kernel, outs, args, "attn_backward", flops, scratch)
    return res[:4], res[4 : 4 + count // 2], res[4 + count // 2 :]


def attn_weight_grads(first, low_mixed, flat, att_low, rest, height):
    width, part = first.shape[1], flat.shape[1]
    unit = width // rest
    wide = width * height // unit

    def kernel(first_ref, mixed_ref, flat_ref, att_ref, out):
        product = dot_tn(first_ref[...], mixed_ref[...]).astype(LOW)
        out[:, :, : 3 * part] = product.reshape(rest, unit, 3 * part)
        product = dot_tn(flat_ref[...], att_ref[...]).astype(LOW)
        for j in range(unit // height):
            chunk = product[:, j * wide : (j + 1) * wide].reshape(rest, height, wide)
            out[:, j * height : (j + 1) * height, 3 * part :] = chunk

    flops = 8 * first.shape[0] * width * part
    out = shape_of((rest, unit, 4 * part), LOW)
    return call(kernel, [out], [first, low_mixed, flat, att_low], "attn_weight_grads", flops)[0]


def mlp_forward(pieces, weight_up, weight_down, bias):
    rest, unit, hidden = weight_up.shape
    width = rest * unit
    total = sum(m.shape[0] for m in pieces)
    count = len(pieces)

    def kernel(*refs):
        piece_refs = refs[:count]
        up, down, bias_ref = refs[count : count + 3]
        second, act, slope = refs[count + 3 : count + 6]
        outs = refs[count + 6 :]
        join(piece_refs, second)
        pre = dot(second[...], flat_rows(up, 0, unit, slice(None))) + bias_ref[...]
        below = 0.5 * (1.0 + lax.erf(pre * ROOT_HALF))
        act[...] = (pre * below).astype(LOW)
        slope[...] = (below + pre * (ROOT_TWO_PI * jnp.exp(-0.5 * pre * pre))).astype(LOW)
        weight = flat_rows(down, 0, down.shape[1], slice(None))
        for start, stop, ref in spans(outs):
            ref[...] = dot(act[start:stop, :], weight).astype(ref.dtype)

    outs = [
        shape_of((total, width), LOW),
        shape_of((total, hidden), LOW),
        shape_of((total, hidden), LOW),
    ] + part_shapes(pieces, width)
    args = list(pieces) + [weight_up, weight_down, bias]
    res = call(kernel, outs, args, "mlp_forward", 4 * total * width * hidden)
    return res[:3], res[3 : 3 + count // 2], res[3 + count // 2 :]


def mlp_backward(pieces, weight_up, weight_down, slope):
    rest, unit, hidden = weight_up.shape
    width = rest * unit
    total = sum(m.shape[0] for m in pieces)
    count = len(pieces)

    def kernel(*refs):
        piece_refs = refs[:count]
        up, down, slope_ref = refs[count : count + 3]
        joined, low_pre, sums = refs[count + 3 : count + 6]
        outs = refs[count + 6 :]
        join(piece_refs, joined)
        weight = flat_rows(down, 0, down.shape[1], slice(None))
        grad = dot_nt(joined[...], weight) * slope_ref[...].astype(WIDE)
        sums[...] = jnp.sum(grad, axis=0, keepdims=True)
        low_pre[...] = grad.astype(LOW)
        weight = flat_rows(up, 0, unit, slice(None))
        for start, stop, ref in spans(outs):
            ref[...] = dot_nt(low_pre[start:stop, :], weight).astype(ref.dtype)

    outs = [
        shape_of((total, width), LOW),
        shape_of((total, hidden), LOW),
        shape_of((1, hidden), WIDE),
    ] + part_shapes(pieces, width)
    args = list(pieces) + [weight_up, weight_down, slope]
    res = call(kernel, outs, args, "mlp_backward", 4 * total * width * hidden)
    return res[:3], res[3 : 3 + count // 2], res[3 + count // 2 :]


def added(refs):
    total = refs[0][...]
    for ref in refs[1:]:
        total = total + ref[...].astype(WIDE)
    return total


def row_of(vectors, kind, depth, which):
    at = kind + 2 * depth + which
    return vectors[at : at + 1, :]


def first_norm(tokens, vectors):
    def kernel(tokens_ref, vec, low):
        unit, _ = normed(tokens_ref[...].astype(WIDE))
        low[...] = (unit * row_of(vec, GAIN, 0, 0) + row_of(vec, SHIFT, 0, 0)).astype(LOW)

    return call(kernel, [shape_of(tokens.shape, LOW)], [tokens, vectors], "first_norm")[0]


def branch_norm(stream, terms, vectors, depth, which):
    after = (depth, 1) if which == 0 else (depth + 1, 0)

    def kernel(stream_ref, *refs):
        (vec, branch, result, low), term_refs = refs[-4:], refs[:-4]
        value = added(term_refs) + row_of(vec, OUT, depth, which)
        branch[...] = value
        value = stream_ref[...].astype(WIDE) + row_of(vec, SCALE, depth, which) * value
        result[...] = value
        unit, _ = normed(value)
        low[...] = (unit * row_of(vec, GAIN, *after) + row_of(vec, SHIFT, *after)).astype(LOW)

    outs = [shape_of(stream.shape, WIDE), shape_of(stream.shape, WIDE), shape_of(stream.shape, LOW)]
    return call(kernel, outs, [stream, *terms, vectors], "branch_norm")


def turn(middle, terms, cotangent, vectors):
    def kernel(middle_ref, *refs):
        (cot, vec, result, low, sums), term_refs = refs[-5:], refs[:-5]
        branch = added(term_refs) + row_of(vec, OUT, 1, 1)
        scale = row_of(vec, SCALE, 1, 1)
        result[...] = (middle_ref[...] + scale * branch).astype(LOW)
        grad = cot[...].astype(WIDE)
        grad_branch = grad * scale
        low[...] = grad_branch.astype(LOW)
        sums[0:1, :] = jnp.sum(grad * branch, axis=0, keepdims=True)
        sums[1:2, :] = jnp.sum(grad_branch, axis=0, keepdims=True)

    shape = middle.shape
    outs = [shape_of(shape, LOW), shape_of(shape, LOW), shape_of((2, shape[1]), WIDE)]
    return call(kernel, outs, [middle, *terms, cotangent, vectors], "turn")


def norm_back(grad, terms, stream, branch, vectors, depth, which, before):
    def kernel(*refs):
        grad_ref, stream_ref, vec = refs[0], refs[1], refs[2]
        inputs = 4 if before else 3
        term_refs = refs[inputs : inputs + len(terms)]
        result, low, sums = (refs[inputs + len(terms) :] + (None,))[:3] if before else (
            None, refs[inputs + len(terms)], refs[inputs + len(terms) + 1],
        )
        came = added(term_refs)
        unit, rate = normed(stream_ref[...].astype(WIDE))
        sums[0:1, :] = jnp.sum(came * unit, axis=0, keepdims=True)
        sums[1:2, :] = jnp.sum(came, axis=0, keepdims=True)
        value = grad_ref[...].astype(WIDE)
        value = value + normed_back(came, unit, rate, row_of(vec, GAIN, depth, which))
        if not before:
            low[...] = value.astype(LOW)
            return
        result[...] = value
        sums[2:3, :] = jnp.sum(value * refs[3][...], axis=0, keepdims=True)
        value = value * row_of(vec, SCALE, *before)
        sums[3:4, :] = jnp.sum(value, axis=0, keepdims=True)
        low[...] = value.astype(LOW)

    shape = grad.shape
    outs = [shape_of(shape, LOW), shape_of((4 if before else 2, shape[1]), WIDE)]
    args = [grad, stream, vectors]
    if before:
        outs = [shape_of(shape, WIDE)] + outs
        args = args + [branch]
    return call(kernel, outs, args + list(terms), "norm_back")


def split_grads(grads, me):
    rows, width = grads[0].shape[0] * len(grads) // 4, grads[0].shape[1]

    def kernel(me_ref, *refs):
        ins, outs = refs[: len(grads)], refs[len(grads) : len(grads) + 4]
        joined = refs[-1]
        join(ins, joined)
        for away, out in enumerate(outs):
            member = jnp.bitwise_xor(me_ref[0], away)
            out[...] = joined[pl.ds(pl.multiple_of(member * rows, rows), rows), :].astype(LOW)

    scratch = [pltpu.VMEM((4 * rows, width), WIDE)]
    out = shape_of((rows, width), LOW)
    return call(kernel, [out] * 4, [me, *grads], "split_grads", scratch=scratch, scalars=1)


def place_grads(qkv_pieces, up_pieces, proj, down, part, rest, me):
    rows, hidden = up_pieces[0][0].shape
    width = 4 * part
    lanes = hidden // rest

    def kernel(me_ref, *refs):
        pieces, (proj_ref, down0, down1) = refs[:16], refs[16:19]
        qkv_out, up_out, proj_out, down_out = refs[19:]
        for depth in range(2):
            for away in range(4):
                member = jnp.bitwise_xor(me_ref[0], away)
                ref = pieces[4 * depth + away]
                for s in range(3):
                    start = pl.multiple_of(s * width + member * part, 128)
                    value = ref[:, s * part : (s + 1) * part].astype(WIDE)
                    qkv_out[depth, :, pl.ds(start, part)] = value
                ref = pieces[8 + 4 * depth + away]
                for f in range(rest):
                    start = pl.multiple_of((f * 4 + member) * lanes, 128)
                    value = ref[:, f * lanes : (f + 1) * lanes].astype(WIDE)
                    up_out[depth, :, pl.ds(start, lanes)] = value
            down_out[depth] = (down0, down1)[depth][...]
        proj_out[...] = proj_ref[...].astype(WIDE)

    outs = [
        shape_of((2, rows, 3 * width), WIDE),
        shape_of((2, rows, 4 * hidden), WIDE),
        shape_of(proj.shape, WIDE),
        shape_of((2,) + down[0].shape, WIDE),
    ]
    args = [me, *qkv_pieces[0], *qkv_pieces[1], *up_pieces[0], *up_pieces[1], proj, *down]
    return call(kernel, outs, args, "place_grads", scalars=1)


def on_device(
    tokens,
    cotangent,
    scene_ids,
    frame_index,
    qkv_weight,
    qkv_bias,
    proj_weight,
    fc1_weight,
    fc1_bias,
    fc2_weight,
    out_bias,
    norm_gain,
    norm_bias,
    layer_scale,
    qk_gain,
    qk_bias,
):
    frames = lax.axis_size("frame")
    team = 2 * frames
    rest = lax.axis_size("outer") * lax.axis_size("inner")
    count = team * rest
    rows, width = tokens.shape
    head_size = qk_gain.shape[-1]
    heads = width // head_size // team
    part = heads * head_size
    hidden = fc1_weight.shape[-1] // team
    mine = lax.axis_index("core") * frames + lax.axis_index("frame")
    here = lax.axis_index("outer") * lax.axis_size("inner") + lax.axis_index("inner")
    me = mine.reshape(1).astype(jnp.int32)
    shard_rows = qkv_weight.shape[1]
    fc2_rows = fc2_weight.shape[1]
    unit = team * shard_rows
    table = ring_table()
    quick = frames == 2 and shard_rows % 32 == 0 and part % 128 == 0 and (hidden // rest) % 128 == 0

    shards = []
    proj_here = lax.ppermute(proj_weight, EVERY, spread(count, team))
    for depth in range(2):
        if quick:
            split = split_weights(qkv_weight[depth], fc1_weight[depth], part, rest, me)
            pieces = [split[0], swap(split[1], "frame"), swap(split[2], "core"), cross(split[3])]
            attn, up = pack_weights(pieces, proj_here[depth], part, me)
            down = fc2_weight[depth]
        else:
            attn = exchange_columns(
                qkv_weight[depth]
                .reshape(shard_rows, 3, team, part)
                .transpose(0, 2, 1, 3)
                .reshape(shard_rows, team, 3 * part)
            ).reshape(unit, 3 * part)
            attn = jnp.concatenate([attn, widen(proj_here[depth], part)], axis=1)
            up = exchange_columns(
                fc1_weight[depth]
                .reshape(shard_rows, rest, team, hidden // rest)
                .transpose(0, 2, 1, 3)
                .reshape(shard_rows, team, hidden)
            ).reshape(unit, hidden)
            down = widen(fc2_weight[depth], hidden)
        shards.append((attn, up, down))

    weights = []
    for depth in range(2):
        attn, up, down = shards[depth]
        (attn,) = ring_gather(attn[: unit // 2], attn[unit // 2 :], table, True)
        up, down = ring_gather(up, down, table, False)
        if quick:
            weights.append(((attn, attn, shard_rows, part), up, down))
        else:
            proj = narrow(attn[:, :, 3 * part :], shard_rows).reshape(1, part, width)
            down = narrow(down, fc2_rows).reshape(1, hidden, width)
            weights.append(((attn, proj, part, width), up, down))

    small_parts = (qkv_bias, fc1_bias, out_bias, norm_gain, norm_bias, layer_scale)
    small = small_gather(jnp.concatenate([m.reshape(-1) for m in small_parts])).astype(WIDE)
    n_qkv, n_up = qkv_bias.size, fc1_bias.size
    bias_qkv = small[:, :n_qkv].reshape(count, 2, -1).transpose(1, 0, 2).reshape(2, 3, team, part)
    bias_qkv = lax.dynamic_index_in_dim(bias_qkv, mine, 2, keepdims=False).reshape(2, 3 * part)
    bias_up = small[:, n_qkv : n_qkv + n_up].reshape(rest, team, 2, -1)
    bias_up = lax.dynamic_index_in_dim(bias_up, mine, 1, keepdims=False)
    bias_up = bias_up.transpose(1, 0, 2).reshape(2, hidden)
    vectors = small[:, n_qkv + n_up :].reshape(count, 16, -1).transpose(1, 0, 2).reshape(16, width)
    head_gain = jnp.tile(qk_gain.astype(WIDE), (1, 1, heads))
    head_shift = jnp.tile(qk_bias.astype(WIDE), (1, 1, heads))

    ids = jnp.concatenate([m.reshape(-1) for m in team_gather(scene_ids.reshape(1, rows))])

    streams, middles, branches, kept = [tokens], [], [], []
    low = first_norm(tokens, vectors)
    for depth in range(2):
        attn_weights, weight_up, weight_down = weights[depth]
        kept_attn, own, peer = attn_forward(
            team_gather(low), attn_weights, bias_qkv[depth : depth + 1], head_gain[depth], head_shift[depth],
            ids, head_size, frames, depth == 0,
        )
        branch_one, middle, low = branch_norm(streams[depth], team_sum(own, peer), vectors, depth, 0)
        kept_mlp, own, peer = mlp_forward(team_gather(low), weight_up, weight_down, bias_up[depth : depth + 1])
        terms = team_sum(own, peer)
        branch_two = None
        if depth == 0:
            branch_two, stream, low = branch_norm(middle, terms, vectors, 0, 1)
            streams.append(stream)
        middles.append(middle)
        branches.append((branch_one, branch_two))
        kept.append((kept_attn, kept_mlp))

    activations, low, turn_sums = turn(middles[1], terms, cotangent, vectors)
    grad = cotangent
    rows_of = {(SCALE, 1, 1): turn_sums[0], (OUT, 1, 1): turn_sums[1]}
    sums_up, sums_qkv, head_sums = [None, None], [None, None], [None, None]
    finals = [None, None]
    for depth in (1, 0):
        attn_weights, weight_up, weight_down = weights[depth]
        kept_attn, (second, act, slope) = kept[depth]
        first, flat = kept_attn[0], kept_attn[4]
        (branch_low, pre_low, sum_up), own, peer = mlp_backward(team_gather(low), weight_up, weight_down, slope)
        sums_up[depth] = sum_up
        grad_down = dot_tn(act, branch_low).astype(LOW)
        grad_up = dot_tn(second, pre_low).astype(LOW)
        grad_middle, low, sums = norm_back(
            grad, team_sum(own, peer), middles[depth], branches[depth][0], vectors, depth, 1, (depth, 0)
        )
        for kind, place, row in ((GAIN, 1, 0), (SHIFT, 1, 1), (SCALE, 0, 2), (OUT, 0, 3)):
            rows_of[kind, depth, place] = sums[row]
        (att_low, mixed_low, sum_qkv, head_sum), own, peer = attn_backward(
            team_gather(low), attn_weights, head_gain[depth], kept_attn, ids, head_size, frames, depth == 0
        )
        sums_qkv[depth], head_sums[depth] = sum_qkv, head_sum
        terms = team_sum(own, peer)
        if depth == 1:
            grad, low, sums = norm_back(
                grad_middle, terms, streams[1], branches[0][1], vectors, 1, 0, (0, 1)
            )
            rows_of[SCALE, 0, 1], rows_of[OUT, 0, 1] = sums[2], sums[3]
        else:
            input_grad, sums = norm_back(grad_middle, terms, tokens, None, vectors, 0, 0, None)
        rows_of[GAIN, depth, 0], rows_of[SHIFT, depth, 0] = sums[0], sums[1]

        grad_up = grad_up.reshape(rest, unit, hidden)
        if quick:
            grad_down = grad_down.reshape(rest, fc2_rows, width)
            attn = attn_weight_grads(first, mixed_low, flat, att_low, rest, shard_rows)
        else:
            grad_down = grad_down.reshape(rest, fc2_rows, width // hidden, hidden)
            grad_down = grad_down.transpose(0, 2, 1, 3).reshape(rest, -1, hidden)
            grad_qkv = dot_tn(first, mixed_low).astype(LOW).reshape(rest, unit, 3 * part)
            grad_proj = dot_tn(flat, att_low).astype(LOW).reshape(rest, shard_rows, team, part)
            grad_proj = grad_proj.transpose(0, 2, 1, 3).reshape(rest, unit, part)
            attn = jnp.concatenate([grad_qkv, grad_proj], axis=2)
        up_sum, down_sum = ring_sum(grad_up, grad_down, table, False)
        attn_sum = ring_sum(attn, attn, table, True)
        if quick:
            up_pieces = split_grads([up_sum], me)
            qkv_pieces = split_grads([m[:, : 3 * part] for m in attn_sum], me)
            up_pieces, qkv_pieces = (
                [m[0], swap(m[1], "frame"), swap(m[2], "core"), cross(m[3])] for m in (up_pieces, qkv_pieces)
            )
            proj_sum = jnp.concatenate([m[:, 3 * part :] for m in attn_sum], axis=0)
            finals[depth] = (qkv_pieces, up_pieces, narrow(proj_sum, shard_rows).astype(LOW), down_sum)
        else:
            attn_sum = jnp.concatenate(attn_sum, axis=0)
            qkv_mine = exchange_columns(
                attn_sum[:, : 3 * part].astype(LOW).reshape(team, shard_rows, 3 * part).transpose(1, 0, 2)
            )
            qkv_mine = qkv_mine.reshape(team, shard_rows, 3, part).transpose(1, 2, 0, 3)
            up_mine = exchange_columns(up_sum.astype(LOW).reshape(team, shard_rows, hidden).transpose(1, 0, 2))
            up_mine = up_mine.reshape(team, shard_rows, rest, hidden // rest).transpose(1, 2, 0, 3)
            finals[depth] = (
                qkv_mine.reshape(shard_rows, -1),
                up_mine.reshape(shard_rows, -1),
                narrow(attn_sum[:, 3 * part :], shard_rows).astype(LOW),
                narrow(down_sum, fc2_rows),
            )

    proj_grad = lax.ppermute(
        jnp.stack([finals[0][2], finals[1][2]]), EVERY, [(b, a) for a, b in spread(count, team)]
    )
    if quick:
        qkv_grad, up_grad, proj_grad, down_grad = place_grads(
            [finals[0][0], finals[1][0]], [finals[0][1], finals[1][1]], proj_grad,
            [finals[0][3], finals[1][3]], part, rest, me,
        )
    else:
        proj_grad = proj_grad.astype(WIDE)
        qkv_grad, up_grad, down_grad = (
            jnp.stack([finals[0][i], finals[1][i]]).astype(WIDE) for i in (0, 1, 3)
        )

    names = [(kind, depth, place) for kind in (OUT, GAIN, SHIFT, SCALE) for depth in (0, 1) for place in (0, 1)]
    token_sums = jnp.stack([rows_of[name] for name in names])
    full_qkv = lax.dynamic_update_slice(
        jnp.zeros((6, team, part), WIDE),
        jnp.concatenate(sums_qkv, axis=0).reshape(6, 1, part),
        (0, mine, 0),
    ).reshape(6, width)
    head_all = jnp.stack(head_sums).reshape(-1, heads, head_size).sum(axis=1).reshape(1, -1)
    head_all = jnp.pad(head_all, ((0, 0), (0, width - head_all.shape[1])))
    team_rows = jnp.concatenate([token_sums, full_qkv, head_all], axis=0)
    team_rows = team_rows + swap(team_rows, "core")
    if frames == 2:
        team_rows = team_rows + swap(team_rows, "frame")
    else:
        team_rows = lax.psum(team_rows, "frame")
    sums_up = jnp.concatenate(sums_up, axis=0).reshape(2, rest, hidden // rest)
    sums_up = jnp.pad(sums_up, ((0, 0), (0, 0), (0, (width - hidden) // rest))).reshape(2, width)
    split = jnp.concatenate([team_rows[:16], sums_up], axis=0)
    split, common = small_sum(split, team_rows[16:])
    vector_grads = lax.dynamic_slice_in_dim(split[:16], mine * (width // count), width // count, 1)
    vector_grads = vector_grads.reshape(4, 2, 2, -1)
    grad_bias_qkv = common[:6].reshape(2, -1)
    grad_bias_qkv = lax.dynamic_slice_in_dim(
        grad_bias_qkv, (here * team + mine) * qkv_bias.shape[1], qkv_bias.shape[1], 1
    )
    head_all = common[6, : 8 * head_size].reshape(2, 2, 2, head_size)
    return (
        activations,
        input_grad,
        qkv_grad,
        grad_bias_qkv,
        proj_grad,
        up_grad,
        split[16:, : hidden // rest],
        down_grad,
        vector_grads[0],
        vector_grads[1],
        vector_grads[2],
        vector_grads[3],
        head_all[:, 0],
        head_all[:, 1],
    )


def solution(mesh):
    scenes, frames = mesh.shape["scene"], mesh.shape["frame"]
    rest = scenes // 2
    outer = 4 if rest % 4 == 0 else rest
    grid = Mesh(mesh.devices.reshape(outer, rest // outer, 2, frames), EVERY)
    by_rows = P(EVERY, None)
    second = P(None, EVERY)
    second_rows = P(None, EVERY, None)
    last = P(None, None, EVERY)
    return jax.shard_map(
        on_device,
        mesh=grid,
        in_specs=(
            by_rows, by_rows, P(EVERY), P(EVERY), second_rows, second, second_rows, second_rows,
            second, second_rows, last, last, last, last, P(), P(),
        ),
        out_specs=(
            by_rows, by_rows, second_rows, second, second_rows, second_rows, second, second_rows,
            last, last, last, last, P(), P(),
        ),
        check_vma=False,
    )
```

time: 865 us -> 629 us (0.73)
  the two profiles are of different devices: /device:TPU:7 before, /device:TPU:0 now
where the time goes in v2:
time: 629 us; the launch traced here: 617 us
  Pallas kernels  231 us (37%)
  starting transfers between devices  184 us (29%)
  waiting for transfers between devices  123 us (20%)
  local copies, waits for them, and re-layouts  58 us (9%)
  matrix products  11.8 us (2%)
    pallas_call x32, Pallas kernels, call(): pl.pallas_call(kernel, out_shape=list(outs), in_specs=in_specs, out_specs...  147 us
    ppermute x112, starting transfers between devices, ring_shift(): lax.ppermute(values, REST, [(order[i], order[(i + sign) % rest]) for i in...  119 us
    pallas_call x32, Pallas kernels, step(): pl.pallas_call(kernel, grid_spec=grid_spec, out_shape=[shape_of((rows, co...  84.7 us
    ppermute x112, waiting for transfers between devices, ring_shift(): lax.ppermute(values, REST, [(order[i], order[(i + sign) % rest]) for i in...  71 us
    ppermute x65, waiting for transfers between devices, swap(): return lax.ppermute(values, axis, [(0, 1), (1, 0)])  45.5 us
    ppermute x65, starting transfers between devices, swap(): return lax.ppermute(values, axis, [(0, 1), (1, 0)])  37.9 us
    unnamed x457, local copies, waits for them, and re-layouts  27.7 us
    ppermute x5, starting transfers between devices, small_gather(): came = lax.ppermute(out, axis, [(i, i ^ step) for i in range(size)])  13.5 us
  transfers between devices with their start and end apart: 193, of which 51 were waited for; matrix products, arithmetic and copies ran while one was open for 7% of the time, Pallas kernels for 31%

profile of v2, /device:TPU:0, one launch (start us, length us, event | category | flops | bytes accessed | tf_op | source)
XLA Modules:
  0.0 617.5 jit_solution(16812830647960662581)
XLA Ops:
  5.3 3.0 collective-permute-start
  16.9 5.6 collective-permute-start.2
  26.8 3.5 collective-permute-start.12
  30.3 3.6 collective-permute-start.3
  33.8 4.1 collective-permute-done.13.refs_9_
  37.9 2.9 collective-permute-start.14
  41.0 3.3 collective-permute-done.14.refs_2_
  44.2 3.0 collective-permute-done.15.refs_10_
  76.0 3.9 collective-permute-done.22.refs_6_
  85.3 3.5 collective-permute-done.40.refs_11_
  91.4 3.1 assemble.4.refs_4_.refs_5_
  95.3 12.3 %attn_forward.2 = (bf16[512,1024]{1,0:T(8,128)(2,1)}, f32[512,512]{1,0:T(8,128)}, bf16[512,768]{1,0:T(8,128)(2,1)}, f32[512,4]{1,0:T(8,128)}, bf16[512,256]{1,0:...) custom-call(bf16[128,1024]{1,0:T(8,128)(2,1)} %first_norm.1.refs_0_,, ...), custom_call_target="tpu_custom_call" | custom-call | flops 1140850688 | bytes 9980928 | tf_op jit(solution)/shard_map/attn_forward/pallas_call | solution.py:60
  116.8 6.6 %collective-permute-done.57.p3 = bf16[32,1792]{1,0:T(8,128)(2,1)S(1)} collective-permute-done((bf16[32,1792]{1,0:T(8,128)(2,1)}, bf16[32,1792]{1,0:T(8,128)(2,1)S(1)}, u32[]{:S(2)}, u32[]{:S(2)}) %collective-permute-start.57) | collective-permute-done | bytes 114720 | tf_op jit(solution)/shard_map/ppermute | solution.py:77
  143.3 6.0 collective-permute-done.59.refs_9_
  152.5 4.5 assemble.5
  157.8 6.5 %mlp_forward.2 = (bf16[512,1024]{1,0:T(8,128)(2,1)}, bf16[512,1024]{1,0:T(8,128)(2,1)}, bf16[512,1024]{1,0:T(8,128)(2,1)}, f32[128,1024]{1,0:T(8,128)}, f32[128,...) custom-call(bf16[128,1024]{1,0:T(8,128)(2,1)} %get-tuple-element.335.refs_0_, ...), custom_call_target="tpu_custom_call" | custom-call | flops 2147483648 | bytes 9965568 | tf_op jit(solution)/shard_map/mlp_forward/pallas_call | solution.py:60
  179.7 5.2 collective-permute-done.65.refs_12_
  196.3 3.8 collective-permute-done.68.refs_6_
  209.3 3.1 assemble.6.refs_4_.refs_5_
  213.2 9.8 %attn_forward.3 = (bf16[512,1024]{1,0:T(8,128)(2,1)}, f32[512,512]{1,0:T(8,128)}, bf16[512,768]{1,0:T(8,128)(2,1)}, f32[512,4]{1,0:T(8,128)}, bf16[512,256]{1,0:...) custom-call(bf16[128,1024]{1,0:T(8,128)(2,1)} %get-tuple-element.358, ...), custom_call_target="tpu_custom_call" | custom-call | flops 1207959552 | bytes 9980928 | tf_op jit(solution)/shard_map/attn_forward/pallas_call | solution.py:60
  228.7 3.1 collective-permute-done.86.refs_5_
  243.5 3.8 collective-permute-done.75.refs_1_
  249.8 4.4 assemble.7
  255.0 6.6 %mlp_forward.3 = (bf16[512,1024]{1,0:T(8,128)(2,1)}, bf16[512,1024]{1,0:T(8,128)(2,1)}, bf16[512,1024]{1,0:T(8,128)(2,1)}, f32[128,1024]{1,0:T(8,128)}, f32[128,...) custom-call(bf16[128,1024]{1,0:T(8,128)(2,1)} %get-tuple-element.383.refs_0_, ...), custom_call_target="tpu_custom_call" | custom-call | flops 2147483648 | bytes 9965568 | tf_op jit(solution)/shard_map/mlp_forward/pallas_call | solution.py:60
  265.9 6.9 %collective-permute-done.94.refs_2_ = bf16[128,1024]{1,0:T(8,128)(2,1)S(1)} collective-permute-done((bf16[128,1024]{1,0:T(8,128)(2,1)S(1)}, bf16[128,1024]{1,0:T(8,128)(2,1)S(1)}, u32[]{:S(2)}, u32[]{:S(2)}) %collective-permute-start.94) | collective-permute-done | bytes 262176 | tf_op jit(solution)/shard_map/ppermute | solution.py:73
  277.4 6.3 %collective-permute-done.95.refs_1_ = bf16[128,1024]{1,0:T(8,128)(2,1)S(1)} collective-permute-done((bf16[128,1024]{1,0:T(8,128)(2,1)}, bf16[128,1024]{1,0:T(8,128)(2,1)S(1)}, u32[]{:S(2)}, u32[]{:S(2)}) %collective-permute-start.95) | collective-permute-done | bytes 262176 | tf_op jit(solution)/shard_map/ppermute | solution.py:73
  285.9 7.5 %mlp_backward.2 = (bf16[512,1024]{1,0:T(8,128)(2,1)}, bf16[512,1024]{1,0:T(8,128)(2,1)}, f32[1,1024]{1,0:T(1,128)}, f32[128,1024]{1,0:T(8,128)}, f32[128,1024]{1...) custom-call(bf16[128,1024]{1,0:T(8,128)(2,1)} %get-tuple-element.407.refs_0_, ...), custom_call_target="tpu_custom_call" | custom-call | flops 2147483648 | bytes 9965568 | tf_op jit(solution)/shard_map/mlp_backward/pallas_call | solution.py:60
  297.8 6.9 %collective-permute-done.100.refs_6_ = bf16[128,1024]{1,0:T(8,128)(2,1)S(1)} collective-permute-done((bf16[128,1024]{1,0:T(8,128)(2,1)S(1)}, bf16[128,1024]{1,0:T(8,128)(2,1)S(1)}, u32[]{:S(2)}, u32[]{:S(2)}) %collective-permute-start.100) | collective-permute-done | bytes 262176 | tf_op jit(solution)/shard_map/ppermute | solution.py:73
  305.4 3.1 norm_back.4
  309.9 6.3 %collective-permute-done.101.refs_1_ = bf16[128,1024]{1,0:T(8,128)(2,1)S(1)} collective-permute-done((bf16[128,1024]{1,0:T(8,128)(2,1)}, bf16[128,1024]{1,0:T(8,128)(2,1)S(1)}, u32[]{:S(2)}, u32[]{:S(2)}) %collective-permute-start.101) | collective-permute-done | bytes 262176 | tf_op jit(solution)/shard_map/ppermute | solution.py:73
  318.4 14.6 %attn_backward.2 = (bf16[512,1024]{1,0:T(8,128)(2,1)}, bf16[512,768]{1,0:T(8,128)(2,1)}, f32[1,768]{1,0:T(1,128)}, f32[4,256]{1,0:T(4,128)}, f32[128,1024]{1,0:T...) custom-call(bf16[128,1024]{1,0:T(8,128)(2,1)} %get-tuple-element.415.refs_0_, ...), custom_call_target="tpu_custom_call" | custom-call | flops 1409286144 | bytes 10507264 | tf_op jit(solution)/shard_map/attn_backward/pallas_call | solution.py:60
  345.8 3.2 norm_back.5
  357.9 4.5 attn_weight_grads.3.refs_0_.refs_1_
  378.6 7.5 %mlp_backward.3 = (bf16[512,1024]{1,0:T(8,128)(2,1)}, bf16[512,1024]{1,0:T(8,128)(2,1)}, f32[1,1024]{1,0:T(1,128)}, f32[128,1024]{1,0:T(8,128)}, f32[128,1024]{1...) custom-call(bf16[128,1024]{1,0:T(8,128)(2,1)} %get-tuple-element.425.refs_0_, ...), custom_call_target="tpu_custom_call" | custom-call | flops 2147483648 | bytes 9965568 | tf_op jit(solution)/shard_map/mlp_backward/pallas_call | solution.py:60
  404.0 3.8 convolution_convert_fusion.3
  407.9 3.8 collective-permute-done.112.refs_6_
  412.4 3.1 norm_back.6
  428.5 4.7 collective-permute-done.143.refs_3_
  444.1 16.1 %attn_backward.3 = (bf16[512,1024]{1,0:T(8,128)(2,1)}, bf16[512,768]{1,0:T(8,128)(2,1)}, f32[1,768]{1,0:T(1,128)}, f32[4,256]{1,0:T(4,128)}, f32[128,1024]{1,0:T...) custom-call(bf16[128,1024]{1,0:T(8,128)(2,1)} %get-tuple-element.432.refs_0_, ...), custom_call_target="tpu_custom_call" | custom-call | flops 1241513984 | bytes 10507264 | tf_op jit(solution)/shard_map/attn_backward/pallas_call | solution.py:60
  466.4 4.5 attn_weight_grads.2.refs_0_.refs_1_
  476.2 2.9 ring_add.51
  481.4 3.5 collective-permute-done.120.refs_3_
  514.3 2.9 ring_add.52
  548.2 2.9 ring_add.63
  579.7 2.9 ring_add.55
  587.1 3.2 collective-permute-done.132.refs_3_
  603.9 4.5 collective-permute-start.169
  613.8 3.5 place_grads.1
  (993 shorter events, 370.4 us)
Async XLA Ops:
  30.3 19.0 %collective-permute-start.3 = (bf16[8,960]{1,0:T(8,128)(2,1)S(1)}, bf16[8,960]{1,0:T(8,128)(2,1)S(1)}, u32[]{:S(2)}, u32[]{:S(2)}) collective-permute-start(bf16[8,960]{1,0:T(8,128)(2,1)S(1)} %pad_maximum_fusion.8), channel_id=1, source_target_pairs={{0,8},{8,0},{16,24},{24,16},{1,9},{9,1},{17,25},{25,17},{2,10},{10... | collective-permute-start | bytes 46088 | tf_op jit(solution)/shard_map/ppermute | solution.py:282
  40.9 15.0 %collective-permute-start.36 = (bf16[128,1024]{1,0:T(8,128)(2,1)S(1)}, bf16[128,1024]{1,0:T(8,128)(2,1)S(1)}, u32[]{:S(2)}, u32[]{:S(2)}) collective-permute-start(bf16[128,1024]{1,0:T(8,128)(2,1)S(1)} %get-tuple-element.609.refs_8_), channel_id=1, source_target_pairs={{4,0},{12,4},{20,12},{28,20},{24,28},{16,24},{8,16},{0,8},{5,1},{1... | collective-permute-start | bytes 786440 | tf_op jit(solution)/shard_map/ppermute | solution.py:197
  55.9 16.9 %collective-permute-start.26 = (s32[1,128]{1,0:T(1,128)S(1)}, s32[1,128]{1,0:T(1,128)S(1)}, u32[]{:S(2)}, u32[]{:S(2)}) collective-permute-start(s32[1,128]{1,0:T(1,128)S(1)} %bitcast.144), channel_id=1, source_target_pairs={{0,1},{1,0},{2,3},{3,2},{4,5},{5,4},{6,7},{7,6},{8,9},{9,8},{10,11... | collective-permute-start | bytes 1544 | tf_op jit(solution)/shard_map/ppermute | solution.py:73
  75.4 19.2 %collective-permute-start.6 = (bf16[128,1024]{1,0:T(8,128)(2,1)}, bf16[128,1024]{1,0:T(8,128)(2,1)S(1)}, u32[]{:S(2)}, u32[]{:S(2)}) collective-permute-start(bf16[128,1024]{1,0:T(8,128)(2,1)} %first_norm.1.refs_0_), channel_id=1, source_target_pairs={{0,2},{2,0},{1,3},{3,1},{4,6},{6,4},{5,7},{7,5},{8,10},{10,8},{9,1... | collective-permute-start | bytes 786440 | tf_op jit(solution)/shard_map/ppermute | solution.py:73
  76.0 18.6 %collective-permute-start.7 = (bf16[128,1024]{1,0:T(8,128)(2,1)S(1)}, bf16[128,1024]{1,0:T(8,128)(2,1)}, u32[]{:S(2)}, u32[]{:S(2)}) collective-permute-start(bf16[128,1024]{1,0:T(8,128)(2,1)S(1)} %collective-permute-done.5.refs_1_), channel_id=1, source_target_pairs={{0,2},{2,0},{1,3},{3,1},{4,6},{6,4},{5,7},{7,5},{8,10},{10,8},{9,1... | collective-permute-start | bytes 786440 | tf_op jit(solution)/shard_map/ppermute | solution.py:73
  88.8 21.2 %collective-permute-start.41 = (bf16[128,1024]{1,0:T(8,128)(2,1)S(1)}, bf16[128,1024]{1,0:T(8,128)(2,1)S(1)}, u32[]{:S(2)}, u32[]{:S(2)}) collective-permute-start(bf16[128,1024]{1,0:T(8,128)(2,1)S(1)} %collective-permute-done.39.refs_3_), channel_id=1, source_target_pairs={{4,12},{12,20},{20,28},{28,24},{24,16},{16,8},{8,0},{0,4},{5,13},{... | collective-permute-start | bytes 786440 | tf_op jit(solution)/shard_map/ppermute | solution.py:197
  89.7 20.3 %collective-permute-start.42 = (bf16[128,1024]{1,0:T(8,128)(2,1)S(1)}, bf16[128,1024]{1,0:T(8,128)(2,1)S(1)}, u32[]{:S(2)}, u32[]{:S(2)}) collective-permute-start(bf16[128,1024]{1,0:T(8,128)(2,1)S(1)} %collective-permute-done.40.refs_11_), channel_id=1, source_target_pairs={{4,0},{12,4},{20,12},{28,20},{24,28},{16,24},{8,16},{0,8},{5,1},{1... | collective-permute-start | bytes 786440 | tf_op jit(solution)/shard_map/ppermute | solution.py:197
  109.5 19.1 %collective-permute-start.29 = (bf16[128,1024]{1,0:T(8,128)(2,1)}, bf16[128,1024]{1,0:T(8,128)(2,1)S(1)}, u32[]{:S(2)}, u32[]{:S(2)}) collective-permute-start(bf16[128,1024]{1,0:T(8,128)(2,1)} %get-tuple-element.331), channel_id=1, source_target_pairs={{0,2},{2,0},{1,3},{3,1},{4,6},{6,4},{5,7},{7,5},{8,10},{10,8},{9,1... | collective-permute-start | bytes 786440 | tf_op jit(solution)/shard_map/ppermute | solution.py:73
  110.0 16.0 %collective-permute-start.43 = (bf16[128,1024]{1,0:T(8,128)(2,1)S(1)}, bf16[128,1024]{1,0:T(8,128)(2,1)S(1)}, u32[]{:S(2)}, u32[]{:S(2)}) collective-permute-start(bf16[128,1024]{1,0:T(8,128)(2,1)S(1)} %collective-permute-done.41.refs_4_), channel_id=1, source_target_pairs={{4,12},{12,20},{20,28},{28,24},{24,16},{16,8},{8,0},{0,4},{5,13},{... | collective-permute-start | bytes 786440 | tf_op jit(solution)/shard_map/ppermute | solution.py:197
  110.8 15.2 %collective-permute-start.44 = (bf16[128,1024]{1,0:T(8,128)(2,1)S(1)}, bf16[128,1024]{1,0:T(8,128)(2,1)S(1)}, u32[]{:S(2)}, u32[]{:S(2)}) collective-permute-start(bf16[128,1024]{1,0:T(8,128)(2,1)S(1)} %collective-permute-done.42.refs_12_), channel_id=1, source_target_pairs={{4,0},{12,4},{20,12},{28,20},{24,28},{16,24},{8,16},{0,8},{5,1},{1... | collective-permute-start | bytes 786440 | tf_op jit(solution)/shard_map/ppermute | solution.py:197
  113.4 15.3 %collective-permute-start.31 = (bf16[128,1024]{1,0:T(8,128)(2,1)S(1)}, bf16[128,1024]{1,0:T(8,128)(2,1)S(1)}, u32[]{:S(2)}, u32[]{:S(2)}) collective-permute-start(bf16[128,1024]{1,0:T(8,128)(2,1)S(1)} %add_convert_fusion.7), channel_id=1, source_target_pairs={{0,1},{1,0},{2,3},{3,2},{4,5},{5,4},{6,7},{7,6},{8,9},{9,8},{10,11... | collective-permute-start | bytes 786440 | tf_op jit(solution)/shard_map/ppermute | solution.py:73
  134.9 22.1 %collective-permute-start.33 = (bf16[128,1024]{1,0:T(8,128)(2,1)}, bf16[128,1024]{1,0:T(8,128)(2,1)S(1)}, u32[]{:S(2)}, u32[]{:S(2)}) collective-permute-start(bf16[128,1024]{1,0:T(8,128)(2,1)} %get-tuple-element.335.refs_0_), channel_id=1, source_target_pairs={{0,2},{2,0},{1,3},{3,1},{4,6},{6,4},{5,7},{7,5},{8,10},{10,8},{9,1... | collective-permute-start | bytes 786440 | tf_op jit(solution)/shard_map/ppermute | solution.py:73
  135.8 15.3 %collective-permute-start.47 = (bf16[128,1024]{1,0:T(8,128)(2,1)S(1)}, bf16[128,1024]{1,0:T(8,128)(2,1)S(1)}, u32[]{:S(2)}, u32[]{:S(2)}) collective-permute-start(bf16[128,1024]{1,0:T(8,128)(2,1)S(1)} %collective-permute-done.45.refs_6_), channel_id=1, source_target_pairs={{4,12},{12,20},{20,28},{28,24},{24,16},{16,8},{8,0},{0,4},{5,13},{... | collective-permute-start | bytes 786440 | tf_op jit(solution)/shard_map/ppermute | solution.py:197
  140.6 16.4 %collective-permute-start.34 = (bf16[128,1024]{1,0:T(8,128)(2,1)}, bf16[128,1024]{1,0:T(8,128)(2,1)S(1)}, u32[]{:S(2)}, u32[]{:S(2)}) collective-permute-start(bf16[128,1024]{1,0:T(8,128)(2,1)} %collective-permute-done.32.refs_1_), channel_id=1, source_target_pairs={{0,2},{2,0},{1,3},{3,1},{4,6},{6,4},{5,7},{7,5},{8,10},{10,8},{9,1... | collective-permute-start | bytes 786440 | tf_op jit(solution)/shard_map/ppermute | solution.py:73
  177.0 15.1 %collective-permute-start.80 = (bf16[128,1024]{1,0:T(8,128)(2,1)S(1)}, bf16[128,1024]{1,0:T(8,128)(2,1)S(1)}, u32[]{:S(2)}, u32[]{:S(2)}) collective-permute-start(bf16[128,1024]{1,0:T(8,128)(2,1)S(1)} %collective-permute-done.78.refs_1_), channel_id=1, source_target_pairs={{4,12},{12,20},{20,28},{28,24},{24,16},{16,8},{8,0},{0,4},{5,13},{... | collective-permute-start | bytes 786440 | tf_op jit(solution)/shard_map/ppermute | solution.py:197
  205.5 17.6 %collective-permute-start.84 = (bf16[128,1024]{1,0:T(8,128)(2,1)S(1)}, bf16[128,1024]{1,0:T(8,128)(2,1)S(1)}, u32[]{:S(2)}, u32[]{:S(2)}) collective-permute-start(bf16[128,1024]{1,0:T(8,128)(2,1)S(1)} %collective-permute-done.82.refs_3_), channel_id=1, source_target_pairs={{4,12},{12,20},{20,28},{28,24},{24,16},{16,8},{8,0},{0,4},{5,13},{... | collective-permute-start | bytes 786440 | tf_op jit(solution)/shard_map/ppermute | solution.py:197
  357.4 18.9 %collective-permute-start.108 = (bf16[128,1024]{1,0:T(8,128)(2,1)S(1)}, bf16[128,1024]{1,0:T(8,128)(2,1)S(1)}, u32[]{:S(2)}, u32[]{:S(2)}) collective-permute-start(bf16[128,1024]{1,0:T(8,128)(2,1)S(1)} %copy-done.186), channel_id=1, source_target_pairs={{0,2},{2,0},{1,3},{3,1},{4,6},{6,4},{5,7},{7,5},{8,10},{10,8},{9,1... | collective-permute-start | bytes 786440 | tf_op jit(solution)/shard_map/ppermute | solution.py:73
  357.4 20.5 %collective-permute-start.109 = (bf16[128,1024]{1,0:T(8,128)(2,1)S(1)}, bf16[128,1024]{1,0:T(8,128)(2,1)S(1)}, u32[]{:S(2)}, u32[]{:S(2)}) collective-permute-start(bf16[128,1024]{1,0:T(8,128)(2,1)S(1)} %collective-permute-done.107.refs_1_), channel_id=1, source_target_pairs={{0,2},{2,0},{1,3},{3,1},{4,6},{6,4},{5,7},{7,5},{8,10},{10,8},{9,1... | collective-permute-start | bytes 786440 | tf_op jit(solution)/shard_map/ppermute | solution.py:73
  370.3 21.7 %collective-permute-start.174 = (bf16[128,1024]{1,0:T(8,128)(2,1)}, bf16[128,1024]{1,0:T(8,128)(2,1)S(1)}, u32[]{:S(2)}, u32[]{:S(2)}) collective-permute-start(bf16[128,1024]{1,0:T(8,128)(2,1)} %get-tuple-element.566), channel_id=1, source_target_pairs={{4,12},{12,20},{20,28},{28,24},{24,16},{16,8},{8,0},{0,4},{5,13},{... | collective-permute-start | bytes 786440 | tf_op jit(solution)/shard_map/ppermute | solution.py:197
  371.1 20.9 %collective-permute-start.175 = (bf16[128,1024]{1,0:T(8,128)(2,1)}, bf16[128,1024]{1,0:T(8,128)(2,1)S(1)}, u32[]{:S(2)}, u32[]{:S(2)}) collective-permute-start(bf16[128,1024]{1,0:T(8,128)(2,1)} %get-tuple-element.567), channel_id=1, source_target_pairs={{4,0},{12,4},{20,12},{28,20},{24,28},{16,24},{8,16},{0,8},{5,1},{1... | collective-permute-start | bytes 786440 | tf_op jit(solution)/shard_map/ppermute | solution.py:197
  386.1 16.7 %collective-permute-start.111 = (bf16[128,1024]{1,0:T(8,128)(2,1)}, bf16[128,1024]{1,0:T(8,128)(2,1)S(1)}, u32[]{:S(2)}, u32[]{:S(2)}) collective-permute-start(bf16[128,1024]{1,0:T(8,128)(2,1)} %get-tuple-element.430), channel_id=1, source_target_pairs={{0,2},{2,0},{1,3},{3,1},{4,6},{6,4},{5,7},{7,5},{8,10},{10,8},{9,1... | collective-permute-start | bytes 786440 | tf_op jit(solution)/shard_map/ppermute | solution.py:73
  396.1 26.6 %collective-permute-start.176 = (bf16[128,1024]{1,0:T(8,128)(2,1)}, bf16[128,1024]{1,0:T(8,128)(2,1)S(1)}, u32[]{:S(2)}, u32[]{:S(2)}) collective-permute-start(bf16[128,1024]{1,0:T(8,128)(2,1)} %get-tuple-element.570), channel_id=1, source_target_pairs={{4,12},{12,20},{20,28},{28,24},{24,16},{16,8},{8,0},{0,4},{5,13},{... | collective-permute-start | bytes 786440 | tf_op jit(solution)/shard_map/ppermute | solution.py:197
  396.9 27.0 %collective-permute-start.177 = (bf16[128,1024]{1,0:T(8,128)(2,1)}, bf16[128,1024]{1,0:T(8,128)(2,1)S(1)}, u32[]{:S(2)}, u32[]{:S(2)}) collective-permute-start(bf16[128,1024]{1,0:T(8,128)(2,1)} %get-tuple-element.571), channel_id=1, source_target_pairs={{4,0},{12,4},{20,12},{28,20},{24,28},{16,24},{8,16},{0,8},{5,1},{1... | collective-permute-start | bytes 786440 | tf_op jit(solution)/shard_map/ppermute | solution.py:197
  402.0 22.5 %collective-permute-start.142 = (bf16[64,1024]{1,0:T(8,128)(2,1)}, bf16[64,1024]{1,0:T(8,128)(2,1)S(1)}, u32[]{:S(2)}, u32[]{:S(2)}) collective-permute-start(bf16[64,1024]{1,0:T(8,128)(2,1)} %get-tuple-element.495), channel_id=1, source_target_pairs={{4,12},{12,20},{20,28},{28,24},{24,16},{16,8},{8,0},{0,4},{5,13},{... | collective-permute-start | bytes 393224 | tf_op jit(solution)/shard_map/ppermute | solution.py:197
  422.8 15.0 %collective-permute-start.154 = (bf16[128,1024]{1,0:T(8,128)(2,1)}, bf16[128,1024]{1,0:T(8,128)(2,1)S(1)}, u32[]{:S(2)}, u32[]{:S(2)}) collective-permute-start(bf16[128,1024]{1,0:T(8,128)(2,1)} %get-tuple-element.522), channel_id=1, source_target_pairs={{4,0},{12,4},{20,12},{28,20},{24,28},{16,24},{8,16},{0,8},{5,1},{1... | collective-permute-start | bytes 786440 | tf_op jit(solution)/shard_map/ppermute | solution.py:197
  424.0 18.3 %collective-permute-start.114 = (bf16[128,1024]{1,0:T(8,128)(2,1)S(1)}, bf16[128,1024]{1,0:T(8,128)(2,1)S(1)}, u32[]{:S(2)}, u32[]{:S(2)}) collective-permute-start(bf16[128,1024]{1,0:T(8,128)(2,1)S(1)} %copy-done.40), channel_id=1, source_target_pairs={{0,2},{2,0},{1,3},{3,1},{4,6},{6,4},{5,7},{7,5},{8,10},{10,8},{9,1... | collective-permute-start | bytes 786440 | tf_op jit(solution)/shard_map/ppermute | solution.py:73
  424.1 19.3 %collective-permute-start.115 = (bf16[128,1024]{1,0:T(8,128)(2,1)S(1)}, bf16[128,1024]{1,0:T(8,128)(2,1)S(1)}, u32[]{:S(2)}, u32[]{:S(2)}) collective-permute-start(bf16[128,1024]{1,0:T(8,128)(2,1)S(1)} %collective-permute-done.113.refs_1_), channel_id=1, source_target_pairs={{0,2},{2,0},{1,3},{3,1},{4,6},{6,4},{5,7},{7,5},{8,10},{10,8},{9,1... | collective-permute-start | bytes 786440 | tf_op jit(solution)/shard_map/ppermute | solution.py:73
  433.2 60.3 %collective-permute-start.178 = (bf16[128,1024]{1,0:T(8,128)(2,1)}, bf16[128,1024]{1,0:T(8,128)(2,1)S(1)}, u32[]{:S(2)}, u32[]{:S(2)}) collective-permute-start(bf16[128,1024]{1,0:T(8,128)(2,1)} %get-tuple-element.574), channel_id=1, source_target_pairs={{4,12},{12,20},{20,28},{28,24},{24,16},{16,8},{8,0},{0,4},{5,13},{... | collective-permute-start | bytes 786440 | tf_op jit(solution)/shard_map/ppermute | solution.py:197
  436.7 58.1 %collective-permute-start.179 = (bf16[128,1024]{1,0:T(8,128)(2,1)S(1)}, bf16[128,1024]{1,0:T(8,128)(2,1)S(1)}, u32[]{:S(2)}, u32[]{:S(2)}) collective-permute-start(bf16[128,1024]{1,0:T(8,128)(2,1)S(1)} %copy-done.179), channel_id=1, source_target_pairs={{4,0},{12,4},{20,12},{28,20},{24,28},{16,24},{8,16},{0,8},{5,1},{1... | collective-permute-start | bytes 786440 | tf_op jit(solution)/shard_map/ppermute | solution.py:197
  441.3 19.0 %collective-permute-start.155 = (bf16[128,1024]{1,0:T(8,128)(2,1)}, bf16[128,1024]{1,0:T(8,128)(2,1)S(1)}, u32[]{:S(2)}, u32[]{:S(2)}) collective-permute-start(bf16[128,1024]{1,0:T(8,128)(2,1)} %get-tuple-element.525), channel_id=1, source_target_pairs={{4,12},{12,20},{20,28},{28,24},{24,16},{16,8},{8,0},{0,4},{5,13},{... | collective-permute-start | bytes 786440 | tf_op jit(solution)/shard_map/ppermute | solution.py:197
  442.3 18.0 %collective-permute-start.156 = (bf16[128,1024]{1,0:T(8,128)(2,1)}, bf16[128,1024]{1,0:T(8,128)(2,1)S(1)}, u32[]{:S(2)}, u32[]{:S(2)}) collective-permute-start(bf16[128,1024]{1,0:T(8,128)(2,1)} %get-tuple-element.526), channel_id=1, source_target_pairs={{4,0},{12,4},{20,12},{28,20},{24,28},{16,24},{8,16},{0,8},{5,1},{1... | collective-permute-start | bytes 786440 | tf_op jit(solution)/shard_map/ppermute | solution.py:197
  473.5 15.0 %collective-permute-start.116 = (bf16[128,1024]{1,0:T(8,128)(2,1)S(1)}, bf16[128,1024]{1,0:T(8,128)(2,1)S(1)}, u32[]{:S(2)}, u32[]{:S(2)}) collective-permute-start(bf16[128,1024]{1,0:T(8,128)(2,1)S(1)} %copy-done.184), channel_id=1, source_target_pairs={{0,2},{2,0},{1,3},{3,1},{4,6},{6,4},{5,7},{7,5},{8,10},{10,8},{9,1... | collective-permute-start | bytes 786440 | tf_op jit(solution)/shard_map/ppermute | solution.py:73
  474.7 15.1 %collective-permute-start.118 = (bf16[128,1024]{1,0:T(8,128)(2,1)S(1)}, bf16[128,1024]{1,0:T(8,128)(2,1)S(1)}, u32[]{:S(2)}, u32[]{:S(2)}) collective-permute-start(bf16[128,1024]{1,0:T(8,128)(2,1)S(1)} %add_convert_fusion), channel_id=1, source_target_pairs={{0,1},{1,0},{2,3},{3,2},{4,5},{5,4},{6,7},{7,6},{8,9},{9,8},{10,11... | collective-permute-start | bytes 786440 | tf_op jit(solution)/shard_map/ppermute | solution.py:73
  484.9 18.4 %collective-permute-start.144 = (bf16[64,1024]{1,0:T(8,128)(2,1)}, bf16[64,1024]{1,0:T(8,128)(2,1)S(1)}, u32[]{:S(2)}, u32[]{:S(2)}) collective-permute-start(bf16[64,1024]{1,0:T(8,128)(2,1)} %get-tuple-element.499), channel_id=1, source_target_pairs={{4,12},{12,20},{20,28},{28,24},{24,16},{16,8},{8,0},{0,4},{5,13},{... | collective-permute-start | bytes 393224 | tf_op jit(solution)/shard_map/ppermute | solution.py:197
  488.5 21.2 %collective-permute-start.159 = (bf16[128,1024]{1,0:T(8,128)(2,1)S(1)}, bf16[128,1024]{1,0:T(8,128)(2,1)S(1)}, u32[]{:S(2)}, u32[]{:S(2)}) collective-permute-start(bf16[128,1024]{1,0:T(8,128)(2,1)S(1)} %copy-done.183), channel_id=1, source_target_pairs={{4,12},{12,20},{20,28},{28,24},{24,16},{16,8},{8,0},{0,4},{5,13},{... | collective-permute-start | bytes 786440 | tf_op jit(solution)/shard_map/ppermute | solution.py:197
  489.8 21.2 %collective-permute-start.160 = (bf16[128,1024]{1,0:T(8,128)(2,1)S(1)}, bf16[128,1024]{1,0:T(8,128)(2,1)S(1)}, u32[]{:S(2)}, u32[]{:S(2)}) collective-permute-start(bf16[128,1024]{1,0:T(8,128)(2,1)S(1)} %copy-done.182), channel_id=1, source_target_pairs={{4,0},{12,4},{20,12},{28,20},{24,28},{16,24},{8,16},{0,8},{5,1},{1... | collective-permute-start | bytes 786440 | tf_op jit(solution)/shard_map/ppermute | solution.py:197
  505.4 16.4 %collective-permute-start.189 = (f32[23,1024]{1,0:T(8,128)S(1)}, f32[23,1024]{1,0:T(8,128)S(1)}, u32[]{:S(2)}, u32[]{:S(2)}) collective-permute-start(f32[23,1024]{1,0:T(8,128)S(1)} %add.120), channel_id=1, source_target_pairs={{0,1},{1,0},{2,3},{3,2},{4,5},{5,4},{6,7},{7,6},{8,9},{9,8},{10,11... | collective-permute-start | bytes 282632 | tf_op jit(solution)/shard_map/ppermute | solution.py:73
  526.2 16.5 %collective-permute-start.190 = (f32[16384]{0:T(1024)S(1)}, f32[16384]{0:T(1024)S(1)}, u32[]{:S(2)}, u32[]{:S(2)}) collective-permute-start(f32[16384]{0:T(1024)S(1)} %pad_maximum_fusion.4), channel_id=1, source_target_pairs={{0,16},{8,24},{16,0},{24,8},{1,17},{9,25},{17,1},{25,9},{2,18},{10... | collective-permute-start | bytes 196616 | tf_op jit(solution)/shard_map/ppermute | solution.py:300
  545.0 18.4 %collective-permute-start.127 = (bf16[64,1024]{1,0:T(8,128)(2,1)}, bf16[64,1024]{1,0:T(8,128)(2,1)S(1)}, u32[]{:S(2)}, u32[]{:S(2)}) collective-permute-start(bf16[64,1024]{1,0:T(8,128)(2,1)} %get-tuple-element.461), channel_id=1, source_target_pairs={{4,12},{12,20},{20,28},{28,24},{24,16},{16,8},{8,0},{0,4},{5,13},{... | collective-permute-start | bytes 393224 | tf_op jit(solution)/shard_map/ppermute | solution.py:197
  546.4 17.0 %collective-permute-start.128 = (bf16[64,1024]{1,0:T(8,128)(2,1)}, bf16[64,1024]{1,0:T(8,128)(2,1)S(1)}, u32[]{:S(2)}, u32[]{:S(2)}) collective-permute-start(bf16[64,1024]{1,0:T(8,128)(2,1)} %get-tuple-element.462), channel_id=1, source_target_pairs={{4,0},{12,4},{20,12},{28,20},{24,28},{16,24},{8,16},{0,8},{5,1},{1... | collective-permute-start | bytes 393224 | tf_op jit(solution)/shard_map/ppermute | solution.py:197
  547.1 22.2 %collective-permute-start.191 = (f32[11776]{0:T(1024)S(1)}, f32[11776]{0:T(1024)S(1)}, u32[]{:S(2)}, u32[]{:S(2)}) collective-permute-start(f32[11776]{0:T(1024)S(1)} %pad_maximum_fusion.5), channel_id=1, source_target_pairs={{0,8},{8,0},{16,24},{24,16},{1,9},{9,1},{17,25},{25,17},{2,10},{10... | collective-permute-start | bytes 141320 | tf_op jit(solution)/shard_map/ppermute | solution.py:300
  561.4 16.4 %collective-permute-start.165 = (bf16[128,1024]{1,0:T(8,128)(2,1)}, bf16[128,1024]{1,0:T(8,128)(2,1)S(1)}, u32[]{:S(2)}, u32[]{:S(2)}) collective-permute-start(bf16[128,1024]{1,0:T(8,128)(2,1)} %get-tuple-element.545), channel_id=1, source_target_pairs={{4,12},{12,20},{20,28},{28,24},{24,16},{16,8},{8,0},{0,4},{5,13},{... | collective-permute-start | bytes 786440 | tf_op jit(solution)/shard_map/ppermute | solution.py:197
  562.7 16.2 %collective-permute-start.166 = (bf16[128,1024]{1,0:T(8,128)(2,1)}, bf16[128,1024]{1,0:T(8,128)(2,1)S(1)}, u32[]{:S(2)}, u32[]{:S(2)}) collective-permute-start(bf16[128,1024]{1,0:T(8,128)(2,1)} %get-tuple-element.546), channel_id=1, source_target_pairs={{4,0},{12,4},{20,12},{28,20},{24,28},{16,24},{8,16},{0,8},{5,1},{1... | collective-permute-start | bytes 786440 | tf_op jit(solution)/shard_map/ppermute | solution.py:197
  569.4 15.0 %collective-permute-start.192 = (f32[9472]{0:T(1024)S(1)}, f32[9472]{0:T(1024)S(1)}, u32[]{:S(2)}, u32[]{:S(2)}) collective-permute-start(f32[9472]{0:T(1024)S(1)} %pad_maximum_fusion.6), channel_id=1, source_target_pairs={{0,4},{4,0},{1,5},{5,1},{2,6},{6,2},{3,7},{7,3},{8,12},{12,8},{9,1... | collective-permute-start | bytes 113672 | tf_op jit(solution)/shard_map/ppermute | solution.py:300
  574.1 21.4 %collective-permute-start.184 = (bf16[32,1024]{1,0:T(8,128)(2,1)S(1)}, bf16[32,1024]{1,0:T(8,128)(2,1)S(1)}, u32[]{:S(2)}, u32[]{:S(2)}) collective-permute-start(bf16[32,1024]{1,0:T(8,128)(2,1)S(1)} %copy-done.214), channel_id=1, source_target_pairs={{0,1},{1,0},{2,3},{3,2},{4,5},{5,4},{6,7},{7,6},{8,9},{9,8},{10,11... | collective-permute-start | bytes 196616 | tf_op jit(solution)/shard_map/ppermute | solution.py:73
  574.6 21.1 %collective-permute-start.185 = (bf16[32,1024]{1,0:T(8,128)(2,1)S(1)}, bf16[32,1024]{1,0:T(8,128)(2,1)S(1)}, u32[]{:S(2)}, u32[]{:S(2)}) collective-permute-start(bf16[32,1024]{1,0:T(8,128)(2,1)S(1)} %copy-done.213), channel_id=1, source_target_pairs={{0,2},{2,0},{1,3},{3,1},{4,6},{6,4},{5,7},{7,5},{8,10},{10,8},{9,1... | collective-permute-start | bytes 196616 | tf_op jit(solution)/shard_map/ppermute | solution.py:73
  577.8 19.4 %collective-permute-start.186 = (bf16[32,1024]{1,0:T(8,128)(2,1)S(1)}, bf16[32,1024]{1,0:T(8,128)(2,1)S(1)}, u32[]{:S(2)}, u32[]{:S(2)}) collective-permute-start(bf16[32,1024]{1,0:T(8,128)(2,1)S(1)} %copy-done.212), channel_id=1, source_target_pairs={{0,3},{1,2},{2,1},{3,0},{4,7},{5,6},{6,5},{7,4},{8,11},{9,10},{10,... | collective-permute-start | bytes 196616 | tf_op jit(solution)/shard_map/ppermute | solution.py:77
  597.6 15.5 %collective-permute-start.187 = (bf16[2,32,1024]{2,1,0:T(8,128)(2,1)S(1)}, bf16[2,32,1024]{2,1,0:T(8,128)(2,1)S(1)}, u32[]{:S(2)}, u32[]{:S(2)}) collective-permute-start(bf16[2,32,1024]{2,1,0:T(8,128)(2,1)S(1)} %pad_maximum_fusion), channel_id=1, source_target_pairs={{0,0},{4,1},{8,2},{12,3},{16,4},{20,5},{24,6},{28,7},{1,8},{5,9},{... | collective-permute-start | bytes 393224 | tf_op jit(solution)/shard_map/ppermute | solution.py:906
  (373 other events, 3424.2 us)

commit v3 on v2

--- a/solution.py
+++ b/solution.py
@@ -17,7 +17,7 @@
 HIGHEST = lax.Precision.HIGHEST
 ROOT_HALF = 0.7071067811865476
 ROOT_TWO_PI = 0.3989422804014327
-VMEM_LIMIT = 56 * 1024 * 1024
+MEBI = 1024 * 1024
 OUT, GAIN, SHIFT, SCALE = 0, 4, 8, 12
 
 
@@ -50,20 +50,25 @@
     return jax.ShapeDtypeStruct(shape, dtype)
 
 
-def call(kernel, outs, args, name, flops=0, scratch=(), specs=None, scalars=0):
+def call(kernel, outs, args, name, flops=0, scratch=(), scalars=0, far_in=(), far_out=()):
+    hbm = pl.BlockSpec(memory_space=pltpu.HBM)
     vmem = pl.BlockSpec(memory_space=pltpu.VMEM)
     smem = pl.BlockSpec(memory_space=pltpu.SMEM)
-    specs = specs or {}
-    in_specs = [smem if i < scalars else specs.get(i, vmem) for i in range(len(args))]
+    in_specs = [smem if i < scalars else hbm if i in far_in else vmem for i in range(len(args))]
     bytes_all = sum(m.size * m.dtype.itemsize for m in args)
     bytes_all += sum(int(np.prod(s.shape)) * s.dtype.itemsize for s in outs)
+    sized = [s for s in scratch if hasattr(s, "shape") and s.memory_space == pltpu.VMEM]
+    held = sum(int(np.prod(s.shape)) * s.dtype.itemsize for s in sized)
+    limit = (held * 5 // 4 + bytes_all * 2 // 5 if flops else bytes_all) + (8 if flops else 3) * MEBI
+    args = [pltpu.with_memory_space_constraint(m, pltpu.HBM) if i in far_in else m for i, m in enumerate(args)]
+    outs = [pltpu.HBM(m.shape, m.dtype) if i in far_out else m for i, m in enumerate(outs)]
     return pl.pallas_call(
         kernel,
         out_shape=list(outs),
         in_specs=in_specs,
-        out_specs=[vmem] * len(outs),
+        out_specs=[hbm if i in far_out else vmem for i in range(len(outs))],
         scratch_shapes=list(scratch),
-        compiler_params=pltpu.CompilerParams(vmem_limit_bytes=VMEM_LIMIT),
+        compiler_params=pltpu.CompilerParams(vmem_limit_bytes=limit),
         cost_estimate=pl.CostEstimate(flops=flops, bytes_accessed=bytes_all, transcendentals=0),
         name=name,
     )(*args)
@@ -77,20 +82,22 @@
     return lax.ppermute(values, TEAM, [(0, 3), (1, 2), (2, 1), (3, 0)])
 
 
-def team_gather(values):
+def team_gather(values, work=None, pump=None):
     if lax.axis_size("frame") == 2:
         far = swap(values, "frame")
-        near = swap(values, "core")
+        near = swap(work(values) if work else values, "core")
+        far = pump(far) if pump else far
         return [values, far, near, swap(far, "core")]
     both = lax.all_gather(values, "frame", axis=0, tiled=True)
     return [both, swap(both, "core")]
 
 
-def team_sum(own, peer):
+def team_sum(own, peer, work=None):
     if lax.axis_size("frame") == 2:
         far = own[1] + swap(peer[1], "core").astype(WIDE)
         came = swap(far.astype(LOW), "frame")
-        return [own[0], swap(peer[0], "core"), came]
+        near = swap(work(peer[0]) if work else peer[0], "core")
+        return [own[0], near, came]
     total = own[0] + swap(peer[0], "core").astype(WIDE)
     return [lax.psum_scatter(total.astype(LOW), "frame", scatter_dimension=0, tiled=True).astype(WIDE)]
 
@@ -107,41 +114,109 @@
     return out.reshape((2 * frames,) + out.shape[2:])
 
 
-def split_weights(qkv, up, part, rest, me):
-    rows = qkv.shape[0]
-    width, hidden_all = qkv.shape[1] // 3, up.shape[1]
-    lanes = hidden_all // 4 // rest
-
-    def kernel(me_ref, qkv_ref, up_ref, *outs):
+SMALL_ROWS = 16
+
+
+def split_weights(depth, weights, vectors, part, rest, me):
+    qkv, up = weights
+    _, rows, width = qkv.shape
+    width //= 3
+    hidden = up.shape[2] // 4
+    lanes = hidden // rest
+    extra = SMALL_ROWS if vectors else 0
+
+    def kernel(me_ref, qkv_ref, up_ref, *refs):
+        small, outs = refs[: len(refs) - 4], refs[-4:]
         for away, out in enumerate(outs):
             member = jnp.bitwise_xor(me_ref[0], away)
             for s in range(3):
                 start = pl.multiple_of(s * width + member * part, 128)
-                out[:, s * part : (s + 1) * part] = qkv_ref[:, pl.ds(start, part)]
+                out[:rows, s * part : (s + 1) * part] = qkv_ref[depth, :, pl.ds(start, part)]
             for f in range(rest):
                 start = pl.multiple_of((f * 4 + member) * lanes, 128)
                 at = 3 * part + f * lanes
-                out[:, at : at + lanes] = up_ref[:, pl.ds(start, lanes)]
-
-    out = shape_of((rows, 3 * part + hidden_all // 4), qkv.dtype)
-    return call(kernel, [out] * 4, [me, qkv, up], "split_weights", scalars=1)
-
-
-def pack_weights(pieces, proj, part, me):
-    rows = proj.shape[0]
+                out[:rows, at : at + lanes] = up_ref[depth, :, pl.ds(start, lanes)]
+            if not vectors:
+                continue
+            out[rows:, :] = jnp.zeros((extra, out.shape[1]), LOW)
+            bias_qkv, bias_up, ids = small[:3]
+            for i, ref in enumerate(small[3:]):
+                for d in range(2):
+                    for j in range(2):
+                        at = rows + 4 * i + 2 * d + j
+                        out[at : at + 1, : ref.shape[2]] = ref[d, j : j + 1, :]
+            out[rows : rows + 2, 128 : 128 + bias_qkv.shape[1]] = bias_qkv[...]
+            out[rows : rows + 2, 256 : 256 + bias_up.shape[1]] = bias_up[...]
+            out[rows : rows + 1, 512 : 512 + ids.shape[1]] = ids[...].astype(WIDE).astype(LOW)
+
+    out = shape_of((rows + extra, 3 * part + hidden), qkv.dtype)
+    return call(kernel, [out] * 4, [me, qkv, up, *vectors], "split_weights", scalars=1)
+
+
+def pack_weights(pieces, proj, depth, part, me, vectors):
+    rows = proj.shape[1]
+    half = 2 * rows
     hidden = pieces[0].shape[1] - 3 * part
 
-    def kernel(me_ref, p0, p1, p2, p3, proj_ref, attn, up):
+    def kernel(me_ref, p0, p1, p2, p3, proj_ref, low_half, high_half, up, *refs):
+        attn, small = refs[-2], refs[-1]
         for away, ref in enumerate((p0, p1, p2, p3)):
             member = jnp.bitwise_xor(me_ref[0], away)
             start = pl.multiple_of(member * rows, rows)
-            attn[pl.ds(start, rows), : 3 * part] = ref[:, : 3 * part]
-            up[pl.ds(start, rows), :] = ref[:, 3 * part :]
+            attn[pl.ds(start, rows), : 3 * part] = ref[:rows, : 3 * part]
+            up[pl.ds(start, rows), :] = ref[:rows, 3 * part :]
+            if vectors:
+                small[member] = ref[rows:, :640]
         for j in range(4):
-            attn[j * rows : (j + 1) * rows, 3 * part :] = proj_ref[:, j * part : (j + 1) * part]
-
-    outs = [shape_of((4 * rows, 4 * part), LOW), shape_of((4 * rows, hidden), LOW)]
-    return call(kernel, outs, [me, *pieces, proj], "pack_weights", scalars=1)
+            attn[j * rows : (j + 1) * rows, 3 * part :] = proj_ref[depth, :, j * part : (j + 1) * part]
+        low_half[:half, :] = attn[:half, :]
+        high_half[...] = attn[half:, :]
+        if vectors:
+            low_half[half:, :] = jnp.zeros((SMALL_ROWS, 4 * part), LOW)
+            for at, start, size in ((0, 0, 32), (128, 128, 96), (512, 256, 128)):
+                joined = [small[m, :, start : start + size].astype(WIDE) for m in range(4)]
+                value = jnp.concatenate(joined, axis=1).astype(LOW)
+                low_half[half:, at : at + 4 * size] = value
+
+    extra = SMALL_ROWS if vectors else 0
+    outs = [
+        shape_of((half + extra, 4 * part), LOW),
+        shape_of((half, 4 * part), LOW),
+        shape_of((4 * rows, hidden), LOW),
+    ]
+    scratch = [pltpu.VMEM((4 * rows, 4 * part), LOW), pltpu.VMEM((4, SMALL_ROWS, 640), LOW)]
+    return call(kernel, outs, [me, *pieces, proj], "pack_weights", scratch=scratch, scalars=1)
+
+
+def unpack_vectors(pieces, rows, table, me):
+    rest, width = len(pieces), pieces[0].shape[1]
+    part = width // 4
+
+    def kernel(me_ref, table_ref, *refs):
+        vec, bias_qkv, bias_up, small, whole, semaphores = refs[rest:]
+        copies = []
+        for k in range(rest):
+            source = refs[k].at[pl.ds(rows, SMALL_ROWS), :]
+            copies.append(pltpu.make_async_copy(source, small.at[table_ref[0, k]], semaphores.at[k]))
+            copies[-1].start()
+        wait_all(copies)
+        for f in range(rest):
+            vec[:, f * 128 : (f + 1) * 128] = small[f, :, :128].astype(WIDE)
+            whole[:, f * 384 : (f + 1) * 384] = small[f, :, 128:512].astype(WIDE)
+            start = pl.multiple_of(512 + me_ref[0] * 128, 128)
+            bias_up[:, f * 128 : (f + 1) * 128] = small[f, :, pl.ds(start, 128)].astype(WIDE)
+        for s in range(3):
+            start = pl.multiple_of(s * width + me_ref[0] * part, 128)
+            bias_qkv[:, s * part : (s + 1) * part] = whole[:, pl.ds(start, part)]
+
+    outs = [shape_of((16, width), WIDE), shape_of((16, 3 * part), WIDE), shape_of((16, width), WIDE)]
+    scratch = [
+        pltpu.VMEM((rest, SMALL_ROWS, width), LOW),
+        pltpu.VMEM((16, 3 * width), WIDE),
+        pltpu.SemaphoreType.DMA((rest,)),
+    ]
+    args = [me, table, *pieces]
+    return call(kernel, outs, args, "unpack_vectors", 0, scratch, 2, far_in=range(2, 2 + rest))
 
 
 def spread(count, team):
@@ -202,76 +277,176 @@
     return lax.optimization_barrier((low_half, high_half))
 
 
-def ring_gather(low_half, high_half, table, joined):
+class RingGather:
+    def __init__(self, low_half, high_half, rest):
+        self.rest = rest
+        self.back, self.ahead = [low_half], [high_half]
+        self.came = (ring_shift(low_half, 1), ring_shift(high_half, -1))
+
+    def take(self, came):
+        self.back.append(came[0])
+        self.ahead.append(came[1])
+        self.came = None
+        if len(self.back) < self.rest:
+            self.came = (ring_shift(came[0], 1), ring_shift(came[1], -1))
+
+
+def steps(count, ring):
+    came = ()
+    for _ in range(count):
+        if ring.came is None:
+            break
+        came = tie(*ring.came)
+        ring.take(came)
+    return came
+
+
+class Pieces:
+    def __init__(self, rows, *lists):
+        self.rows = rows
+        self.lists = lists
+        self.args = [m for arrays, _, _ in lists for m in arrays]
+        self.count = len(self.args)
+        height = sum(min(arrays[0].shape[0], arrays[-1].shape[0], rows) for arrays, _, _ in lists)
+        self.shape = (len(lists[0][0]), height, self.args[0].shape[1])
+
+    def start(self, refs, table_ref, target, semaphores):
+        copies = []
+        for arrays, side, first in self.lists:
+            for k in range(len(arrays)):
+                source = refs[len(copies)].at[pl.ds(0, self.rows), :]
+                spot = target.at[table_ref[side, k], pl.ds(first, self.rows), :]
+                copies.append(pltpu.make_async_copy(source, spot, semaphores.at[len(copies)]))
+                copies[-1].start()
+        return copies
+
+
+class Whole:
+    count = 1
+
+    def __init__(self, array, first, rows):
+        self.first = first
+        self.args = [array]
+        self.shape = (array.shape[0], rows, array.shape[2])
+
+    def start(self, refs, table_ref, target, semaphores):
+        source = refs[0].at[:, pl.ds(self.first, self.shape[1]), :]
+        copy = pltpu.make_async_copy(source, target, semaphores.at[0])
+        copy.start()
+        return [copy]
+
+
+def wait_all(copies):
+    for copy in copies:
+        copy.wait()
+
+
+def tie(*values):
+    return lax.optimization_barrier(values)
+
+
+class RingSums:
+    def __init__(self, rest):
+        self.rest = rest
+        self.active = []
+        self.waiting = []
+        self.came = None
+        self.started = []
+
+    def work(self, value):
+        if self.came is not None:
+            self.came = tie(*self.came, value)[:2]
+        self.pump()
+        started, self.started = self.started, []
+        return tie(value, *started)[0] if started else value
+
+    def add(self, low_parts, high_parts, done):
+        self.waiting.append(
+            {"parts": (low_parts, high_parts), "rows": low_parts[0].shape[0], "done": done, "hop": 0}
+        )
+
+    def pump(self, *values):
+        if self.came is not None:
+            tied = tie(*values, *self.came)
+            values, self.came = tied[: len(values)], tied[len(values) :]
+        rings = self.active + self.waiting
+        self.waiting = []
+        if not rings:
+            return values if len(values) != 1 else values[0]
+        columns = rings[0]["parts"][0][0].shape[1]
+        moving, ended, plans, args = 0, [], [], []
+        start = 0
+        for ring in rings:
+            came_at = start if ring["hop"] else None
+            if ring["hop"]:
+                start += ring["rows"]
+            args += [ring["parts"][side][ring["hop"]] for side in range(2)]
+            ring["hop"] += 1
+            if ring["hop"] == self.rest:
+                plans.append((ring["rows"], came_at, None))
+                ended.append(ring)
+            else:
+                plans.append((ring["rows"], came_at, moving))
+                moving += ring["rows"]
+        came = list(self.came) if self.came is not None else []
+
+        size = sum(rows for rows, _, _ in plans)
+
+        def kernel(*refs):
+            came_refs = refs[: len(came)]
+            part_refs = refs[len(came) : len(came) + len(args)]
+            outs, local, semaphores = refs[len(came) + len(args) : -2], refs[-2], refs[-1]
+            copies, at = [], 0
+            for i, (rows, _, _) in enumerate(plans):
+                for side in range(2):
+                    spot = local.at[side, pl.ds(at, rows), :]
+                    copies.append(
+                        pltpu.make_async_copy(part_refs[2 * i + side], spot, semaphores.at[2 * i + side])
+                    )
+                    copies[-1].start()
+                at += rows
+            for copy in copies:
+                copy.wait()
+            final, at = (2 if moving else 0), 0
+            for rows, came_at, goes_to in plans:
+                for side in range(2):
+                    value = local[side, at : at + rows, :]
+                    if came_at is not None:
+                        other = came_refs[side][came_at : came_at + rows, :]
+                        value = value.astype(WIDE) + other.astype(WIDE)
+                    if goes_to is None:
+                        outs[final + side][...] = value.astype(WIDE)
+                    else:
+                        outs[side][goes_to : goes_to + rows, :] = value.astype(LOW)
+                if goes_to is None:
+                    final += 2
+                at += rows
+
+        outs = [shape_of((moving, columns), LOW)] * 2 if moving else []
+        for ring in ended:
+            outs += [shape_of((ring["rows"], columns), WIDE)] * 2
+        scratch = [pltpu.VMEM((2, size, columns), LOW), pltpu.SemaphoreType.DMA((len(args),))]
+        far_in = range(len(came), len(came) + len(args))
+        res = call(kernel, outs, came + args, "ring_add", 0, scratch, far_in=far_in)
+        at = 2 if moving else 0
+        for ring in ended:
+            ring["done"](res[at], res[at + 1])
+            at += 2
+        self.active = [ring for ring in rings if ring["hop"] < self.rest]
+        self.started += list(res[:2])
+        self.came = (ring_shift(res[0], 1), ring_shift(res[1], -1)) if moving else None
+        return values if len(values) != 1 else values[0]
+
+    def busy(self):
+        return bool(self.active or self.waiting)
+
+
+def hop_order(low_parts, high_parts, table):
     rest = table.shape[1]
-    rows, columns = low_half.shape
-    back, ahead = [low_half], [high_half]
-    for _ in range(rest - 1):
-        low_half, high_half = ring_step(low_half, high_half)
-        back.append(low_half)
-        ahead.append(high_half)
-
-    def kernel(table_ref, *refs):
-        outs = refs[2 * rest :]
-        for k in range(rest):
-            if joined:
-                outs[0][table_ref[0, k], :rows, :] = refs[k][...]
-                outs[0][table_ref[1, k], rows:, :] = refs[rest + k][...]
-            else:
-                outs[0][table_ref[0, k], :, :] = refs[k][...]
-                outs[1][table_ref[1, k], :, :] = refs[rest + k][...]
-
-    if joined:
-        outs = [shape_of((rest, 2 * rows, columns), LOW)]
-    else:
-        outs = [shape_of((rest, rows, columns), LOW)] * 2
-    return call(kernel, outs, [table, *back, *ahead], "assemble", scalars=1)
-
-
-def ring_sum(low_parts, high_parts, table, joined):
-    rest = table.shape[1]
-    _, rows, columns = low_parts.shape
-    rows = rows // 2 if joined else rows
-
-    def step(k, came):
-        last = k == rest
-        dtype = WIDE if last else LOW
-
-        def kernel(table_ref, *refs):
-            ins, outs = refs[: len(refs) - 2], refs[len(refs) - 2 :]
-            for i in range(2):
-                value = ins[i][0]
-                if came:
-                    value = (value.astype(WIDE) + ins[2 + i][...].astype(WIDE)).astype(dtype)
-                outs[i][...] = value
-
-        whole = pl.BlockSpec((rows, columns), lambda i, t: (0, 0))
-        grid_spec = pltpu.PrefetchScalarGridSpec(
-            num_scalar_prefetch=1,
-            grid=(1,),
-            in_specs=[
-                pl.BlockSpec((1, rows, columns), lambda i, t: (t[0, k % rest], 0, 0)),
-                pl.BlockSpec(
-                    (1, rows, columns), lambda i, t: (t[1, k % rest], 1 if joined else 0, 0)
-                ),
-            ]
-            + [whole] * len(came),
-            out_specs=[whole, whole],
-        )
-        return pl.pallas_call(
-            kernel,
-            grid_spec=grid_spec,
-            out_shape=[shape_of((rows, columns), dtype)] * 2,
-            cost_estimate=pl.CostEstimate(
-                flops=0, bytes_accessed=12 * rows * columns, transcendentals=0
-            ),
-            name="ring_add",
-        )(table, low_parts, high_parts, *came)
-
-    came = step(1, [])
-    for k in range(2, rest + 1):
-        came = step(k, ring_step(*came))
-    return came
+    return [
+        [lax.dynamic_index_in_dim(parts, table[side, k % rest], 0, keepdims=False) for k in range(1, rest + 1)]
+        for side, parts in ((0, low_parts), (1, high_parts))
+    ]
 
 
 def small_gather(values):
@@ -363,8 +538,22 @@
     return [shape_of((m.shape[0], width), WIDE if i < half else LOW) for i, m in enumerate(pieces)]
 
 
-def attn_forward(pieces, weights, bias, head_gain, head_shift, ids, head_size, frames, use_frame):
-    attn, proj, height, wide = weights
+def load_semaphores(sources):
+    return [pltpu.SemaphoreType.DMA((source.count,)) for source in sources]
+
+
+def start_loads(sources, table_ref, far_refs, targets, semaphores):
+    at, copies = 0, []
+    for source, target, semaphore in zip(sources, targets, semaphores):
+        copies.append(source.start(far_refs[at : at + source.count], table_ref, target, semaphore))
+        at += source.count
+    return copies
+
+
+def attn_forward(pieces, weights, bias, head_gain, head_shift, ids, head_size, frames, use_frame, vectors=None):
+    attn, proj, height, wide, table = weights
+    sources = [attn] if proj is None else [attn, proj]
+    far = [m for source in sources for m in source.args]
     rest, unit, _ = attn.shape
     width, part = rest * unit, head_gain.shape[-1]
     total = sum(m.shape[0] for m in pieces)
@@ -373,14 +562,29 @@
     lanes = min(128, part)
     per = lanes // head_size
     scale = head_size ** (-0.5)
-
-    def kernel(*refs):
+    more = 0 if vectors is None else 1
+
+    def kernel(table_ref, *refs):
+        far_refs, refs = refs[: len(far)], refs[len(far) :]
+        semaphores, refs = refs[-len(sources) :], refs[: -len(sources)]
+        targets, refs = refs[-len(sources) :], refs[: -len(sources)]
+        copies = start_loads(sources, table_ref, far_refs, targets, semaphores)
+        wq, wp = targets[0], targets[-1]
         piece_refs = refs[:count]
-        wq, wp, bias_ref, gain_ref, shift_ref, ids_col, ids_row = refs[count : count + 7]
-        first, raw, qkv, lse, flat = refs[count + 7 : count + 12]
-        outs = refs[count + 12 :]
-        join(piece_refs, first)
+        bias_ref, gain_ref, shift_ref, ids_col, ids_row = refs[count : count + 5]
+        first, raw, qkv, lse, flat = refs[count + 5 + more : count + 10 + more]
+        outs = refs[count + 10 + more :]
+        if more:
+            vec = refs[count + 5]
+            for start, stop, ref in spans(piece_refs):
+                unit_one, _ = normed(ref[...].astype(WIDE))
+                value = unit_one * row_of(vec, GAIN, 0, 0) + row_of(vec, SHIFT, 0, 0)
+                first[start:stop, :] = value.astype(LOW)
+        else:
+            join(piece_refs, first)
         matrix = head_means(part, head_size)
+        for group_copies in copies:
+            wait_all(group_copies)
         mixed = dot(first[...], flat_rows(wq, 0, unit, slice(0, 3 * part))) + bias_ref[...]
         raw[...] = mixed[:, : 2 * part]
         for i in range(2):
@@ -422,10 +626,15 @@
         shape_of((total, part // head_size), WIDE),
         shape_of((total, part), LOW),
     ] + part_shapes(pieces, width)
-    args = list(pieces) + [attn, proj, bias, head_gain, head_shift, ids.reshape(-1, 1), ids.reshape(1, -1)]
+    outs += [shape_of(source.shape, LOW) for source in sources]
+    args = [table] + far + list(pieces)
+    args += [bias, head_gain, head_shift, ids.reshape(-1, 1), ids.reshape(1, -1)]
+    args += [vectors] if more else []
     flops = 2 * total * (width * 4 * part + group * 2 * part)
-    res = call(kernel, outs, args, "attn_forward", flops)
-    return res[:5], res[5 : 5 + count // 2], res[5 + count // 2 :]
+    scratch = load_semaphores(sources)
+    res = call(kernel, outs, args, "attn_forward", flops, scratch, 1, far_in=range(1, 1 + len(far)))
+    weights = (res[5 + count], None if proj is None else res[6 + count], height, wide)
+    return res[:5], res[5 : 5 + count // 2], res[5 + count // 2 : 5 + count], weights
 
 
 def attn_backward(pieces, weights, head_gain, kept, ids, head_size, frames, use_frame):
@@ -439,13 +648,15 @@
     lanes = min(128, part)
     per = lanes // head_size
     scale = head_size ** (-0.5)
+    extra = 0 if proj is None else 1
 
     def kernel(*refs):
-        piece_refs = refs[:count]
-        wq, wp, gain_ref, raw_ref, qkv_ref, lse_ref, ids_col, ids_row = refs[count : count + 8]
-        joined, low_mixed, sums, head_sums = refs[count + 8 : count + 12]
-        outs = refs[count + 12 : count + 12 + count]
-        grad_out, grad_three = refs[count + 12 + count :]
+        piece_refs, wq, wp = refs[:count], refs[count], refs[count + extra]
+        refs = refs[extra + 1 :]
+        gain_ref, raw_ref, qkv_ref, lse_ref, ids_col, ids_row = refs[count : count + 6]
+        joined, low_mixed, sums, head_sums = refs[count + 6 : count + 10]
+        outs = refs[count + 10 : count + 10 + count]
+        grad_out, grad_three = refs[count + 10 + count :]
         join(piece_refs, joined)
         grad_flat = jnp.zeros((total, part), WIDE)
         for a in range(0, width, wide):
@@ -510,46 +721,91 @@
         shape_of((4, part), WIDE),
     ] + part_shapes(pieces, width)
     scratch = [pltpu.VMEM((total, part), LOW), pltpu.VMEM((total, 3 * part), WIDE)]
-    args = list(pieces) + [attn, proj, head_gain, raw, qkv, lse, ids.reshape(-1, 1), ids.reshape(1, -1)]
+    args = list(pieces) + [attn] + ([] if proj is None else [proj])
+    args += [head_gain, raw, qkv, lse, ids.reshape(-1, 1), ids.reshape(1, -1)]
     flops = 2 * total * (width * 4 * part + group * 5 * part)
     res = call(kernel, outs, args, "attn_backward", flops, scratch)
     return res[:4], res[4 : 4 + count // 2], res[4 + count // 2 :]
 
 
-def attn_weight_grads(first, low_mixed, flat, att_low, rest, height):
+def attn_weight_grads(first, low_mixed, flat, att_low, rest, height, table):
     width, part = first.shape[1], flat.shape[1]
     unit = width // rest
     wide = width * height // unit
 
-    def kernel(first_ref, mixed_ref, flat_ref, att_ref, out):
+    def kernel(table_ref, first_ref, mixed_ref, flat_ref, att_ref, *refs):
+        outs, packed, semaphores = refs[:-2], refs[-2], refs[-1]
         product = dot_tn(first_ref[...], mixed_ref[...]).astype(LOW)
-        out[:, :, : 3 * part] = product.reshape(rest, unit, 3 * part)
+        packed[:, :, : 3 * part] = product.reshape(rest, unit, 3 * part)
         product = dot_tn(flat_ref[...], att_ref[...]).astype(LOW)
         for j in range(unit // height):
             chunk = product[:, j * wide : (j + 1) * wide].reshape(rest, height, wide)
-            out[:, j * height : (j + 1) * height, 3 * part :] = chunk
+            packed[:, j * height : (j + 1) * height, 3 * part :] = chunk
+        copies = []
+        for k in range(rest):
+            for side in range(2):
+                source = packed.at[table_ref[side, (k + 1) % rest], pl.ds(side * (unit // 2), unit // 2), :]
+                at = side * rest + k
+                copies.append(pltpu.make_async_copy(source, outs[at], semaphores.at[at]))
+                copies[-1].start()
+        for copy in copies:
+            copy.wait()
 
     flops = 8 * first.shape[0] * width * part
-    out = shape_of((rest, unit, 4 * part), LOW)
-    return call(kernel, [out], [first, low_mixed, flat, att_low], "attn_weight_grads", flops)[0]
-
-
-def mlp_forward(pieces, weight_up, weight_down, bias):
-    rest, unit, hidden = weight_up.shape
+    outs = [shape_of((unit // 2, 4 * part), LOW)] * (2 * rest)
+    scratch = [pltpu.VMEM((rest, unit, 4 * part), LOW), pltpu.SemaphoreType.DMA((2 * rest,))]
+    args = [table, first, low_mixed, flat, att_low]
+    res = call(kernel, outs, args, "attn_weight_grads", flops, scratch, 1, far_out=range(len(outs)))
+    return res[:rest], res[rest:]
+
+
+def mlp_weight_grads(second, pre_low, act, branch_low, rest, table):
+    width, hidden = second.shape[1], act.shape[1]
+
+    def kernel(table_ref, second_ref, pre_ref, act_ref, branch_ref, *refs):
+        outs, packs, semaphores = refs[:-3], refs[-3:-1], refs[-1]
+        copies = []
+        for side, (left, right) in enumerate(((second_ref, pre_ref), (act_ref, branch_ref))):
+            pack = packs[side]
+            pack[...] = dot_tn(left[...], right[...]).astype(LOW).reshape(pack.shape)
+            for k in range(rest):
+                at = side * rest + k
+                source = pack.at[table_ref[side, (k + 1) % rest]]
+                copies.append(pltpu.make_async_copy(source, outs[at], semaphores.at[at]))
+                copies[-1].start()
+        for copy in copies:
+            copy.wait()
+
+    flops = 4 * second.shape[0] * width * hidden
+    up, down = (width // rest, hidden), (hidden // rest, width)
+    outs = [shape_of(up, LOW)] * rest + [shape_of(down, LOW)] * rest
+    scratch = [pltpu.VMEM((rest,) + m, LOW) for m in (up, down)] + [pltpu.SemaphoreType.DMA((2 * rest,))]
+    args = [table, second, pre_low, act, branch_low]
+    res = call(kernel, outs, args, "mlp_weight_grads", flops, scratch, 1, far_out=range(len(outs)))
+    return res[:rest], res[rest:]
+
+
+def mlp_forward(pieces, sources, table, bias):
+    rest, unit, hidden = sources[0].shape
     width = rest * unit
+    far = [m for source in sources for m in source.args]
     total = sum(m.shape[0] for m in pieces)
     count = len(pieces)
 
-    def kernel(*refs):
+    def kernel(table_ref, *refs):
+        far_refs, refs, (up, down), semaphores = refs[: len(far)], refs[len(far) : -4], refs[-4:-2], refs[-2:]
+        copies, more_copies = start_loads(sources, table_ref, far_refs, (up, down), semaphores)
         piece_refs = refs[:count]
-        up, down, bias_ref = refs[count : count + 3]
-        second, act, slope = refs[count + 3 : count + 6]
-        outs = refs[count + 6 :]
+        bias_ref = refs[count]
+        second, act, slope = refs[count + 1 : count + 4]
+        outs = refs[count + 4 :]
         join(piece_refs, second)
+        wait_all(copies)
         pre = dot(second[...], flat_rows(up, 0, unit, slice(None))) + bias_ref[...]
         below = 0.5 * (1.0 + lax.erf(pre * ROOT_HALF))
         act[...] = (pre * below).astype(LOW)
         slope[...] = (below + pre * (ROOT_TWO_PI * jnp.exp(-0.5 * pre * pre))).astype(LOW)
+        wait_all(more_copies)
         weight = flat_rows(down, 0, down.shape[1], slice(None))
         for start, stop, ref in spans(outs):
             ref[...] = dot(act[start:stop, :], weight).astype(ref.dtype)
@@ -559,9 +815,11 @@
         shape_of((total, hidden), LOW),
         shape_of((total, hidden), LOW),
     ] + part_shapes(pieces, width)
-    args = list(pieces) + [weight_up, weight_down, bias]
-    res = call(kernel, outs, args, "mlp_forward", 4 * total * width * hidden)
-    return res[:3], res[3 : 3 + count // 2], res[3 + count // 2 :]
+    outs += [shape_of(source.shape, LOW) for source in sources]
+    args = [table] + far + list(pieces) + [bias]
+    flops, far_in = 4 * total * width * hidden, range(1, 1 + len(far))
+    res = call(kernel, outs, args, "mlp_forward", flops, load_semaphores(sources), 1, far_in=far_in)
+    return res[:3], res[3 : 3 + count // 2], res[3 + count // 2 : 3 + count], res[3 + count :]
 
 
 def mlp_backward(pieces, weight_up, weight_down, slope):
@@ -604,14 +862,6 @@
 def row_of(vectors, kind, depth, which):
     at = kind + 2 * depth + which
     return vectors[at : at + 1, :]
-
-
-def first_norm(tokens, vectors):
-    def kernel(tokens_ref, vec, low):
-        unit, _ = normed(tokens_ref[...].astype(WIDE))
-        low[...] = (unit * row_of(vec, GAIN, 0, 0) + row_of(vec, SHIFT, 0, 0)).astype(LOW)
-
-    return call(kernel, [shape_of(tokens.shape, LOW)], [tokens, vectors], "first_norm")[0]
 
 
 def branch_norm(stream, terms, vectors, depth, which):
@@ -690,7 +940,7 @@
             member = jnp.bitwise_xor(me_ref[0], away)
             out[...] = joined[pl.ds(pl.multiple_of(member * rows, rows), rows), :].astype(LOW)
 
-    scratch = [pltpu.VMEM((4 * rows, width), WIDE)]
+    scratch = [pltpu.VMEM((4 * rows, width), grads[0].dtype)]
     out = shape_of((rows, width), LOW)
     return call(kernel, [out] * 4, [me, *grads], "split_grads", scratch=scratch, scalars=1)
 
@@ -716,7 +966,7 @@
                     start = pl.multiple_of((f * 4 + member) * lanes, 128)
                     value = ref[:, f * lanes : (f + 1) * lanes].astype(WIDE)
                     up_out[depth, :, pl.ds(start, lanes)] = value
-            down_out[depth] = (down0, down1)[depth][...]
+            down_out[depth] = (down0, down1)[depth][...].astype(WIDE)
         proj_out[...] = proj_ref[...].astype(WIDE)
 
     outs = [
@@ -764,16 +1014,36 @@
     unit = team * shard_rows
     table = ring_table()
     quick = frames == 2 and shard_rows % 32 == 0 and part % 128 == 0 and (hidden // rest) % 128 == 0
-
-    shards = []
-    proj_here = lax.ppermute(proj_weight, EVERY, spread(count, team))
-    for depth in range(2):
-        if quick:
-            split = split_weights(qkv_weight[depth], fc1_weight[depth], part, rest, me)
+    quick = quick and hidden == width and width // count == 32 and count * rows // FRAME_TOK <= 256
+
+    small_parts = (qkv_bias, fc1_bias, out_bias, norm_gain, norm_bias, layer_scale)
+    head_gain = jnp.tile(qk_gain.astype(WIDE), (1, 1, heads))
+    head_shift = jnp.tile(qk_bias.astype(WIDE), (1, 1, heads))
+    weights = []
+    if quick:
+        proj_here = lax.ppermute(proj_weight, EVERY, spread(count, team))
+        shards, below = [], None
+        for depth in range(2):
+            small = (qkv_bias, fc1_bias, scene_ids.reshape(1, rows)) + small_parts[2:]
+            split = split_weights(depth, (qkv_weight, fc1_weight), () if depth else small, part, rest, me)
             pieces = [split[0], swap(split[1], "frame"), swap(split[2], "core"), cross(split[3])]
-            attn, up = pack_weights(pieces, proj_here[depth], part, me)
-            down = fc2_weight[depth]
-        else:
+            if depth == 0:
+                below = pieces
+            shards.append(pack_weights(pieces, proj_here, depth, part, me, depth == 0))
+        ids = jnp.concatenate([m[shard_rows, 512 : 512 + rows] for m in below]).astype(jnp.int32)
+        tokens_all = team_gather(tokens)
+        half = unit // 2
+        rings = []
+        for depth in range(2):
+            low_half, high_half, up = shards[depth]
+            rings.append(RingGather(low_half, high_half, rest))
+            rings.append(RingGather(up, fc2_weight[depth], rest))
+            for ring in rings[-2:]:
+                steps(rest, ring)
+        vectors, bias_qkv, bias_up = unpack_vectors(rings[0].back, half, table, me)
+    else:
+        proj_here = lax.ppermute(proj_weight, EVERY, spread(count, team))
+        for depth in range(2):
             attn = exchange_columns(
                 qkv_weight[depth]
                 .reshape(shard_rows, 3, team, part)
@@ -788,45 +1058,44 @@
                 .reshape(shard_rows, team, hidden)
             ).reshape(unit, hidden)
             down = widen(fc2_weight[depth], hidden)
-        shards.append((attn, up, down))
-
-    weights = []
+            attn, up, down = (lax.all_gather(m, REST, axis=0, tiled=False) for m in (attn, up, down))
+            proj = Whole(narrow(attn[:, :, 3 * part :], shard_rows).reshape(1, part, width), 0, part)
+            down = Whole(narrow(down, fc2_rows).reshape(1, hidden, width), 0, hidden)
+            weights.append(((Whole(attn, 0, unit), proj, part, width, table), (Whole(up, 0, unit), down)))
+        small = small_gather(jnp.concatenate([m.reshape(-1) for m in small_parts])).astype(WIDE)
+        n_qkv, n_up = qkv_bias.size, fc1_bias.size
+        bias_qkv = small[:, :n_qkv].reshape(count, 2, -1).transpose(1, 0, 2).reshape(2, 3, team, part)
+        bias_qkv = lax.dynamic_index_in_dim(bias_qkv, mine, 2, keepdims=False).reshape(2, 3 * part)
+        bias_up = small[:, n_qkv : n_qkv + n_up].reshape(rest, team, 2, -1)
+        bias_up = lax.dynamic_index_in_dim(bias_up, mine, 1, keepdims=False)
+        bias_up = bias_up.transpose(1, 0, 2).reshape(2, hidden)
+        vectors = small[:, n_qkv + n_up :].reshape(count, 16, -1).transpose(1, 0, 2).reshape(16, width)
+        ids = jnp.concatenate([m.reshape(-1) for m in team_gather(scene_ids.reshape(1, rows))])
+        tokens_all = team_gather(tokens)
+
+    gathered = []
+    streams, middles, branches, kept = [tokens], [], [], []
     for depth in range(2):
-        attn, up, down = shards[depth]
-        (attn,) = ring_gather(attn[: unit // 2], attn[unit // 2 :], table, True)
-        up, down = ring_gather(up, down, table, False)
+        work = None
         if quick:
-            weights.append(((attn, attn, shard_rows, part), up, down))
+            ring = rings[2 * depth]
+            attn_source = Pieces(half, (ring.back, 0, 0), (ring.ahead, 1, half))
+            attn_weights = (attn_source, None, shard_rows, part, table)
         else:
-            proj = narrow(attn[:, :, 3 * part :], shard_rows).reshape(1, part, width)
-            down = narrow(down, fc2_rows).reshape(1, hidden, width)
-            weights.append(((attn, proj, part, width), up, down))
-
-    small_parts = (qkv_bias, fc1_bias, out_bias, norm_gain, norm_bias, layer_scale)
-    small = small_gather(jnp.concatenate([m.reshape(-1) for m in small_parts])).astype(WIDE)
-    n_qkv, n_up = qkv_bias.size, fc1_bias.size
-    bias_qkv = small[:, :n_qkv].reshape(count, 2, -1).transpose(1, 0, 2).reshape(2, 3, team, part)
-    bias_qkv = lax.dynamic_index_in_dim(bias_qkv, mine, 2, keepdims=False).reshape(2, 3 * part)
-    bias_up = small[:, n_qkv : n_qkv + n_up].reshape(rest, team, 2, -1)
-    bias_up = lax.dynamic_index_in_dim(bias_up, mine, 1, keepdims=False)
-    bias_up = bias_up.transpose(1, 0, 2).reshape(2, hidden)
-    vectors = small[:, n_qkv + n_up :].reshape(count, 16, -1).transpose(1, 0, 2).reshape(16, width)
-    head_gain = jnp.tile(qk_gain.astype(WIDE), (1, 1, heads))
-    head_shift = jnp.tile(qk_bias.astype(WIDE), (1, 1, heads))
-
-    ids = jnp.concatenate([m.reshape(-1) for m in team_gather(scene_ids.reshape(1, rows))])
-
-    streams, middles, branches, kept = [tokens], [], [], []
-    low = first_norm(tokens, vectors)
-    for depth in range(2):
-        attn_weights, weight_up, weight_down = weights[depth]
-        kept_attn, own, peer = attn_forward(
-            team_gather(low), attn_weights, bias_qkv[depth : depth + 1], head_gain[depth], head_shift[depth],
-            ids, head_size, frames, depth == 0,
+            attn_weights, mlp_sources = weights[depth]
+        kept_attn, own, peer, attn_weights = attn_forward(
+            team_gather(low, work, work) if depth else tokens_all, attn_weights, bias_qkv[depth : depth + 1],
+            head_gain[depth], head_shift[depth], ids, head_size, frames, depth == 0, None if depth else vectors,
         )
-        branch_one, middle, low = branch_norm(streams[depth], team_sum(own, peer), vectors, depth, 0)
-        kept_mlp, own, peer = mlp_forward(team_gather(low), weight_up, weight_down, bias_up[depth : depth + 1])
-        terms = team_sum(own, peer)
+        terms = team_sum(own, peer, work)
+        branch_one, middle, low = branch_norm(streams[depth], terms, vectors, depth, 0)
+        pieces = team_gather(low, work, work)
+        if quick:
+            ring = rings[2 * depth + 1]
+            mlp_sources = (Pieces(unit, (ring.back, 0, 0)), Pieces(unit, (ring.ahead, 1, 0)))
+        kept_mlp, own, peer, mlp_weights = mlp_forward(pieces, mlp_sources, table, bias_up[depth : depth + 1])
+        gathered.append((attn_weights, mlp_weights))
+        terms = team_sum(own, peer, work)
         branch_two = None
         if depth == 0:
             branch_two, stream, low = branch_norm(middle, terms, vectors, 0, 1)
@@ -839,25 +1108,85 @@
     grad = cotangent
     rows_of = {(SCALE, 1, 1): turn_sums[0], (OUT, 1, 1): turn_sums[1]}
     sums_up, sums_qkv, head_sums = [None, None], [None, None], [None, None]
-    finals = [None, None]
+    finals = [{}, {}]
+    ring = RingSums(rest)
+
+    def end_mlp(depth):
+        def end(up_sum, down_sum):
+            if not quick:
+                up = exchange_columns(up_sum.astype(LOW).reshape(team, shard_rows, hidden).transpose(1, 0, 2))
+                up = up.reshape(team, shard_rows, rest, hidden // rest).transpose(1, 2, 0, 3)
+                finals[depth].update(up=up.reshape(shard_rows, -1), down=narrow(down_sum, fc2_rows))
+                return
+            end_up(depth)(up_sum)
+            finals[depth].update(down=down_sum)
+
+        return end
+
+    def end_up(depth):
+        def end(*halves):
+            m = split_grads(halves, me)
+            finals[depth].update(up=[m[0], swap(m[1], "frame"), swap(m[2], "core"), cross(m[3])])
+
+        return end
+
+    def end_attn(depth):
+        def end(low_sum, high_sum):
+            if not quick:
+                both = jnp.concatenate([low_sum, high_sum], axis=0)
+                qkv = exchange_columns(
+                    both[:, : 3 * part].astype(LOW).reshape(team, shard_rows, 3 * part).transpose(1, 0, 2)
+                )
+                qkv = qkv.reshape(team, shard_rows, 3, part).transpose(1, 2, 0, 3)
+                proj = narrow(both[:, 3 * part :], shard_rows)
+                finals[depth].update(qkv=qkv.reshape(shard_rows, -1), proj=proj.astype(LOW))
+                return
+            m = split_grads([low_sum[:, : 3 * part], high_sum[:, : 3 * part]], me)
+            proj = jnp.concatenate([n[:, 3 * part :] for n in (low_sum, high_sum)], axis=0)
+            finals[depth].update(
+                qkv=[m[0], swap(m[1], "frame"), swap(m[2], "core"), cross(m[3])],
+                proj=narrow(proj, shard_rows).astype(LOW),
+            )
+
+        return end
+
     for depth in (1, 0):
-        attn_weights, weight_up, weight_down = weights[depth]
+        attn_weights, (weight_up, weight_down) = gathered[depth]
         kept_attn, (second, act, slope) = kept[depth]
         first, flat = kept_attn[0], kept_attn[4]
-        (branch_low, pre_low, sum_up), own, peer = mlp_backward(team_gather(low), weight_up, weight_down, slope)
+        pieces = team_gather(low, ring.work)
+        (branch_low, pre_low, sum_up), own, peer = mlp_backward(pieces, weight_up, weight_down, slope)
         sums_up[depth] = sum_up
-        grad_down = dot_tn(act, branch_low).astype(LOW)
-        grad_up = dot_tn(second, pre_low).astype(LOW)
+        if quick:
+            mlp_parts = mlp_weight_grads(second, pre_low, act, branch_low, rest, table)
+        else:
+            grad_up = dot_tn(second, pre_low).astype(LOW).reshape(rest, unit, hidden)
+            grad_down = dot_tn(act, branch_low).astype(LOW)
+            grad_down = grad_down.reshape(rest, fc2_rows, width // hidden, hidden)
+            grad_down = grad_down.transpose(0, 2, 1, 3).reshape(rest, -1, hidden)
+            mlp_parts = hop_order(grad_up, grad_down, table)
+        ring.add(*mlp_parts, end_mlp(depth))
+        terms = team_sum(own, peer, ring.work)
         grad_middle, low, sums = norm_back(
-            grad, team_sum(own, peer), middles[depth], branches[depth][0], vectors, depth, 1, (depth, 0)
+            grad, terms, middles[depth], branches[depth][0], vectors, depth, 1, (depth, 0)
         )
         for kind, place, row in ((GAIN, 1, 0), (SHIFT, 1, 1), (SCALE, 0, 2), (OUT, 0, 3)):
             rows_of[kind, depth, place] = sums[row]
+        pieces = team_gather(low, ring.work, ring.pump)
         (att_low, mixed_low, sum_qkv, head_sum), own, peer = attn_backward(
-            team_gather(low), attn_weights, head_gain[depth], kept_attn, ids, head_size, frames, depth == 0
+            pieces, attn_weights, head_gain[depth], kept_attn, ids, head_size, frames, depth == 0
         )
         sums_qkv[depth], head_sums[depth] = sum_qkv, head_sum
-        terms = team_sum(own, peer)
+        if quick:
+            attn_parts = attn_weight_grads(first, mixed_low, flat, att_low, rest, shard_rows, table)
+        else:
+            grad_qkv = dot_tn(first, mixed_low).astype(LOW).reshape(rest, unit, 3 * part)
+            grad_proj = dot_tn(flat, att_low).astype(LOW).reshape(rest, shard_rows, team, part)
+            grad_proj = grad_proj.transpose(0, 2, 1, 3).reshape(rest, unit, part)
+            attn = jnp.concatenate([grad_qkv, grad_proj], axis=2)
+            attn_parts = hop_order(attn[:, : unit // 2], attn[:, unit // 2 :], table)
+        ring.add(*attn_parts, end_attn(depth))
+        terms = team_sum(own, peer, ring.work)
         if depth == 1:
             grad, low, sums = norm_back(
                 grad_middle, terms, streams[1], branches[0][1], vectors, 1, 0, (0, 1)
@@ -866,55 +1195,21 @@
         else:
             input_grad, sums = norm_back(grad_middle, terms, tokens, None, vectors, 0, 0, None)
         rows_of[GAIN, depth, 0], rows_of[SHIFT, depth, 0] = sums[0], sums[1]
-
-        grad_up = grad_up.reshape(rest, unit, hidden)
-        if quick:
-            grad_down = grad_down.reshape(rest, fc2_rows, width)
-            attn = attn_weight_grads(first, mixed_low, flat, att_low, rest, shard_rows)
-        else:
-            grad_down = grad_down.reshape(rest, fc2_rows, width // hidden, hidden)
-            grad_down = grad_down.transpose(0, 2, 1, 3).reshape(rest, -1, hidden)
-            grad_qkv = dot_tn(first, mixed_low).astype(LOW).reshape(rest, unit, 3 * part)
-            grad_proj = dot_tn(flat, att_low).astype(LOW).reshape(rest, shard_rows, team, part)
-            grad_proj = grad_proj.transpose(0, 2, 1, 3).reshape(rest, unit, part)
-            attn = jnp.concatenate([grad_qkv, grad_proj], axis=2)
-        up_sum, down_sum = ring_sum(grad_up, grad_down, table, False)
-        attn_sum = ring_sum(attn, attn, table, True)
-        if quick:
-            up_pieces = split_grads([up_sum], me)
-            qkv_pieces = split_grads([m[:, : 3 * part] for m in attn_sum], me)
-            up_pieces, qkv_pieces = (
-                [m[0], swap(m[1], "frame"), swap(m[2], "core"), cross(m[3])] for m in (up_pieces, qkv_pieces)
-            )
-            proj_sum = jnp.concatenate([m[:, 3 * part :] for m in attn_sum], axis=0)
-            finals[depth] = (qkv_pieces, up_pieces, narrow(proj_sum, shard_rows).astype(LOW), down_sum)
-        else:
-            attn_sum = jnp.concatenate(attn_sum, axis=0)
-            qkv_mine = exchange_columns(
-                attn_sum[:, : 3 * part].astype(LOW).reshape(team, shard_rows, 3 * part).transpose(1, 0, 2)
-            )
-            qkv_mine = qkv_mine.reshape(team, shard_rows, 3, part).transpose(1, 2, 0, 3)
-            up_mine = exchange_columns(up_sum.astype(LOW).reshape(team, shard_rows, hidden).transpose(1, 0, 2))
-            up_mine = up_mine.reshape(team, shard_rows, rest, hidden // rest).transpose(1, 2, 0, 3)
-            finals[depth] = (
-                qkv_mine.reshape(shard_rows, -1),
-                up_mine.reshape(shard_rows, -1),
-                narrow(attn_sum[:, 3 * part :], shard_rows).astype(LOW),
-                narrow(down_sum, fc2_rows),
-            )
+    while ring.busy():
+        ring.pump()
 
     proj_grad = lax.ppermute(
-        jnp.stack([finals[0][2], finals[1][2]]), EVERY, [(b, a) for a, b in spread(count, team)]
+        jnp.stack([finals[0]["proj"], finals[1]["proj"]]), EVERY, [(b, a) for a, b in spread(count, team)]
     )
     if quick:
         qkv_grad, up_grad, proj_grad, down_grad = place_grads(
-            [finals[0][0], finals[1][0]], [finals[0][1], finals[1][1]], proj_grad,
-            [finals[0][3], finals[1][3]], part, rest, me,
+            [m["qkv"] for m in finals], [m["up"] for m in finals], proj_grad,
+            [m["down"] for m in finals], part, rest, me,
         )
     else:
         proj_grad = proj_grad.astype(WIDE)
         qkv_grad, up_grad, down_grad = (
-            jnp.stack([finals[0][i], finals[1][i]]).astype(WIDE) for i in (0, 1, 3)
+            jnp.stack([m[name] for m in finals]).astype(WIDE) for name in ("qkv", "up", "down")
         )
 
     names = [(kind, depth, place) for kind in (OUT, GAIN, SHIFT, SCALE) for depth in (0, 1) for place in (0, 1)]

time: 629 us -> 502 us (0.80)
  the two profiles are of different devices: /device:TPU:0 before, /device:TPU:7 now
where the time goes in v3:
time: 502 us; the launch traced here: 492 us
  waiting for transfers between devices  170 us (34%)
  starting transfers between devices  162 us (32%)
  Pallas kernels  115 us (23%)
  local copies, waits for them, and re-layouts  36.4 us (7%)
  other arithmetic  6.28 us (1%)
    pallas_call x46, Pallas kernels, call(): pl.pallas_call(kernel, out_shape=list(outs), in_specs=in_specs, out_specs...  115 us
    ppermute x86, waiting for transfers between devices, ring_shift(): lax.ppermute(values, REST, [(order[i], order[(i + sign) % rest]) for i in...  94.6 us
    ppermute x62, starting transfers between devices, swap(): return lax.ppermute(values, axis, [(0, 1), (1, 0)])  78 us
    ppermute x86, starting transfers between devices, ring_shift(): lax.ppermute(values, REST, [(order[i], order[(i + sign) % rest]) for i in...  65.9 us
    ppermute x62, waiting for transfers between devices, swap(): return lax.ppermute(values, axis, [(0, 1), (1, 0)])  42.8 us
    unnamed x213, local copies, waits for them, and re-layouts  23.4 us
    ppermute x3, waiting for transfers between devices, small_sum(): came = lax.ppermute(packed, axis, pairs)  18.1 us
    ppermute x6, waiting for transfers between devices, cross(): return lax.ppermute(values, TEAM, [(0, 3), (1, 2), (2, 1), (3, 0)])  14.2 us
  transfers between devices with their start and end apart: 159, of which 67 were waited for; matrix products, arithmetic and copies ran while one was open for 4% of the time, Pallas kernels for 19%

profile of v3, /device:TPU:7, one launch (start us, length us, event | category | flops | bytes accessed | tf_op | source)
XLA Modules:
  0.0 492.0 jit_solution(8116170352590590230)
XLA Ops:
  0.6 5.8 %collective-permute-start.3 = (bf16[2,32,1024]{2,1,0:T(8,128)(2,1)}, bf16[2,32,1024]{2,1,0:T(8,128)(2,1)S(1)}, u32[]{:S(2)}, u32[]{:S(2)}) collective-permute-start(bf16[2,32,1024]{2,1,0:T(8,128)(2,1)} %param.22), channel_id=1, source_target_pairs={{0,0},{1,4},{2,8},{3,12},{4,16},{5,20},{6,24},{7,28},{8,1},{9,5},{... | collective-permute-start | bytes 393224 | tf_op jit(solution)/shard_map/ppermute | solution.py:1024
  19.5 3.8 collective-permute-done.2.p3
  24.9 3.1 collective-permute-done.5.refs_9_
  35.3 3.2 collective-permute-done.24.refs_1_
  43.5 4.2 collective-permute-done.11.refs_12_
  47.7 2.9 collective-permute-done.10.refs_4_
  57.4 6.3 %collective-permute-done.15.refs_14_ = bf16[64,1024]{1,0:T(8,128)(2,1)} collective-permute-done((bf16[64,1024]{1,0:T(8,128)(2,1)S(1)}, bf16[64,1024]{1,0:T(8,128)(2,1)}, u32[]{:S(2)}, u32[]{:S(2)}) %collective-permute-start.15) | collective-permute-done | bytes 131104 | tf_op jit(solution)/shard_map/ppermute | solution.py:272
  65.7 3.4 collective-permute-start.19
  77.5 11.1 %attn_forward.2 = (bf16[512,1024]{1,0:T(8,128)(2,1)S(1)}, f32[512,512]{1,0:T(8,128)S(1)}, bf16[512,768]{1,0:T(8,128)(2,1)S(1)}, f32[512,4]{1,0:T(8,128)S(1)}, bf...) custom-call(s32[2,8]{1,0:T(2,128)S(1)} %fusion.1.table_ref, ...), custom_call_target="tpu_custom_call" | custom-call | flops 1140850688 | bytes 10308672 | tf_op jit(solution)/shard_map/attn_forward/pallas_call | solution.py:65
  96.8 4.1 collective-permute-done.32.refs_5_
  107.5 6.5 %collective-permute-done.46.p3 = bf16[32,1792]{1,0:T(8,128)(2,1)S(1)} collective-permute-done((bf16[32,1792]{1,0:T(8,128)(2,1)S(1)}, bf16[32,1792]{1,0:T(8,128)(2,1)S(1)}, u32[]{:S(2)}, u32[]{:S(2)}) %collective-permute-start.46) | collective-permute-done | bytes 114720 | tf_op jit(solution)/shard_map/ppermute | solution.py:82
  121.8 3.5 collective-permute-done.36.refs_7_
  126.9 6.1 %mlp_forward.2 = (bf16[512,1024]{1,0:T(8,128)(2,1)S(1)}, bf16[512,1024]{1,0:T(8,128)(2,1)S(1)}, bf16[512,1024]{1,0:T(8,128)(2,1)S(1)}, f32[128,1024]{1,0:T(8,128...) custom-call(s32[2,8]{1,0:T(2,128)S(1)} %fusion.1.table_ref, ...), custom_call_target="tpu_custom_call" | custom-call | flops 2147483648 | bytes 14159936 | tf_op jit(solution)/shard_map/mlp_forward/pallas_call | solution.py:65
  151.4 2.8 collective-permute-done.54.refs_12_
  164.6 2.7 collective-permute-done.57.refs_6_
  167.3 4.2 collective-permute-start.62
  176.8 8.8 %attn_forward.3 = (bf16[512,1024]{1,0:T(8,128)(2,1)S(1)}, f32[512,512]{1,0:T(8,128)S(1)}, bf16[512,768]{1,0:T(8,128)(2,1)S(1)}, f32[512,4]{1,0:T(8,128)S(1)}, bf...) custom-call(s32[2,8]{1,0:T(2,128)S(1)} %fusion.1.table_ref, ...), custom_call_target="tpu_custom_call" | custom-call | flops 1207959552 | bytes 9980992 | tf_op jit(solution)/shard_map/attn_forward/pallas_call | solution.py:65
  185.5 5.8 %collective-permute-start.65 = (bf16[128,1024]{1,0:T(8,128)(2,1)S(1)}, bf16[128,1024]{1,0:T(8,128)(2,1)S(1)}, u32[]{:S(2)}, u32[]{:S(2)}) collective-permute-start(bf16[128,1024]{1,0:T(8,128)(2,1)S(1)} %get-tuple-element.424), channel_id=1, source_target_pairs={{0,2},{2,0},{1,3},{3,1},{4,6},{6,4},{5,7},{7,5},{8,10},{10,8},{9,1... | collective-permute-start | bytes 786440 | tf_op jit(solution)/shard_map/ppermute | solution.py:78
  193.6 5.7 %collective-permute-done.75.refs_5_ = bf16[128,1024]{1,0:T(8,128)(2,1)S(1)} collective-permute-done((bf16[128,1024]{1,0:T(8,128)(2,1)S(1)}, bf16[128,1024]{1,0:T(8,128)(2,1)S(1)}, u32[]{:S(2)}, u32[]{:S(2)}) %collective-permute-start.75) | collective-permute-done | bytes 262176 | tf_op jit(solution)/shard_map/ppermute | solution.py:272
  202.7 4.4 collective-permute-done.77.refs_6_
  214.4 6.1 %mlp_forward.3 = (bf16[512,1024]{1,0:T(8,128)(2,1)S(1)}, bf16[512,1024]{1,0:T(8,128)(2,1)S(1)}, bf16[512,1024]{1,0:T(8,128)(2,1)S(1)}, f32[128,1024]{1,0:T(8,128...) custom-call(s32[2,8]{1,0:T(2,128)S(1)} %fusion.1.table_ref, ...), custom_call_target="tpu_custom_call" | custom-call | flops 2147483648 | bytes 14159936 | tf_op jit(solution)/shard_map/mlp_forward/pallas_call | solution.py:65
  220.5 3.5 collective-permute-start.85
  225.6 7.3 %collective-permute-done.86.refs_2_ = bf16[128,1024]{1,0:T(8,128)(2,1)S(1)} collective-permute-done((bf16[128,1024]{1,0:T(8,128)(2,1)S(1)}, bf16[128,1024]{1,0:T(8,128)(2,1)S(1)}, u32[]{:S(2)}, u32[]{:S(2)}) %collective-permute-start.86) | collective-permute-done | bytes 262176 | tf_op jit(solution)/shard_map/ppermute | solution.py:78
  235.2 5.1 %collective-permute-done.87.refs_1_ = bf16[128,1024]{1,0:T(8,128)(2,1)S(1)} collective-permute-done((bf16[128,1024]{1,0:T(8,128)(2,1)S(1)}, bf16[128,1024]{1,0:T(8,128)(2,1)S(1)}, u32[]{:S(2)}, u32[]{:S(2)}) %collective-permute-start.87) | collective-permute-done | bytes 262176 | tf_op jit(solution)/shard_map/ppermute | solution.py:78
  243.6 4.0 mlp_backward.2
  248.1 4.5 mlp_weight_grads.2
  255.8 5.7 %collective-permute-done.92.refs_6_ = bf16[128,1024]{1,0:T(8,128)(2,1)S(1)} collective-permute-done((bf16[128,1024]{1,0:T(8,128)(2,1)S(1)}, bf16[128,1024]{1,0:T(8,128)(2,1)S(1)}, u32[]{:S(2)}, u32[]{:S(2)}) %collective-permute-start.92) | collective-permute-done | bytes 262176 | tf_op jit(solution)/shard_map/ppermute | solution.py:78
  276.5 10.5 %attn_backward.2 = (bf16[512,1024]{1,0:T(8,128)(2,1)S(1)}, bf16[512,768]{1,0:T(8,128)(2,1)S(1)}, f32[1,768]{1,0:T(1,128)S(1)}, f32[4,256]{1,0:T(4,128)S(1)}, f32...) custom-call(bf16[128,1024]{1,0:T(8,128)(2,1)S(1)} %get-tuple-element, ...), custom_call_target="tpu_custom_call" | custom-call | flops 1409286144 | bytes 8410112 | tf_op jit(solution)/shard_map/attn_backward/pallas_call | solution.py:65
  287.6 3.3 attn_weight_grads.2
  294.6 5.3 %collective-permute-done.104.refs_6_ = bf16[128,1024]{1,0:T(8,128)(2,1)S(1)} collective-permute-done((bf16[128,1024]{1,0:T(8,128)(2,1)S(1)}, bf16[128,1024]{1,0:T(8,128)(2,1)S(1)}, u32[]{:S(2)}, u32[]{:S(2)}) %collective-permute-start.104) | collective-permute-done | bytes 262176 | tf_op jit(solution)/shard_map/ppermute | solution.py:78
  311.1 4.0 mlp_backward.3
  315.7 4.4 collective-permute-done.110.refs_0_
  320.5 4.6 mlp_weight_grads.3
  331.1 6.8 %collective-permute-done.114.refs_6_ = bf16[128,1024]{1,0:T(8,128)(2,1)S(1)} collective-permute-done((bf16[128,1024]{1,0:T(8,128)(2,1)S(1)}, bf16[128,1024]{1,0:T(8,128)(2,1)S(1)}, u32[]{:S(2)}, u32[]{:S(2)}) %collective-permute-start.114) | collective-permute-done | bytes 262176 | tf_op jit(solution)/shard_map/ppermute | solution.py:78
  342.5 2.7 ring_add.22
  347.4 3.1 collective-permute-start.120
  352.6 6.9 %collective-permute-done.118.refs_0_ = bf16[320,1024]{1,0:T(8,128)(2,1)} collective-permute-done((bf16[320,1024]{1,0:T(8,128)(2,1)}, bf16[320,1024]{1,0:T(8,128)(2,1)}, u32[]{:S(2)}, u32[]{:S(2)}) %collective-permute-start.118) | collective-permute-done | bytes 655392 | tf_op jit(solution)/shard_map/ppermute | solution.py:272
  360.0 3.5 collective-permute-start.121
  364.7 2.9 ring_add.23
  371.0 13.5 %attn_backward.3 = (bf16[512,1024]{1,0:T(8,128)(2,1)S(1)}, bf16[512,768]{1,0:T(8,128)(2,1)S(1)}, f32[1,768]{1,0:T(1,128)S(1)}, f32[4,256]{1,0:T(4,128)S(1)}, f32...) custom-call(bf16[128,1024]{1,0:T(8,128)(2,1)} %get-tuple-element.560., ...), custom_call_target="tpu_custom_call" | custom-call | flops 1241513984 | bytes 8410112 | tf_op jit(solution)/shard_map/attn_backward/pallas_call | solution.py:65
  385.6 3.3 attn_weight_grads.3
  395.0 4.1 collective-permute-done.126.refs_5_
  413.0 11.3 %collective-permute-done.156 = f32[16384]{0:T(1024)S(1)} collective-permute-done((f32[16384]{0:T(1024)S(1)}, f32[16384]{0:T(1024)S(1)}, u32[]{:S(2)}, u32[]{:S(2)}) %collective-permute-start.156) | collective-permute-done | bytes 65568 | tf_op jit(solution)/shard_map/ppermute | solution.py:475
  427.6 6.8 %collective-permute-done.157 = f32[11776]{0:T(1024)S(1)} collective-permute-done((f32[11776]{0:T(1024)S(1)}, f32[11776]{0:T(1024)S(1)}, u32[]{:S(2)}, u32[]{:S(2)}) %collective-permute-start.157) | collective-permute-done | bytes 47136 | tf_op jit(solution)/shard_map/ppermute | solution.py:475
  438.1 4.4 collective-permute-done.133.refs_0_
  446.4 6.3 %collective-permute-start.151 = (bf16[32,1024]{1,0:T(8,128)(2,1)S(1)}, bf16[32,1024]{1,0:T(8,128)(2,1)S(1)}, u32[]{:S(2)}, u32[]{:S(2)}) collective-permute-start(bf16[32,1024]{1,0:T(8,128)(2,1)S(1)} %get-tuple-element.669), channel_id=1, source_target_pairs={{0,2},{2,0},{1,3},{3,1},{4,6},{6,4},{5,7},{7,5},{8,10},{10,8},{9,1... | collective-permute-start | bytes 196616 | tf_op jit(solution)/shard_map/ppermute | solution.py:78
  474.6 4.1 collective-permute-start.153
  484.8 2.9 collective-permute-done.149.refs_11_
  (631 shorter events, 239.9 us)
Async XLA Ops:
  0.6 17.7 %collective-permute-start.3 = (bf16[2,32,1024]{2,1,0:T(8,128)(2,1)}, bf16[2,32,1024]{2,1,0:T(8,128)(2,1)S(1)}, u32[]{:S(2)}, u32[]{:S(2)}) collective-permute-start(bf16[2,32,1024]{2,1,0:T(8,128)(2,1)} %param.22), channel_id=1, source_target_pairs={{0,0},{1,4},{2,8},{3,12},{4,16},{5,20},{6,24},{7,28},{8,1},{9,5},{... | collective-permute-start | bytes 393224 | tf_op jit(solution)/shard_map/ppermute | solution.py:1024
  17.0 18.4 %collective-permute-start.25 = (bf16[128,1024]{1,0:T(8,128)(2,1)S(1)}, bf16[128,1024]{1,0:T(8,128)(2,1)}, u32[]{:S(2)}, u32[]{:S(2)}) collective-permute-start(bf16[128,1024]{1,0:T(8,128)(2,1)S(1)} %get-tuple-element.689.refs_8_), channel_id=1, source_target_pairs={{4,0},{12,4},{20,12},{28,20},{24,28},{16,24},{8,16},{0,8},{5,1},{1... | collective-permute-start | bytes 786440 | tf_op jit(solution)/shard_map/ppermute | solution.py:272
  18.3 47.3 %collective-permute-start.18 = (bf16[128,1024]{1,0:T(8,128)(2,1)}, bf16[128,1024]{1,0:T(8,128)(2,1)S(1)}, u32[]{:S(2)}, u32[]{:S(2)}) collective-permute-start(bf16[128,1024]{1,0:T(8,128)(2,1)} %refs_1_.3), channel_id=1, source_target_pairs={{0,1},{1,0},{2,3},{3,2},{4,5},{5,4},{6,7},{7,6},{8,9},{9,8},{10,11... | collective-permute-start | bytes 786440 | tf_op jit(solution)/shard_map/ppermute | solution.py:78
  38.5 13.6 %collective-permute-start.26 = (bf16[128,1024]{1,0:T(8,128)(2,1)}, bf16[128,1024]{1,0:T(8,128)(2,1)S(1)}, u32[]{:S(2)}, u32[]{:S(2)}) collective-permute-start(bf16[128,1024]{1,0:T(8,128)(2,1)} %collective-permute-done.24.refs_1_), channel_id=1, source_target_pairs={{4,12},{12,20},{20,28},{28,24},{24,16},{16,8},{8,0},{0,4},{5,13},{... | collective-permute-start | bytes 786440 | tf_op jit(solution)/shard_map/ppermute | solution.py:272
  39.1 13.0 %collective-permute-start.27 = (bf16[128,1024]{1,0:T(8,128)(2,1)}, bf16[128,1024]{1,0:T(8,128)(2,1)}, u32[]{:S(2)}, u32[]{:S(2)}) collective-permute-start(bf16[128,1024]{1,0:T(8,128)(2,1)} %collective-permute-done.25.refs_9_), channel_id=1, source_target_pairs={{4,0},{12,4},{20,12},{28,20},{24,28},{16,24},{8,16},{0,8},{5,1},{1... | collective-permute-start | bytes 786440 | tf_op jit(solution)/shard_map/ppermute | solution.py:272
  52.1 17.0 %collective-permute-start.28 = (bf16[128,1024]{1,0:T(8,128)(2,1)S(1)}, bf16[128,1024]{1,0:T(8,128)(2,1)S(1)}, u32[]{:S(2)}, u32[]{:S(2)}) collective-permute-start(bf16[128,1024]{1,0:T(8,128)(2,1)S(1)} %collective-permute-done.26.refs_2_), channel_id=1, source_target_pairs={{4,12},{12,20},{20,28},{28,24},{24,16},{16,8},{8,0},{0,4},{5,13},{... | collective-permute-start | bytes 786440 | tf_op jit(solution)/shard_map/ppermute | solution.py:272
  53.4 16.7 %collective-permute-start.29 = (bf16[128,1024]{1,0:T(8,128)(2,1)}, bf16[128,1024]{1,0:T(8,128)(2,1)}, u32[]{:S(2)}, u32[]{:S(2)}) collective-permute-start(bf16[128,1024]{1,0:T(8,128)(2,1)} %collective-permute-done.27.refs_10_), channel_id=1, source_target_pairs={{4,0},{12,4},{20,12},{28,20},{24,28},{16,24},{8,16},{0,8},{5,1},{1... | collective-permute-start | bytes 786440 | tf_op jit(solution)/shard_map/ppermute | solution.py:272
  70.1 22.8 %collective-permute-start.30 = (bf16[128,1024]{1,0:T(8,128)(2,1)}, bf16[128,1024]{1,0:T(8,128)(2,1)S(1)}, u32[]{:S(2)}, u32[]{:S(2)}) collective-permute-start(bf16[128,1024]{1,0:T(8,128)(2,1)} %copy-done.72), channel_id=1, source_target_pairs={{4,12},{12,20},{20,28},{28,24},{24,16},{16,8},{8,0},{0,4},{5,13},{... | collective-permute-start | bytes 786440 | tf_op jit(solution)/shard_map/ppermute | solution.py:272
  71.2 21.7 %collective-permute-start.31 = (bf16[128,1024]{1,0:T(8,128)(2,1)}, bf16[128,1024]{1,0:T(8,128)(2,1)S(1)}, u32[]{:S(2)}, u32[]{:S(2)}) collective-permute-start(bf16[128,1024]{1,0:T(8,128)(2,1)} %collective-permute-done.29.refs_11_), channel_id=1, source_target_pairs={{4,0},{12,4},{20,12},{28,20},{24,28},{16,24},{8,16},{0,8},{5,1},{1... | collective-permute-start | bytes 786440 | tf_op jit(solution)/shard_map/ppermute | solution.py:272
  96.3 10.3 %collective-permute-start.44 = (bf16[32,1792]{1,0:T(8,128)(2,1)S(1)}, bf16[32,1792]{1,0:T(8,128)(2,1)S(1)}, u32[]{:S(2)}, u32[]{:S(2)}) collective-permute-start(bf16[32,1792]{1,0:T(8,128)(2,1)S(1)} %get-tuple-element.401), channel_id=1, source_target_pairs={{0,1},{1,0},{2,3},{3,2},{4,5},{5,4},{6,7},{7,6},{8,9},{9,8},{10,11... | collective-permute-start | bytes 344072 | tf_op jit(solution)/shard_map/ppermute | solution.py:78
  101.7 14.0 %collective-permute-start.34 = (bf16[128,1024]{1,0:T(8,128)(2,1)S(1)}, bf16[128,1024]{1,0:T(8,128)(2,1)S(1)}, u32[]{:S(2)}, u32[]{:S(2)}) collective-permute-start(bf16[128,1024]{1,0:T(8,128)(2,1)S(1)} %collective-permute-done.32.refs_5_), channel_id=1, source_target_pairs={{4,12},{12,20},{20,28},{28,24},{24,16},{16,8},{8,0},{0,4},{5,13},{... | collective-permute-start | bytes 786440 | tf_op jit(solution)/shard_map/ppermute | solution.py:272
  102.7 12.9 %collective-permute-start.35 = (bf16[128,1024]{1,0:T(8,128)(2,1)S(1)}, bf16[128,1024]{1,0:T(8,128)(2,1)S(1)}, u32[]{:S(2)}, u32[]{:S(2)}) collective-permute-start(bf16[128,1024]{1,0:T(8,128)(2,1)S(1)} %collective-permute-done.33.refs_13_), channel_id=1, source_target_pairs={{4,0},{12,4},{20,12},{28,20},{24,28},{16,24},{8,16},{0,8},{5,1},{1... | collective-permute-start | bytes 786440 | tf_op jit(solution)/shard_map/ppermute | solution.py:272
  103.5 16.5 %collective-permute-start.38 = (bf16[128,1024]{1,0:T(8,128)(2,1)S(1)}, bf16[128,1024]{1,0:T(8,128)(2,1)S(1)}, u32[]{:S(2)}, u32[]{:S(2)}) collective-permute-start(bf16[128,1024]{1,0:T(8,128)(2,1)S(1)} %get-tuple-element.393.refs_16_), channel_id=1, source_target_pairs={{0,1},{1,0},{2,3},{3,2},{4,5},{5,4},{6,7},{7,6},{8,9},{9,8},{10,11... | collective-permute-start | bytes 786440 | tf_op jit(solution)/shard_map/ppermute | solution.py:78
  120.5 17.4 %collective-permute-start.49 = (bf16[64,1024]{1,0:T(8,128)(2,1)S(1)}, bf16[64,1024]{1,0:T(8,128)(2,1)S(1)}, u32[]{:S(2)}, u32[]{:S(2)}) collective-permute-start(bf16[64,1024]{1,0:T(8,128)(2,1)S(1)} %collective-permute-done.47.refs_1_), channel_id=1, source_target_pairs={{4,12},{12,20},{20,28},{28,24},{24,16},{16,8},{8,0},{0,4},{5,13},{... | collective-permute-start | bytes 393224 | tf_op jit(solution)/shard_map/ppermute | solution.py:272
  125.3 12.6 %collective-permute-start.50 = (bf16[64,1024]{1,0:T(8,128)(2,1)S(1)}, bf16[64,1024]{1,0:T(8,128)(2,1)S(1)}, u32[]{:S(2)}, u32[]{:S(2)}) collective-permute-start(bf16[64,1024]{1,0:T(8,128)(2,1)S(1)} %collective-permute-done.48.refs_9_), channel_id=1, source_target_pairs={{4,0},{12,4},{20,12},{28,20},{24,28},{16,24},{8,16},{0,8},{5,1},{1... | collective-permute-start | bytes 393224 | tf_op jit(solution)/shard_map/ppermute | solution.py:272
  144.4 10.9 %collective-permute-start.41 = (bf16[128,1024]{1,0:T(8,128)(2,1)S(1)}, bf16[128,1024]{1,0:T(8,128)(2,1)S(1)}, u32[]{:S(2)}, u32[]{:S(2)}) collective-permute-start(bf16[128,1024]{1,0:T(8,128)(2,1)S(1)} %get-tuple-element.396), channel_id=1, source_target_pairs={{0,2},{2,0},{1,3},{3,1},{4,6},{6,4},{5,7},{7,5},{8,10},{10,8},{9,1... | collective-permute-start | bytes 786440 | tf_op jit(solution)/shard_map/ppermute | solution.py:78
  157.6 14.0 %collective-permute-start.61 = (bf16[128,1024]{1,0:T(8,128)(2,1)}, bf16[128,1024]{1,0:T(8,128)(2,1)}, u32[]{:S(2)}, u32[]{:S(2)}) collective-permute-start(bf16[128,1024]{1,0:T(8,128)(2,1)} %get-tuple-element.420.refs_16_), channel_id=1, source_target_pairs={{0,1},{1,0},{2,3},{3,2},{4,5},{5,4},{6,7},{7,6},{8,9},{9,8},{10,11... | collective-permute-start | bytes 786440 | tf_op jit(solution)/shard_map/ppermute | solution.py:78
  159.3 13.3 %collective-permute-start.71 = (bf16[128,1024]{1,0:T(8,128)(2,1)S(1)}, bf16[128,1024]{1,0:T(8,128)(2,1)S(1)}, u32[]{:S(2)}, u32[]{:S(2)}) collective-permute-start(bf16[128,1024]{1,0:T(8,128)(2,1)S(1)} %collective-permute-done.69.refs_2_), channel_id=1, source_target_pairs={{4,12},{12,20},{20,28},{28,24},{24,16},{16,8},{8,0},{0,4},{5,13},{... | collective-permute-start | bytes 786440 | tf_op jit(solution)/shard_map/ppermute | solution.py:272
  163.3 10.2 %collective-permute-start.72 = (bf16[128,1024]{1,0:T(8,128)(2,1)}, bf16[128,1024]{1,0:T(8,128)(2,1)}, u32[]{:S(2)}, u32[]{:S(2)}) collective-permute-start(bf16[128,1024]{1,0:T(8,128)(2,1)} %collective-permute-done.70.refs_10_), channel_id=1, source_target_pairs={{4,0},{12,4},{20,12},{28,20},{24,28},{16,24},{8,16},{0,8},{5,1},{1... | collective-permute-start | bytes 786440 | tf_op jit(solution)/shard_map/ppermute | solution.py:272
  173.6 17.7 %collective-permute-start.73 = (bf16[128,1024]{1,0:T(8,128)(2,1)}, bf16[128,1024]{1,0:T(8,128)(2,1)S(1)}, u32[]{:S(2)}, u32[]{:S(2)}) collective-permute-start(bf16[128,1024]{1,0:T(8,128)(2,1)} %copy-done.76), channel_id=1, source_target_pairs={{4,12},{12,20},{20,28},{28,24},{24,16},{16,8},{8,0},{0,4},{5,13},{... | collective-permute-start | bytes 786440 | tf_op jit(solution)/shard_map/ppermute | solution.py:272
  175.9 15.4 %collective-permute-start.74 = (bf16[128,1024]{1,0:T(8,128)(2,1)}, bf16[128,1024]{1,0:T(8,128)(2,1)S(1)}, u32[]{:S(2)}, u32[]{:S(2)}) collective-permute-start(bf16[128,1024]{1,0:T(8,128)(2,1)} %collective-permute-done.72.refs_11_), channel_id=1, source_target_pairs={{4,0},{12,4},{20,12},{28,20},{24,28},{16,24},{8,16},{0,8},{5,1},{1... | collective-permute-start | bytes 786440 | tf_op jit(solution)/shard_map/ppermute | solution.py:272
  265.4 11.0 %collective-permute-start.98 = (bf16[128,1024]{1,0:T(8,128)(2,1)S(1)}, bf16[128,1024]{1,0:T(8,128)(2,1)S(1)}, u32[]{:S(2)}, u32[]{:S(2)}) collective-permute-start(bf16[128,1024]{1,0:T(8,128)(2,1)S(1)} %get-tuple-element.477.refs_0_), channel_id=1, source_target_pairs={{0,2},{2,0},{1,3},{3,1},{4,6},{6,4},{5,7},{7,5},{8,10},{10,8},{9,1... | collective-permute-start | bytes 786440 | tf_op jit(solution)/shard_map/ppermute | solution.py:78
  274.8 12.8 %collective-permute-start.100 = (bf16[128,1024]{1,0:T(8,128)(2,1)S(1)}, bf16[128,1024]{1,0:T(8,128)(2,1)S(1)}, u32[]{:S(2)}, u32[]{:S(2)}) collective-permute-start(bf16[128,1024]{1,0:T(8,128)(2,1)S(1)} %get-tuple-element.488), channel_id=1, source_target_pairs={{4,12},{12,20},{20,28},{28,24},{24,16},{16,8},{8,0},{0,4},{5,13},{... | collective-permute-start | bytes 786440 | tf_op jit(solution)/shard_map/ppermute | solution.py:272
  275.4 12.3 %collective-permute-start.101 = (bf16[128,1024]{1,0:T(8,128)(2,1)S(1)}, bf16[128,1024]{1,0:T(8,128)(2,1)S(1)}, u32[]{:S(2)}, u32[]{:S(2)}) collective-permute-start(bf16[128,1024]{1,0:T(8,128)(2,1)S(1)} %get-tuple-element.489), channel_id=1, source_target_pairs={{4,0},{12,4},{20,12},{28,20},{24,28},{16,24},{8,16},{0,8},{5,1},{1... | collective-permute-start | bytes 786440 | tf_op jit(solution)/shard_map/ppermute | solution.py:272
  309.4 10.7 %collective-permute-start.110 = (bf16[192,1024]{1,0:T(8,128)(2,1)S(1)}, bf16[192,1024]{1,0:T(8,128)(2,1)S(1)}, u32[]{:S(2)}, u32[]{:S(2)}) collective-permute-start(bf16[192,1024]{1,0:T(8,128)(2,1)S(1)} %get-tuple-element.518), channel_id=1, source_target_pairs={{4,12},{12,20},{20,28},{28,24},{24,16},{16,8},{8,0},{0,4},{5,13},{... | collective-permute-start | bytes 1179656 | tf_op jit(solution)/shard_map/ppermute | solution.py:272
  309.9 10.6 %collective-permute-start.111 = (bf16[192,1024]{1,0:T(8,128)(2,1)S(1)}, bf16[192,1024]{1,0:T(8,128)(2,1)S(1)}, u32[]{:S(2)}, u32[]{:S(2)}) collective-permute-start(bf16[192,1024]{1,0:T(8,128)(2,1)S(1)} %get-tuple-element.519), channel_id=1, source_target_pairs={{4,0},{12,4},{20,12},{28,20},{24,28},{16,24},{8,16},{0,8},{5,1},{1... | collective-permute-start | bytes 1179656 | tf_op jit(solution)/shard_map/ppermute | solution.py:272
  315.1 14.8 %collective-permute-start.113 = (bf16[128,1024]{1,0:T(8,128)(2,1)S(1)}, bf16[128,1024]{1,0:T(8,128)(2,1)S(1)}, u32[]{:S(2)}, u32[]{:S(2)}) collective-permute-start(bf16[128,1024]{1,0:T(8,128)(2,1)S(1)} %get-tuple-element.544), channel_id=1, source_target_pairs={{0,2},{2,0},{1,3},{3,1},{4,6},{6,4},{5,7},{7,5},{8,10},{10,8},{9,1... | collective-permute-start | bytes 786440 | tf_op jit(solution)/shard_map/ppermute | solution.py:78
  326.7 15.2 %collective-permute-start.116 = (bf16[320,1024]{1,0:T(8,128)(2,1)S(1)}, bf16[320,1024]{1,0:T(8,128)(2,1)S(1)}, u32[]{:S(2)}, u32[]{:S(2)}) collective-permute-start(bf16[320,1024]{1,0:T(8,128)(2,1)S(1)} %get-tuple-element.540), channel_id=1, source_target_pairs={{4,12},{12,20},{20,28},{28,24},{24,16},{16,8},{8,0},{0,4},{5,13},{... | collective-permute-start | bytes 1966088 | tf_op jit(solution)/shard_map/ppermute | solution.py:272
  327.6 14.8 %collective-permute-start.117 = (bf16[320,1024]{1,0:T(8,128)(2,1)S(1)}, bf16[320,1024]{1,0:T(8,128)(2,1)S(1)}, u32[]{:S(2)}, u32[]{:S(2)}) collective-permute-start(bf16[320,1024]{1,0:T(8,128)(2,1)S(1)} %get-tuple-element.541), channel_id=1, source_target_pairs={{4,0},{12,4},{20,12},{28,20},{24,28},{16,24},{8,16},{0,8},{5,1},{1... | collective-permute-start | bytes 1966088 | tf_op jit(solution)/shard_map/ppermute | solution.py:272
  345.2 14.3 %collective-permute-start.118 = (bf16[320,1024]{1,0:T(8,128)(2,1)}, bf16[320,1024]{1,0:T(8,128)(2,1)}, u32[]{:S(2)}, u32[]{:S(2)}) collective-permute-start(bf16[320,1024]{1,0:T(8,128)(2,1)} %get-tuple-element.557), channel_id=1, source_target_pairs={{4,12},{12,20},{20,28},{28,24},{24,16},{16,8},{8,0},{0,4},{5,13},{... | collective-permute-start | bytes 1966088 | tf_op jit(solution)/shard_map/ppermute | solution.py:272
  346.0 14.0 %collective-permute-start.119 = (bf16[320,1024]{1,0:T(8,128)(2,1)}, bf16[320,1024]{1,0:T(8,128)(2,1)}, u32[]{:S(2)}, u32[]{:S(2)}) collective-permute-start(bf16[320,1024]{1,0:T(8,128)(2,1)} %get-tuple-element.558), channel_id=1, source_target_pairs={{4,0},{12,4},{20,12},{28,20},{24,28},{16,24},{8,16},{0,8},{5,1},{1... | collective-permute-start | bytes 1966088 | tf_op jit(solution)/shard_map/ppermute | solution.py:272
  347.4 23.5 %collective-permute-start.120 = (bf16[128,1024]{1,0:T(8,128)(2,1)}, bf16[128,1024]{1,0:T(8,128)(2,1)S(1)}, u32[]{:S(2)}, u32[]{:S(2)}) collective-permute-start(bf16[128,1024]{1,0:T(8,128)(2,1)} %get-tuple-element.560.refs_0_), channel_id=1, source_target_pairs={{0,2},{2,0},{1,3},{3,1},{4,6},{6,4},{5,7},{7,5},{8,10},{10,8},{9,1... | collective-permute-start | bytes 786440 | tf_op jit(solution)/shard_map/ppermute | solution.py:78
  360.0 10.9 %collective-permute-start.121 = (bf16[128,1024]{1,0:T(8,128)(2,1)}, bf16[128,1024]{1,0:T(8,128)(2,1)S(1)}, u32[]{:S(2)}, u32[]{:S(2)}) collective-permute-start(bf16[128,1024]{1,0:T(8,128)(2,1)} %collective-permute-done.115.refs_1_), channel_id=1, source_target_pairs={{0,2},{2,0},{1,3},{3,1},{4,6},{6,4},{5,7},{7,5},{8,10},{10,8},{9,1... | collective-permute-start | bytes 786440 | tf_op jit(solution)/shard_map/ppermute | solution.py:78
  369.2 19.7 %collective-permute-start.122 = (bf16[192,1024]{1,0:T(8,128)(2,1)S(1)}, bf16[192,1024]{1,0:T(8,128)(2,1)S(1)}, u32[]{:S(2)}, u32[]{:S(2)}) collective-permute-start(bf16[192,1024]{1,0:T(8,128)(2,1)S(1)} %get-tuple-element.575), channel_id=1, source_target_pairs={{4,12},{12,20},{20,28},{28,24},{24,16},{16,8},{8,0},{0,4},{5,13},{... | collective-permute-start | bytes 1179656 | tf_op jit(solution)/shard_map/ppermute | solution.py:272
  370.1 18.8 %collective-permute-start.123 = (bf16[192,1024]{1,0:T(8,128)(2,1)S(1)}, bf16[192,1024]{1,0:T(8,128)(2,1)S(1)}, u32[]{:S(2)}, u32[]{:S(2)}) collective-permute-start(bf16[192,1024]{1,0:T(8,128)(2,1)S(1)} %get-tuple-element.576), channel_id=1, source_target_pairs={{4,0},{12,4},{20,12},{28,20},{24,28},{16,24},{8,16},{0,8},{5,1},{1... | collective-permute-start | bytes 1179656 | tf_op jit(solution)/shard_map/ppermute | solution.py:272
  393.4 13.6 %collective-permute-start.127 = (bf16[256,1024]{1,0:T(8,128)(2,1)S(1)}, bf16[256,1024]{1,0:T(8,128)(2,1)S(1)}, u32[]{:S(2)}, u32[]{:S(2)}) collective-permute-start(bf16[256,1024]{1,0:T(8,128)(2,1)S(1)} %get-tuple-element.591), channel_id=1, source_target_pairs={{4,12},{12,20},{20,28},{28,24},{24,16},{16,8},{8,0},{0,4},{5,13},{... | collective-permute-start | bytes 1572872 | tf_op jit(solution)/shard_map/ppermute | solution.py:272
  393.8 13.3 %collective-permute-start.128 = (bf16[256,1024]{1,0:T(8,128)(2,1)S(1)}, bf16[256,1024]{1,0:T(8,128)(2,1)S(1)}, u32[]{:S(2)}, u32[]{:S(2)}) collective-permute-start(bf16[256,1024]{1,0:T(8,128)(2,1)S(1)} %get-tuple-element.592), channel_id=1, source_target_pairs={{4,0},{12,4},{20,12},{28,20},{24,28},{16,24},{8,16},{0,8},{5,1},{1... | collective-permute-start | bytes 1572872 | tf_op jit(solution)/shard_map/ppermute | solution.py:272
  408.6 15.8 %collective-permute-start.129 = (bf16[256,1024]{1,0:T(8,128)(2,1)S(1)}, bf16[256,1024]{1,0:T(8,128)(2,1)S(1)}, u32[]{:S(2)}, u32[]{:S(2)}) collective-permute-start(bf16[256,1024]{1,0:T(8,128)(2,1)S(1)} %get-tuple-element.605), channel_id=1, source_target_pairs={{4,12},{12,20},{20,28},{28,24},{24,16},{16,8},{8,0},{0,4},{5,13},{... | collective-permute-start | bytes 1572872 | tf_op jit(solution)/shard_map/ppermute | solution.py:272
  409.2 15.2 %collective-permute-start.130 = (bf16[256,1024]{1,0:T(8,128)(2,1)S(1)}, bf16[256,1024]{1,0:T(8,128)(2,1)S(1)}, u32[]{:S(2)}, u32[]{:S(2)}) collective-permute-start(bf16[256,1024]{1,0:T(8,128)(2,1)S(1)} %get-tuple-element.606), channel_id=1, source_target_pairs={{4,0},{12,4},{20,12},{28,20},{24,28},{16,24},{8,16},{0,8},{5,1},{1... | collective-permute-start | bytes 1572872 | tf_op jit(solution)/shard_map/ppermute | solution.py:272
  411.4 12.8 %collective-permute-start.156 = (f32[16384]{0:T(1024)S(1)}, f32[16384]{0:T(1024)S(1)}, u32[]{:S(2)}, u32[]{:S(2)}) collective-permute-start(f32[16384]{0:T(1024)S(1)} %pad_maximum_fusion.4), channel_id=1, source_target_pairs={{0,16},{8,24},{16,0},{24,8},{1,17},{9,25},{17,1},{25,9},{2,18},{10... | collective-permute-start | bytes 196616 | tf_op jit(solution)/shard_map/ppermute | solution.py:475
  438.0 14.7 %collective-permute-start.158 = (f32[9472]{0:T(1024)}, f32[9472]{0:T(1024)}, u32[]{:S(2)}, u32[]{:S(2)}) collective-permute-start(f32[9472]{0:T(1024)} %pad_maximum_fusion.6), channel_id=1, source_target_pairs={{0,4},{4,0},{1,5},{5,1},{2,6},{6,2},{3,7},{7,3},{8,12},{12,8},{9,1... | collective-permute-start | bytes 113672 | tf_op jit(solution)/shard_map/ppermute | solution.py:475
  444.0 12.0 %collective-permute-start.135 = (bf16[64,1024]{1,0:T(8,128)(2,1)S(1)}, bf16[64,1024]{1,0:T(8,128)(2,1)S(1)}, u32[]{:S(2)}, u32[]{:S(2)}) collective-permute-start(bf16[64,1024]{1,0:T(8,128)(2,1)S(1)} %get-tuple-element.631), channel_id=1, source_target_pairs={{4,12},{12,20},{20,28},{28,24},{24,16},{16,8},{8,0},{0,4},{5,13},{... | collective-permute-start | bytes 393224 | tf_op jit(solution)/shard_map/ppermute | solution.py:272
  445.6 10.4 %collective-permute-start.136 = (bf16[64,1024]{1,0:T(8,128)(2,1)S(1)}, bf16[64,1024]{1,0:T(8,128)(2,1)S(1)}, u32[]{:S(2)}, u32[]{:S(2)}) collective-permute-start(bf16[64,1024]{1,0:T(8,128)(2,1)S(1)} %get-tuple-element.632), channel_id=1, source_target_pairs={{4,0},{12,4},{20,12},{28,20},{24,28},{16,24},{8,16},{0,8},{5,1},{1... | collective-permute-start | bytes 393224 | tf_op jit(solution)/shard_map/ppermute | solution.py:272
  445.7 26.6 %collective-permute-start.150 = (bf16[32,1024]{1,0:T(8,128)(2,1)S(1)}, bf16[32,1024]{1,0:T(8,128)(2,1)S(1)}, u32[]{:S(2)}, u32[]{:S(2)}) collective-permute-start(bf16[32,1024]{1,0:T(8,128)(2,1)S(1)} %get-tuple-element.668), channel_id=1, source_target_pairs={{0,1},{1,0},{2,3},{3,2},{4,5},{5,4},{6,7},{7,6},{8,9},{9,8},{10,11... | collective-permute-start | bytes 196616 | tf_op jit(solution)/shard_map/ppermute | solution.py:78
  446.4 27.2 %collective-permute-start.151 = (bf16[32,1024]{1,0:T(8,128)(2,1)S(1)}, bf16[32,1024]{1,0:T(8,128)(2,1)S(1)}, u32[]{:S(2)}, u32[]{:S(2)}) collective-permute-start(bf16[32,1024]{1,0:T(8,128)(2,1)S(1)} %get-tuple-element.669), channel_id=1, source_target_pairs={{0,2},{2,0},{1,3},{3,1},{4,6},{6,4},{5,7},{7,5},{8,10},{10,8},{9,1... | collective-permute-start | bytes 196616 | tf_op jit(solution)/shard_map/ppermute | solution.py:78
  452.7 21.1 %collective-permute-start.152 = (bf16[32,1024]{1,0:T(8,128)(2,1)S(1)}, bf16[32,1024]{1,0:T(8,128)(2,1)S(1)}, u32[]{:S(2)}, u32[]{:S(2)}) collective-permute-start(bf16[32,1024]{1,0:T(8,128)(2,1)S(1)} %get-tuple-element.670), channel_id=1, source_target_pairs={{0,3},{1,2},{2,1},{3,0},{4,7},{5,6},{6,5},{7,4},{8,11},{9,10},{10,... | collective-permute-start | bytes 196616 | tf_op jit(solution)/shard_map/ppermute | solution.py:82
  468.6 11.6 %collective-permute-start.145 = (bf16[32,768]{1,0:T(8,128)(2,1)S(1)}, bf16[32,768]{1,0:T(8,128)(2,1)S(1)}, u32[]{:S(2)}, u32[]{:S(2)}) collective-permute-start(bf16[32,768]{1,0:T(8,128)(2,1)S(1)} %get-tuple-element.659), channel_id=1, source_target_pairs={{0,2},{2,0},{1,3},{3,1},{4,6},{6,4},{5,7},{7,5},{8,10},{10,8},{9,1... | collective-permute-start | bytes 147464 | tf_op jit(solution)/shard_map/ppermute | solution.py:78
  474.6 15.0 %collective-permute-start.153 = (bf16[2,32,1024]{2,1,0:T(8,128)(2,1)S(1)}, bf16[2,32,1024]{2,1,0:T(8,128)(2,1)S(1)}, u32[]{:S(2)}, u32[]{:S(2)}) collective-permute-start(bf16[2,32,1024]{2,1,0:T(8,128)(2,1)S(1)} %pad_maximum_fusion), channel_id=1, source_target_pairs={{0,0},{4,1},{8,2},{12,3},{16,4},{20,5},{24,6},{28,7},{1,8},{5,9},{... | collective-permute-start | bytes 393224 | tf_op jit(solution)/shard_map/ppermute | solution.py:1201
  (217 other events, 2384.5 us)
